TPU v7x, 32 devices: a whole 2x2x4 slice. The times are simulated.
32 devices in a mesh: leaf: 8 (over z, y), rhs: 4 (over x, core).
Axes of the slice: x: 2, y: 2, z: 4, core: 2. Of those that a mesh axis runs over, the one named last changes fastest.
Arguments:
- leaf_rhs: float32 [2, 64, 4096], P(None, 'rhs', 'leaf'), may hold values from -6 to 6
- sep_rhs: float32 [2, 64, 3, 64], P(None, 'rhs', None, 'leaf'), may hold values from -6 to 6
- leaf_inv: bfloat16 [2, 512, 4096], P(None, 'rhs', 'leaf'), may hold values from -0.1875 to 0.1875
- leaf_low: bfloat16 [2, 512, 64], P(None, None, 'leaf'), may hold values from -0.1875 to 0.1875
- sep_inv: bfloat16 [2, 8, 896], P(None, None, 'leaf'), as said below
- sep_low: bfloat16 [2, 8, 384], P(None, None, 'leaf'), as said below
- leaf_live: int32 [8], P('leaf'), may hold values from 1 to 4
- targets: int32 [3, 8], replicated, may hold values from 0 to 7, as said below
Outputs:
- leaf_solution: float32 [2, 64, 4096], P(None, 'rhs', 'leaf')
- sep_solution: float32 [2, 64, 3, 64], P(None, 'rhs', None, 'leaf')
Inputs may be any that keep to these rules, and one draw needn't show every extreme that they name: `targets`: in row l, the entries of each aligned group of 2 ** (l + 1) devices are a permutation of 0 to 2 ** (l + 1) - 1. Rows of a leaf front beyond 128 * leaf_live are padding and are ignored. `sep_inv`: entries are independent, of mean zero, with spread inversely proportional to the square root of the front's order. `sep_low`: entries are independent, of mean zero, with spread inversely proportional to the square root of the front's order.
All inputs are finite; a program needn't handle non-finite values.
Results may differ from a plain program's by a relative error of at most 0.025.
Values may be sent and summed in bfloat16 or wider, within the bound.
No kernel may reach another device: no remote copies, remote signals or barrier semaphores. Data moves between devices by JAX's collectives and lax.ppermute only.
A program may use at most 64 MiB of HBM per device.

v0:
```python
import jax
import jax.numpy as jnp
from jax import lax
from jax.sharding import PartitionSpec as P

exact_mode = lax.Precision.HIGHEST


def complex_dot(operand, factor):
    row_count = operand.shape[1]
    stacked = jnp.concatenate([operand[0], operand[1]], axis=0)
    real_acc = jnp.dot(stacked, factor[0], preferred_element_type=jnp.float32)
    imag_acc = jnp.dot(stacked, factor[1], preferred_element_type=jnp.float32)
    return jnp.stack(
        [real_acc[:row_count] - imag_acc[row_count:], imag_acc[:row_count] + real_acc[row_count:]]
    )


def complex_dot_back(operand, factor):
    row_count = operand.shape[1]
    stacked = jnp.concatenate([operand[0], operand[1]], axis=0)
    contract = (((1,), (1,)), ((), ()))
    real_acc = lax.dot_general(stacked, factor[0], contract, preferred_element_type=jnp.float32)
    imag_acc = lax.dot_general(stacked, factor[1], contract, preferred_element_type=jnp.float32)
    return jnp.stack(
        [real_acc[:row_count] - imag_acc[row_count:], imag_acc[:row_count] + real_acc[row_count:]]
    )


def to_blocks(values_in, group_size):
    return (
        values_in.reshape(2, values_in.shape[1], group_size, -1)
        .transpose(2, 0, 1, 3)
        .reshape(group_size, -1)
    )


def from_blocks(blocks, columns):
    group_size = blocks.shape[0]
    return blocks.reshape(group_size, 2, columns, -1).transpose(1, 2, 0, 3).reshape(2, columns, -1)


def selector(dest_index, total_slots):
    return (dest_index[:, None] == jnp.arange(total_slots, dtype=jnp.int32)[None, :]).astype(
        jnp.float32
    )


def exchange_sum(blocks, global_dest, devices):
    routed = jnp.dot(selector(global_dest, devices).T, blocks, precision=exact_mode)
    received = lax.all_to_all(
        routed.astype(jnp.bfloat16), "leaf", split_axis=0, concat_axis=0, tiled=True
    ).astype(routed.dtype)
    return jnp.sum(received, axis=0)


def collect(blocks, local_dest, level_bits, device, devices):
    group_start = device >> level_bits << level_bits
    return exchange_sum(blocks, group_start + local_dest, devices)


def exchange_blocks(own_block, level_bits, device, devices):
    group_size = 2**level_bits
    group_start = device >> level_bits << level_bits
    slot_index = jnp.arange(devices, dtype=jnp.int32)[:, None]
    inside = (slot_index >= group_start) & (slot_index < group_start + group_size)
    routed = jnp.where(inside, own_block[None, :], jnp.zeros_like(own_block)[None, :])
    received = lax.all_to_all(routed, "leaf", split_axis=0, concat_axis=0, tiled=True)
    return lax.dynamic_slice_in_dim(received, group_start, group_size, 0)


def spread(own_block, level_bits, device, devices):
    return exchange_blocks(own_block, level_bits, device, devices)


def body(leaf_rhs, sep_rhs, leaf_inv, leaf_low, sep_inv, sep_low, leaf_live, targets):
    devices = lax.axis_size("leaf")
    tree_depth = devices.bit_length() - 1
    device = lax.axis_index("leaf")
    leaf_rows = leaf_low.shape[1]
    sep_width = sep_inv.shape[1]
    columns = leaf_rhs.shape[1]
    live_mask = (jnp.arange(leaf_rows) < leaf_live[0] * 128).astype(jnp.float32)
    leaf_z = (leaf_rhs * live_mask).astype(jnp.bfloat16)
    leaf_w = complex_dot(leaf_z, lax.all_gather(leaf_inv, "rhs", axis=1, tiled=True))
    leaf_w = leaf_w * live_mask
    first_dest = lax.dynamic_slice_in_dim(targets[0], device, 1)
    arriving = collect(complex_dot(leaf_z, leaf_low).reshape(1, -1), first_dest, 1, device, devices)
    solved_w = []
    for level_now in range(1, tree_depth + 1):
        group_size = 2**level_now
        offset = sep_width * (group_size - 2)
        level_z = (
            sep_rhs[:, :, level_now - 1, :] - arriving.reshape(2, columns, sep_width)
        ).astype(jnp.bfloat16)
        inv_rows = sep_inv[:, :, offset : offset + sep_width * group_size]
        own_w = collect(
            to_blocks(complex_dot(level_z, inv_rows), group_size),
            jnp.arange(group_size, dtype=jnp.int32),
            level_now,
            device,
            devices,
        )
        solved_w.append(own_w.reshape(2, columns, sep_width))
        if level_now < tree_depth:
            low_rows = sep_low[:, :, offset : offset + sep_width * group_size]
            group_start = device >> level_now << level_now
            dest_index = lax.dynamic_slice_in_dim(targets[level_now], group_start, group_size)
            arriving = collect(
                to_blocks(complex_dot(level_z, low_rows), group_size),
                dest_index,
                level_now + 1,
                device,
                devices,
            )
    solved_x = [solved_w[level_now] for level_now in range(tree_depth)]
    for level_now in range(tree_depth - 1, 0, -1):
        group_size = 2**level_now
        offset = sep_width * (group_size - 2)
        low_rows = sep_low[:, :, offset : offset + sep_width * group_size]
        parent_x = spread(
            solved_x[level_now].astype(jnp.bfloat16).reshape(-1), level_now + 1, device, devices
        )
        group_start = device >> level_now << level_now
        dest_index = lax.dynamic_slice_in_dim(targets[level_now], group_start, group_size)
        picked = jnp.dot(
            selector(dest_index, 2 * group_size).astype(jnp.bfloat16),
            parent_x,
            preferred_element_type=jnp.float32,
        ).astype(jnp.bfloat16)
        solved_x[level_now - 1] = solved_w[level_now - 1] - complex_dot_back(
            from_blocks(picked, columns), low_rows
        )
    parent_x = spread(solved_x[0].astype(jnp.bfloat16).reshape(-1), 1, device, devices)
    picked = jnp.dot(
        selector(first_dest, 2).astype(jnp.bfloat16), parent_x, preferred_element_type=jnp.float32
    ).astype(jnp.bfloat16)
    leaf_x = (
        leaf_w - complex_dot_back(picked.reshape(2, columns, sep_width), leaf_low)
    ) * live_mask
    return (leaf_x, jnp.stack(solved_x, axis=2))


def solution(mesh):
    placed = (
        P(None, "rhs", "leaf"),
        P(None, "rhs", None, "leaf"),
        P(None, "rhs", "leaf"),
        P(None, None, "leaf"),
        P(None, None, "leaf"),
        P(None, None, "leaf"),
        P("leaf"),
        P(),
    )
    return jax.shard_map(
        body,
        mesh=mesh,
        in_specs=placed,
        out_specs=(P(None, "rhs", "leaf"), P(None, "rhs", None, "leaf")),
        check_vma=False,
    )
```

profile of v0, /device:TPU:0, one launch (start us, length us, event | category | flops | bytes accessed | tf_op | source)
XLA Modules:
  0.0 126.7 jit_solution(12387838563110704113)
XLA Ops:
  7.2 0.7 all-gather.2.cloned.1.call-update
  8.6 0.7 copy-done.3
  9.8 0.6 copy-done.5
  10.4 0.7 constant_dynamic-slice_fusion.4
  11.9 0.5 broadcast.219
  12.4 0.6 reduce.14
  12.9 0.6 reshape.467
  13.5 7.3 %all-to-all-start = ((bf16[8,2,128]{2,1,0:T(2,128)(2,1)}), bf16[8,2,128]{2,1,0:T(2,128)(2,1)S(1)}, u32[]{:S(2)}, u32[]{:S(2)}) async-start(bf16[8,2,128]{2,1,0:T(2,128)(2,1)} %reshape.467), calls=%async_computation | async-start | bytes 8192 | tf_op jit(solution)/shard_map/all_to_all | solution.py:51
  21.3 5.9 %all-to-all-done = bf16[8,2,128]{2,1,0:T(2,128)(2,1)S(1)} async-done(((bf16[8,2,128]{2,1,0:T(2,128)(2,1)}), bf16[8,2,128]{2,1,0:T(2,128)(2,1)S(1)}, u32[]{:S(2)}, u32[]{:S(2)}) %all-to-all-start) | async-done | bytes 4128 | tf_op jit(solution)/shard_map/all_to_all | solution.py:51
  27.6 0.6 copy-done.4
  28.6 0.5 copy-done.1
  30.4 0.6 reduce.16
  31.0 0.6 reshape.471
  31.6 3.3 %all-to-all-start.2 = ((bf16[8,2,128]{2,1,0:T(2,128)(2,1)}), bf16[8,2,128]{2,1,0:T(2,128)(2,1)S(1)}, u32[]{:S(2)}, u32[]{:S(2)}) async-start(bf16[8,2,128]{2,1,0:T(2,128)(2,1)} %reshape.471), calls=%async_computation.2 | async-start | bytes 8192 | tf_op jit(solution)/shard_map/all_to_all | solution.py:51
  35.2 0.6 reduce.15
  35.7 0.6 reshape.469
  36.3 4.9 %all-to-all-done.2 = bf16[8,2,128]{2,1,0:T(2,128)(2,1)S(1)} async-done(((bf16[8,2,128]{2,1,0:T(2,128)(2,1)}), bf16[8,2,128]{2,1,0:T(2,128)(2,1)S(1)}, u32[]{:S(2)}, u32[]{:S(2)}) %all-to-all-start.2) | async-done | bytes 4128 | tf_op jit(solution)/shard_map/all_to_all | solution.py:51
  41.2 3.3 %all-to-all-start.1 = ((bf16[8,2,128]{2,1,0:T(2,128)(2,1)}), bf16[8,2,128]{2,1,0:T(2,128)(2,1)S(1)}, u32[]{:S(2)}, u32[]{:S(2)}) async-start(bf16[8,2,128]{2,1,0:T(2,128)(2,1)} %reshape.469), calls=%async_computation.1 | async-start | bytes 8192 | tf_op jit(solution)/shard_map/all_to_all | solution.py:51
  46.8 0.6 reduce.18
  47.3 0.6 reshape.475
  47.9 2.9 %all-to-all-done.1 = bf16[8,2,128]{2,1,0:T(2,128)(2,1)S(1)} async-done(((bf16[8,2,128]{2,1,0:T(2,128)(2,1)}), bf16[8,2,128]{2,1,0:T(2,128)(2,1)S(1)}, u32[]{:S(2)}, u32[]{:S(2)}) %all-to-all-start.1) | async-done | bytes 4128 | tf_op jit(solution)/shard_map/all_to_all | solution.py:51
  50.9 3.3 %all-to-all-start.4 = ((bf16[8,2,128]{2,1,0:T(2,128)(2,1)}), bf16[8,2,128]{2,1,0:T(2,128)(2,1)S(1)}, u32[]{:S(2)}, u32[]{:S(2)}) async-start(bf16[8,2,128]{2,1,0:T(2,128)(2,1)} %reshape.475), calls=%async_computation.4 | async-start | bytes 8192 | tf_op jit(solution)/shard_map/all_to_all | solution.py:51
  54.4 0.6 reduce.17
  55.0 0.6 reshape.473
  55.6 4.9 %all-to-all-done.4 = bf16[8,2,128]{2,1,0:T(2,128)(2,1)S(1)} async-done(((bf16[8,2,128]{2,1,0:T(2,128)(2,1)}), bf16[8,2,128]{2,1,0:T(2,128)(2,1)S(1)}, u32[]{:S(2)}, u32[]{:S(2)}) %all-to-all-start.4) | async-done | bytes 4128 | tf_op jit(solution)/shard_map/all_to_all | solution.py:51
  60.5 3.3 %all-to-all-start.3 = ((bf16[8,2,128]{2,1,0:T(2,128)(2,1)}), bf16[8,2,128]{2,1,0:T(2,128)(2,1)S(1)}, u32[]{:S(2)}, u32[]{:S(2)}) async-start(bf16[8,2,128]{2,1,0:T(2,128)(2,1)} %reshape.473), calls=%async_computation.3 | async-start | bytes 8192 | tf_op jit(solution)/shard_map/all_to_all | solution.py:51
  65.3 0.6 reduce.19
  65.9 0.6 reshape.477
  66.5 3.6 %all-to-all-done.3 = bf16[8,2,128]{2,1,0:T(2,128)(2,1)S(1)} async-done(((bf16[8,2,128]{2,1,0:T(2,128)(2,1)}), bf16[8,2,128]{2,1,0:T(2,128)(2,1)S(1)}, u32[]{:S(2)}, u32[]{:S(2)}) %all-to-all-start.3) | async-done | bytes 4128 | tf_op jit(solution)/shard_map/all_to_all | solution.py:51
  70.2 3.3 %all-to-all-start.5 = ((bf16[8,2,128]{2,1,0:T(2,128)(2,1)}), bf16[8,2,128]{2,1,0:T(2,128)(2,1)S(1)}, u32[]{:S(2)}, u32[]{:S(2)}) async-start(bf16[8,2,128]{2,1,0:T(2,128)(2,1)} %reshape.477), calls=%async_computation.5 | async-start | bytes 8192 | tf_op jit(solution)/shard_map/all_to_all | solution.py:51
  73.6 6.2 %all-to-all-done.5 = bf16[8,2,128]{2,1,0:T(2,128)(2,1)S(1)} async-done(((bf16[8,2,128]{2,1,0:T(2,128)(2,1)}), bf16[8,2,128]{2,1,0:T(2,128)(2,1)S(1)}, u32[]{:S(2)}, u32[]{:S(2)}) %all-to-all-start.5) | async-done | bytes 4128 | tf_op jit(solution)/shard_map/all_to_all | solution.py:51
  79.9 0.6 reduce.20
  80.5 0.6 reshape.479
  81.1 3.3 %all-to-all-start.6 = ((bf16[8,2,128]{2,1,0:T(2,128)(2,1)}), bf16[8,2,128]{2,1,0:T(2,128)(2,1)S(1)}, u32[]{:S(2)}, u32[]{:S(2)}) async-start(bf16[8,2,128]{2,1,0:T(2,128)(2,1)} %reshape.479), calls=%async_computation.6 | async-start | bytes 8192 | tf_op jit(solution)/shard_map/all_to_all | solution.py:68
  84.6 6.1 %all-to-all-done.6 = bf16[8,2,128]{2,1,0:T(2,128)(2,1)S(1)} async-done(((bf16[8,2,128]{2,1,0:T(2,128)(2,1)}), bf16[8,2,128]{2,1,0:T(2,128)(2,1)S(1)}, u32[]{:S(2)}, u32[]{:S(2)}) %all-to-all-start.6) | async-done | bytes 4128 | tf_op jit(solution)/shard_map/all_to_all | solution.py:68
  92.0 0.6 reduce.21
  92.6 0.6 reshape.481
  93.2 3.3 %all-to-all-start.7 = ((bf16[8,2,128]{2,1,0:T(2,128)(2,1)}), bf16[8,2,128]{2,1,0:T(2,128)(2,1)S(1)}, u32[]{:S(2)}, u32[]{:S(2)}) async-start(bf16[8,2,128]{2,1,0:T(2,128)(2,1)} %reshape.481), calls=%async_computation.7 | async-start | bytes 8192 | tf_op jit(solution)/shard_map/all_to_all | solution.py:68
  96.7 6.2 %all-to-all-done.7 = bf16[8,2,128]{2,1,0:T(2,128)(2,1)S(1)} async-done(((bf16[8,2,128]{2,1,0:T(2,128)(2,1)}), bf16[8,2,128]{2,1,0:T(2,128)(2,1)S(1)}, u32[]{:S(2)}, u32[]{:S(2)}) %all-to-all-start.7) | async-done | bytes 4128 | tf_op jit(solution)/shard_map/all_to_all | solution.py:68
  104.1 0.6 reduce.22
  104.7 0.6 reshape.483
  105.3 3.3 %all-to-all-start.8 = ((bf16[8,2,128]{2,1,0:T(2,128)(2,1)}), bf16[8,2,128]{2,1,0:T(2,128)(2,1)S(1)}, u32[]{:S(2)}, u32[]{:S(2)}) async-start(bf16[8,2,128]{2,1,0:T(2,128)(2,1)} %reshape.483), calls=%async_computation.8 | async-start | bytes 8192 | tf_op jit(solution)/shard_map/all_to_all | solution.py:68
  108.8 0.7 copy.129
  109.5 5.5 %all-to-all-done.8 = bf16[8,2,128]{2,1,0:T(2,128)(2,1)S(1)} async-done(((bf16[8,2,128]{2,1,0:T(2,128)(2,1)}), bf16[8,2,128]{2,1,0:T(2,128)(2,1)S(1)}, u32[]{:S(2)}, u32[]{:S(2)}) %all-to-all-start.8) | async-done | bytes 4128 | tf_op jit(solution)/shard_map/all_to_all | solution.py:68
  114.9 0.8 fusion.95
  116.7 1.2 fusion.5
  118.0 1.2 fusion.6
  119.2 0.6 fusion.8
  (160 shorter events, 11.4 us)
Async XLA Ops:
  7.2 1.4 %copy-start = (f32[2,16,512]{2,1,0:T(8,128)S(1)}, f32[2,16,512]{2,1,0:T(8,128)}, u32[]{:S(2)}) copy-start(f32[2,16,512]{2,1,0:T(8,128)} %param.8) | copy-start | bytes 196612
  7.2 109.5 %all-gather.2.cloned.1.call-start = ((), (), s32[]{:S(2)}) async-start(), calls=%async_computation.9 | async-start | bytes 1310720 | tf_op jit(solution)/shard_map/all_gather | solution.py:85
  8.6 0.7 copy-start.3
  9.7 0.7 copy-start.5
  12.4 8.5 %copy-start.2 = (f32[2,16,3,8]{1,3,2,0:T(8,128)S(1)}, f32[2,16,3,8]{1,3,2,0:T(8,128)}, u32[]{:S(2)}) copy-start(f32[2,16,3,8]{1,3,2,0:T(8,128)} %param.9) | copy-start | bytes 9220
  13.5 13.7 %all-to-all-start = ((bf16[8,2,128]{2,1,0:T(2,128)(2,1)}), bf16[8,2,128]{2,1,0:T(2,128)(2,1)S(1)}, u32[]{:S(2)}, u32[]{:S(2)}) async-start(bf16[8,2,128]{2,1,0:T(2,128)(2,1)} %reshape.467), calls=%async_computation | async-start | bytes 8192 | tf_op jit(solution)/shard_map/all_to_all | solution.py:51
  27.5 0.7 copy-start.4
  28.4 0.7 copy-start.1
  31.6 9.6 %all-to-all-start.2 = ((bf16[8,2,128]{2,1,0:T(2,128)(2,1)}), bf16[8,2,128]{2,1,0:T(2,128)(2,1)S(1)}, u32[]{:S(2)}, u32[]{:S(2)}) async-start(bf16[8,2,128]{2,1,0:T(2,128)(2,1)} %reshape.471), calls=%async_computation.2 | async-start | bytes 8192 | tf_op jit(solution)/shard_map/all_to_all | solution.py:51
  41.2 9.6 %all-to-all-start.1 = ((bf16[8,2,128]{2,1,0:T(2,128)(2,1)}), bf16[8,2,128]{2,1,0:T(2,128)(2,1)S(1)}, u32[]{:S(2)}, u32[]{:S(2)}) async-start(bf16[8,2,128]{2,1,0:T(2,128)(2,1)} %reshape.469), calls=%async_computation.1 | async-start | bytes 8192 | tf_op jit(solution)/shard_map/all_to_all | solution.py:51
  50.9 9.6 %all-to-all-start.4 = ((bf16[8,2,128]{2,1,0:T(2,128)(2,1)}), bf16[8,2,128]{2,1,0:T(2,128)(2,1)S(1)}, u32[]{:S(2)}, u32[]{:S(2)}) async-start(bf16[8,2,128]{2,1,0:T(2,128)(2,1)} %reshape.475), calls=%async_computation.4 | async-start | bytes 8192 | tf_op jit(solution)/shard_map/all_to_all | solution.py:51
  60.5 9.6 %all-to-all-start.3 = ((bf16[8,2,128]{2,1,0:T(2,128)(2,1)}), bf16[8,2,128]{2,1,0:T(2,128)(2,1)S(1)}, u32[]{:S(2)}, u32[]{:S(2)}) async-start(bf16[8,2,128]{2,1,0:T(2,128)(2,1)} %reshape.473), calls=%async_computation.3 | async-start | bytes 8192 | tf_op jit(solution)/shard_map/all_to_all | solution.py:51
  70.2 9.6 %all-to-all-start.5 = ((bf16[8,2,128]{2,1,0:T(2,128)(2,1)}), bf16[8,2,128]{2,1,0:T(2,128)(2,1)S(1)}, u32[]{:S(2)}, u32[]{:S(2)}) async-start(bf16[8,2,128]{2,1,0:T(2,128)(2,1)} %reshape.477), calls=%async_computation.5 | async-start | bytes 8192 | tf_op jit(solution)/shard_map/all_to_all | solution.py:51
  81.1 9.6 %all-to-all-start.6 = ((bf16[8,2,128]{2,1,0:T(2,128)(2,1)}), bf16[8,2,128]{2,1,0:T(2,128)(2,1)S(1)}, u32[]{:S(2)}, u32[]{:S(2)}) async-start(bf16[8,2,128]{2,1,0:T(2,128)(2,1)} %reshape.479), calls=%async_computation.6 | async-start | bytes 8192 | tf_op jit(solution)/shard_map/all_to_all | solution.py:68
  93.2 9.6 %all-to-all-start.7 = ((bf16[8,2,128]{2,1,0:T(2,128)(2,1)}), bf16[8,2,128]{2,1,0:T(2,128)(2,1)S(1)}, u32[]{:S(2)}, u32[]{:S(2)}) async-start(bf16[8,2,128]{2,1,0:T(2,128)(2,1)} %reshape.481), calls=%async_computation.7 | async-start | bytes 8192 | tf_op jit(solution)/shard_map/all_to_all | solution.py:68
  105.3 9.6 %all-to-all-start.8 = ((bf16[8,2,128]{2,1,0:T(2,128)(2,1)}), bf16[8,2,128]{2,1,0:T(2,128)(2,1)S(1)}, u32[]{:S(2)}, u32[]{:S(2)}) async-start(bf16[8,2,128]{2,1,0:T(2,128)(2,1)} %reshape.483), calls=%async_computation.8 | async-start | bytes 8192 | tf_op jit(solution)/shard_map/all_to_all | solution.py:68
Sparse Core Ops, SparseCore 0:
  9.6 19.4 all-gather.1
where the time goes:
time: 128 us; the launch traced here: 127 us
  waiting for transfers between devices  46.9 us (37%)
  starting transfers between devices  33.8 us (26%)
  between operations  15.9 us (12%)
  local copies, waits for them, and re-layouts  14.4 us (11%)
  matrix products  8.46 us (7%)
  other arithmetic  7.26 us (6%)
    all_to_all x6, waiting for transfers between devices, exchange_sum(): lax.all_to_all(routed.astype(jnp.bfloat16), 'leaf', split_axis=0, concat_...  28.5 us
    all_to_all x6, starting transfers between devices, exchange_sum(): lax.all_to_all(routed.astype(jnp.bfloat16), 'leaf', split_axis=0, concat_...  23.8 us
    all_to_all x3, waiting for transfers between devices, exchange_blocks(): lax.all_to_all(routed, 'leaf', split_axis=0, concat_axis=0, tiled=True)  17.8 us
    all_to_all x3, starting transfers between devices, exchange_blocks(): lax.all_to_all(routed, 'leaf', split_axis=0, concat_axis=0, tiled=True)  9.93 us
    unnamed x34, local copies, waits for them, and re-layouts  8.84 us
    all_to_all x7, other arithmetic, exchange_sum(): lax.all_to_all(routed.astype(jnp.bfloat16), 'leaf', split_axis=0, concat_...  3.5 us
  transfers between devices with their start and end apart: 10, of which 9 were waited for; matrix products, arithmetic and copies ran while one was open for 19% of the time, Pallas kernels for 0%

commit v1 on v0

--- a/solution.py
+++ b/solution.py
@@ -1,9 +1,15 @@
+import functools
+
 import jax
 import jax.numpy as jnp
 from jax import lax
+from jax.experimental import pallas as pl
+from jax.experimental.pallas import tpu as pltpu
 from jax.sharding import PartitionSpec as P
 
 exact_mode = lax.Precision.HIGHEST
+VMEM = pltpu.MemorySpace.VMEM
+SMEM = pltpu.MemorySpace.SMEM
 
 
 def complex_dot(operand, factor):
@@ -59,7 +65,7 @@
     return exchange_sum(blocks, group_start + local_dest, devices)
 
 
-def exchange_blocks(own_block, level_bits, device, devices):
+def spread(own_block, level_bits, device, devices):
     group_size = 2**level_bits
     group_start = device >> level_bits << level_bits
     slot_index = jnp.arange(devices, dtype=jnp.int32)[:, None]
@@ -69,11 +75,7 @@
     return lax.dynamic_slice_in_dim(received, group_start, group_size, 0)
 
 
-def spread(own_block, level_bits, device, devices):
-    return exchange_blocks(own_block, level_bits, device, devices)
-
-
-def body(leaf_rhs, sep_rhs, leaf_inv, leaf_low, sep_inv, sep_low, leaf_live, targets):
+def level_by_level(leaf_rhs, sep_rhs, leaf_w, leaf_low, sep_inv, sep_low, leaf_live, targets):
     devices = lax.axis_size("leaf")
     tree_depth = devices.bit_length() - 1
     device = lax.axis_index("leaf")
@@ -82,8 +84,6 @@
     columns = leaf_rhs.shape[1]
     live_mask = (jnp.arange(leaf_rows) < leaf_live[0] * 128).astype(jnp.float32)
     leaf_z = (leaf_rhs * live_mask).astype(jnp.bfloat16)
-    leaf_w = complex_dot(leaf_z, lax.all_gather(leaf_inv, "rhs", axis=1, tiled=True))
-    leaf_w = leaf_w * live_mask
     first_dest = lax.dynamic_slice_in_dim(targets[0], device, 1)
     arriving = collect(complex_dot(leaf_z, leaf_low).reshape(1, -1), first_dest, 1, device, devices)
     solved_w = []
@@ -138,7 +138,242 @@
     leaf_x = (
         leaf_w - complex_dot_back(picked.reshape(2, columns, sep_width), leaf_low)
     ) * live_mask
-    return (leaf_x, jnp.stack(solved_x, axis=2))
+    return leaf_x, jnp.stack(solved_x, axis=2)
+
+
+def masked_rows(leaf_rhs_ref, live_ref):
+    rows = leaf_rhs_ref.shape[2]
+    live = lax.broadcasted_iota(jnp.int32, (1, rows), 1) < live_ref[0] * 128
+    stacked = jnp.concatenate([leaf_rhs_ref[0], leaf_rhs_ref[1]], axis=0)
+    return jnp.where(live, stacked, 0.0).astype(jnp.bfloat16), live
+
+
+def leaf_product_kernel(parts, live_ref, leaf_rhs_ref, *refs):
+    inv_refs, out_ref, z_ref = refs[:parts], refs[parts], refs[parts + 1]
+    columns = leaf_rhs_ref.shape[1]
+    depth = inv_refs[0].shape[1]
+    leaf_z, live = masked_rows(leaf_rhs_ref, live_ref)
+    z_ref[...] = leaf_z
+    mine = lax.axis_index("rhs")
+    total = [None, None]
+    for step in range(parts):
+        owner = mine ^ step
+        piece = z_ref[:, pl.ds(pl.multiple_of(owner * depth, 128), depth)]
+        for part in range(2):
+            term = jnp.dot(piece, inv_refs[step][part], preferred_element_type=jnp.float32)
+            total[part] = term if step == 0 else total[part] + term
+    real_acc, imag_acc = total
+    out_ref[0] = jnp.where(live, real_acc[:columns] - imag_acc[columns:], 0.0)
+    out_ref[1] = jnp.where(live, imag_acc[:columns] + real_acc[columns:], 0.0)
+
+
+def xor_permute(values_in, axis, offset):
+    count = lax.axis_size(axis)
+    return lax.ppermute(values_in, axis, [(source, source ^ offset) for source in range(count)])
+
+
+def leaf_product(leaf_rhs, leaf_inv, leaf_live):
+    parts = lax.axis_size("rhs")
+    pieces = {0: leaf_inv}
+    offset = parts // 2
+    while offset >= 1:
+        for known in list(pieces):
+            pieces[known ^ offset] = xor_permute(pieces[known], "rhs", offset)
+        offset //= 2
+    ordered = [pieces[step] for step in range(parts)]
+    columns, rows = leaf_rhs.shape[1:]
+    return pl.pallas_call(
+        functools.partial(leaf_product_kernel, parts),
+        out_shape=jax.ShapeDtypeStruct((2, columns, rows), jnp.float32),
+        in_specs=[pl.BlockSpec(memory_space=SMEM)]
+        + [pl.BlockSpec(memory_space=VMEM)] * (1 + parts),
+        out_specs=pl.BlockSpec(memory_space=VMEM),
+        scratch_shapes=[pltpu.VMEM((2 * columns, rows), jnp.bfloat16)],
+        cost_estimate=pl.CostEstimate(
+            flops=8 * columns * rows * rows, bytes_accessed=4 * rows * rows, transcendentals=0
+        ),
+    )(leaf_live, leaf_rhs, *ordered)
+
+
+def pack_kernel(live_ref, leaf_rhs_ref, low_ref, rhs_ref, inv_ref, sep_low_ref, out_ref):
+    columns = leaf_rhs_ref.shape[1]
+    depth = rhs_ref.shape[1]
+    leaf_z, _ = masked_rows(leaf_rhs_ref, live_ref)
+    panel = jnp.concatenate([low_ref[0], low_ref[1]], axis=0)
+    product = lax.dot_general(
+        panel, leaf_z, (((1,), (1,)), ((), ())), preferred_element_type=jnp.float32
+    )
+    width = low_ref.shape[1]
+    update = [
+        product[:width, :columns] - product[width:, columns:],
+        product[width:, :columns] + product[:width, columns:],
+    ]
+    used = (1 + depth) * columns + sep_low_ref.shape[2]
+    halves = []
+    for part in range(2):
+        pieces = [update[part]] + [rhs_ref[part, level] for level in range(depth)]
+        pieces.append(sep_low_ref[part].astype(jnp.float32))
+        if used < 128:
+            pieces.append(jnp.zeros((width, 128 - used), jnp.float32))
+        pieces.append(inv_ref[part].astype(jnp.float32))
+        if inv_ref.shape[2] < 128:
+            pieces.append(jnp.zeros((width, 128 - inv_ref.shape[2]), jnp.float32))
+        halves.append(jnp.concatenate(pieces, axis=1))
+    out_ref[...] = jnp.concatenate(halves, axis=0).astype(jnp.bfloat16)
+
+
+def tree_kernel(
+    live_ref, targets_ref, gathered_ref, leaf_w_ref, low_ref, leaf_out_ref, sep_out_ref, panel_ref, turn_ref
+):
+    depth, devices = targets_ref.shape
+    width = low_ref.shape[1]
+    columns = leaf_w_ref.shape[1]
+    slab = 2 * width
+    size = devices * slab
+    device = lax.axis_index("leaf")
+    row = lax.broadcasted_iota(jnp.int32, (size, size), 0)
+    lane = lax.broadcasted_iota(jnp.int32, (size, size), 1)
+    lane_row = lax.broadcasted_iota(jnp.int32, (1, size), 1)
+    row_part, lane_part = (row // width) % 2, (lane // width) % 2
+
+    def owner(level, block):
+        if level == 0:
+            return jnp.int32(block)
+        group = 2**level
+        return block // group * group + targets_ref[level - 1, block]
+
+    def rows_of(level):
+        return jnp.concatenate(
+            [
+                gathered_ref[pl.ds(pl.multiple_of((owner(level, block) ^ device) * slab, slab), slab), :]
+                for block in range(devices)
+            ],
+            axis=0,
+        )
+
+    raw = [rows_of(level) for level in range(depth + 1)]
+    pick_row = lax.broadcasted_iota(jnp.int32, (columns, size), 0)
+    pick_lane = lax.broadcasted_iota(jnp.int32, (columns, size), 1)
+    back = (((1,), (1,)), ((), ()))
+
+    def side(level):
+        pick = jnp.where(pick_lane == pick_row + level * columns, 1.0, 0.0).astype(jnp.bfloat16)
+        return lax.dot_general(pick, raw[level][:, :size], back, preferred_element_type=jnp.float32)
+
+    def spread_lanes(source, first_lane, level, column_of):
+        wanted = first_lane + column_of * width + lane_row % width
+        pick = jnp.where(row == wanted, 1.0, 0.0).astype(jnp.bfloat16)
+        plain = jnp.dot(source, pick, preferred_element_type=jnp.float32)
+        swapped = plain.reshape(devices, 2, width, size)
+        swapped = jnp.concatenate([swapped[:, 1:], swapped[:, :1]], axis=1).reshape(size, size)
+        signed = jnp.where(row_part == 0, plain, -plain)
+        full = jnp.where(lane_part == 0, signed, swapped)
+        inside = row // (slab * 2**level) == lane // (slab * 2**level)
+        return jnp.where(inside, full, 0.0).astype(jnp.bfloat16)
+
+    low_start = (1 + depth) * columns
+    inverse, lower = [None], [None]
+    for level in range(1, depth + 1):
+        offset = width * (2**level - 2)
+        target_lane = jnp.zeros((1, size), jnp.int32)
+        for block in range(devices):
+            target_lane = jnp.where(lane_row // slab == block, targets_ref[level - 1, block], target_lane)
+        inverse.append(spread_lanes(raw[level][:, size:], offset, level, target_lane))
+        if level < depth:
+            own_lane = (lane_row // slab) % 2**level
+            lower.append(spread_lanes(raw[level][:, :size], low_start + offset, level, own_lane))
+
+    arriving = side(0)
+    partial = [None]
+    for level in range(1, depth + 1):
+        level_z = (side(level) - arriving).astype(jnp.bfloat16)
+        partial.append(jnp.dot(level_z, inverse[level], preferred_element_type=jnp.float32))
+        if level < depth:
+            arriving = jnp.dot(level_z, lower[level], preferred_element_type=jnp.float32)
+
+    sign = jnp.where((lane_row // width) % 2 == 0, 1.0, -1.0)
+    solved = list(partial)
+    for level in range(depth - 1, 0, -1):
+        parent = (solved[level + 1] * sign).astype(jnp.bfloat16)
+        product = lax.dot_general(parent, lower[level], back, preferred_element_type=jnp.float32)
+        solved[level] = partial[level] - product * sign
+
+    leaf_rows = low_ref.shape[2]
+    panel_ref[...] = jnp.zeros_like(panel_ref)
+    first = jnp.concatenate([low_ref[0], -low_ref[1]], axis=0)
+    second = jnp.concatenate([low_ref[1], low_ref[0]], axis=0)
+    panel_ref[pl.ds(pl.multiple_of(device * slab, slab), slab), :] = jnp.concatenate([first, second], axis=1)
+    live = lax.broadcasted_iota(jnp.int32, (1, leaf_rows), 1) < live_ref[0] * 128
+    product = jnp.dot(
+        solved[1].astype(jnp.bfloat16), panel_ref[...], preferred_element_type=jnp.float32
+    )
+    for part in range(2):
+        leaf_out_ref[part] = jnp.where(
+            live, leaf_w_ref[part] - product[:, part * leaf_rows : (part + 1) * leaf_rows], 0.0
+        )
+
+    stacked = jnp.concatenate(
+        solved[1:] + [jnp.zeros((size - depth * columns, size), jnp.float32)], axis=0
+    )
+    turn_ref[...] = stacked.T
+    for level in range(1, depth + 1):
+        place = jnp.int32(0)
+        for block in range(devices):
+            place = jnp.where(owner(level, block) == device, block, place)
+        block_rows = turn_ref[pl.ds(pl.multiple_of(place * slab, slab), slab), :]
+        for part in range(2):
+            sep_out_ref[part, level - 1] = block_rows[
+                part * width : (part + 1) * width, (level - 1) * columns : level * columns
+            ]
+
+
+def gathered_tree(leaf_rhs, sep_rhs, leaf_w, leaf_low, sep_inv, sep_low, leaf_live, targets):
+    devices = lax.axis_size("leaf")
+    columns, leaf_rows = leaf_rhs.shape[1:]
+    width = sep_inv.shape[1]
+    depth = sep_rhs.shape[2]
+    slab = 2 * width
+    size = devices * slab
+    panel = leaf_low.transpose(0, 2, 1)
+    tree_rhs = sep_rhs.transpose(0, 2, 3, 1)
+    held = pl.pallas_call(
+        pack_kernel,
+        out_shape=jax.ShapeDtypeStruct((slab, 2 * size), jnp.bfloat16),
+        in_specs=[pl.BlockSpec(memory_space=SMEM)] + [pl.BlockSpec(memory_space=VMEM)] * 5,
+        out_specs=pl.BlockSpec(memory_space=VMEM),
+    )(leaf_live, leaf_rhs, panel, tree_rhs, sep_inv, sep_low)
+    offset = 1
+    while offset < devices:
+        held = jnp.concatenate([held, xor_permute(held, "leaf", offset)], axis=0)
+        offset *= 2
+    leaf_x, sep_x = pl.pallas_call(
+        tree_kernel,
+        out_shape=(
+            jax.ShapeDtypeStruct((2, columns, leaf_rows), jnp.float32),
+            jax.ShapeDtypeStruct((2, depth, width, columns), jnp.float32),
+        ),
+        in_specs=[pl.BlockSpec(memory_space=SMEM)] * 2 + [pl.BlockSpec(memory_space=VMEM)] * 3,
+        out_specs=(pl.BlockSpec(memory_space=VMEM), pl.BlockSpec(memory_space=VMEM)),
+        scratch_shapes=[
+            pltpu.VMEM((size, 2 * leaf_rows), jnp.bfloat16),
+            pltpu.VMEM((size, size), jnp.float32),
+        ],
+    )(leaf_live, targets, held, leaf_w, panel)
+    return leaf_x, sep_x.transpose(0, 3, 1, 2)
+
+
+def body(leaf_rhs, sep_rhs, leaf_inv, leaf_low, sep_inv, sep_low, leaf_live, targets):
+    devices = lax.axis_size("leaf")
+    columns = leaf_rhs.shape[1]
+    width, depth = sep_inv.shape[1], sep_rhs.shape[2]
+    leaf_w = leaf_product(leaf_rhs, leaf_inv, leaf_live)
+    fits = (
+        devices * 2 * width == 128
+        and (1 + depth) * columns + sep_low.shape[2] <= 128
+        and sep_inv.shape[2] <= 128
+    )
+    solve = gathered_tree if fits else level_by_level
+    return solve(leaf_rhs, sep_rhs, leaf_w, leaf_low, sep_inv, sep_low, leaf_live, targets)
 
 
 def solution(mesh):

time: 128 us -> 26.1 us (0.20)
  waiting for transfers between devices: 46.9 us -> 6.22 us
  starting transfers between devices: 33.8 us -> 9.2 us
  between operations: 15.9 us -> 1.31 us
  local copies, waits for them, and re-layouts: 14.4 us -> 1.39 us
  matrix products: 8.46 us -> 0 us
  Pallas kernels: 0 us -> 6.32 us
  other arithmetic: 7.26 us -> 1.34 us
    all_to_all x9 -> x0, waiting for transfers between devices: 46.2 us -> none  [the longest x6 28.5 us: exchange_sum(): lax.all_to_all(routed.astype(jnp.bfloat16), 'leaf', split_axis=0, concat_...]
    all_to_all x9 -> x0, starting transfers between devices: 33.8 us -> none  [the longest x6 23.8 us: exchange_sum(): lax.all_to_all(routed.astype(jnp.bfloat16), 'leaf', split_axis=0, concat_...]
    ppermute x0 -> x6, starting transfers between devices: none -> 9.2 us  [xor_permute(): lax.ppermute(values_in, axis, [(source, source ^ offset) for source in ra...]
    dot_general x28 -> x0, matrix products: 8.46 us -> none  [the longest x7 2.38 us: complex_dot(): real_acc = jnp.dot(stacked, factor[0], preferred_element_type=jnp.float32)]
    unnamed x34 -> x8, local copies, waits for them, and re-layouts: 8.84 us -> 1.39 us
    pallas_call x0 -> x3, Pallas kernels: none -> 6.32 us  [the longest x1 2.53 us: gathered_tree(): pl.pallas_call(tree_kernel, out_shape=(jax.ShapeDtypeStruct((2, columns,...]
    ppermute x0 -> x6, waiting for transfers between devices: none -> 6.22 us  [xor_permute(): lax.ppermute(values_in, axis, [(source, source ^ offset) for source in ra...]
    all_to_all x7 -> x0, other arithmetic: 3.5 us -> none  [exchange_sum(): lax.all_to_all(routed.astype(jnp.bfloat16), 'leaf', split_axis=0, concat_...]
  transfers between devices with their start and end apart: 10 -> 6, of which waited for: 9 -> 3; matrix products, arithmetic and copies ran while one was open for 19% -> 5% of each run, Pallas kernels for 0% -> 7%
where the time goes in v1:
time: 26.1 us; the launch traced here: 25.8 us
  starting transfers between devices  9.2 us (35%)
  Pallas kernels  6.32 us (24%)
  waiting for transfers between devices  6.22 us (24%)
  local copies, waits for them, and re-layouts  1.39 us (5%)
  other arithmetic  1.34 us (5%)
  between operations  1.31 us (5%)
    ppermute x6, starting transfers between devices, xor_permute(): lax.ppermute(values_in, axis, [(source, source ^ offset) for source in ra...  9.2 us
    ppermute x6, waiting for transfers between devices, xor_permute(): lax.ppermute(values_in, axis, [(source, source ^ offset) for source in ra...  6.22 us
    pallas_call x1, Pallas kernels, gathered_tree(): pl.pallas_call(tree_kernel, out_shape=(jax.ShapeDtypeStruct((2, columns,...  2.53 us
    pallas_call x1, Pallas kernels, leaf_product(): pl.pallas_call(functools.partial(leaf_product_kernel, parts), out_shape=j...  2.1 us
    pallas_call x1, Pallas kernels, gathered_tree(): pl.pallas_call(pack_kernel, out_shape=jax.ShapeDtypeStruct((slab, 2 * siz...  1.68 us
    unnamed x8, local copies, waits for them, and re-layouts  1.39 us
    concatenate x3, other arithmetic, gathered_tree(): held = jnp.concatenate([held, xor_permute(held, 'leaf', offset)], axis=0)  1.34 us
  transfers between devices with their start and end apart: 6, of which 3 were waited for; matrix products, arithmetic and copies ran while one was open for 5% of the time, Pallas kernels for 7%

profile of v1, /device:TPU:0, one launch (start us, length us, event | category | flops | bytes accessed | tf_op | source)
XLA Modules:
  0.0 25.8 jit_solution(6896036207706269358)
XLA Ops:
  0.6 3.0 %collective-permute-start.4 = (bf16[2,128,512]{2,1,0:T(8,128)(2,1)}, bf16[2,128,512]{2,1,0:T(8,128)(2,1)S(1)}, u32[]{:S(2)}, u32[]{:S(2)}) collective-permute-start(bf16[2,128,512]{2,1,0:T(8,128)(2,1)} %refs_0_.1), channel_id=1, source_target_pairs={{0,2},{1,3},{2,0},{3,1},{4,6},{5,7},{6,4},{7,5},{8,10},{9,11},{10,... | collective-permute-start | bytes 786440 | tf_op jit(solution)/shard_map/ppermute | solution.py:172
  4.3 1.7 %shard_map.95 = bf16[16,256]{1,0:T(8,128)(2,1)} custom-call(s32[1]{0:T(128)S(6)} %copy.10.live_ref, f32[2,16,512]{2,1,0:T(8,128)} %leaf_rhs_ref.3, bf16[2,8,512]{2,1,0:T(8,128)(2,1)} %bitcast.3, f32[2,3,8,16]{3,2,1,0:T(8,128)} %bitcast.5, bf16[2,8,112]{2,1,0:T(8,128)(2,1)} %inv_ref.1, bf16[2,8,48]{2,1,0:T(8,128)(2,1)} %sep_low_ref.1), custom_call_target="tpu_custom_call" | custom-call | tf_op jit(solution)/shard_map/pallas_call | solution.py:339
  6.0 0.0 copy-start.3
  6.0 1.5 %collective-permute-start = (bf16[16,256]{1,0:T(8,128)(2,1)}, bf16[16,256]{1,0:T(8,128)(2,1)S(1)}, u32[]{:S(2)}, u32[]{:S(2)}) collective-permute-start(bf16[16,256]{1,0:T(8,128)(2,1)} %shard_map.95), channel_id=1, source_target_pairs={{0,4},{4,0},{8,12},{12,8},{16,20},{20,16},{24,28},{28,24},{1,5},{5... | collective-permute-start | bytes 24584 | tf_op jit(solution)/shard_map/ppermute | solution.py:172
  7.5 2.3 %collective-permute-done = bf16[16,256]{1,0:T(8,128)(2,1)S(1)} collective-permute-done((bf16[16,256]{1,0:T(8,128)(2,1)}, bf16[16,256]{1,0:T(8,128)(2,1)S(1)}, u32[]{:S(2)}, u32[]{:S(2)}) %collective-permute-start) | collective-permute-done | bytes 8224 | tf_op jit(solution)/shard_map/ppermute | solution.py:172
  9.8 0.7 %pad_maximum_fusion.2 = bf16[32,256]{1,0:T(8,128)(2,1)S(1)} fusion(bf16[16,256]{1,0:T(8,128)(2,1)S(1)} %collective-permute-done, bf16[16,256]{1,0:T(8,128)(2,1)} %shard_map.95), kind=kLoop, calls=%fused_computation.2 | loop fusion | flops 32768 | bytes 32768 | tf_op jit(solution)/shard_map/concatenate | solution.py:347
  10.5 1.6 %collective-permute-start.1 = (bf16[32,256]{1,0:T(8,128)(2,1)S(1)}, bf16[32,256]{1,0:T(8,128)(2,1)S(1)}, u32[]{:S(2)}, u32[]{:S(2)}) collective-permute-start(bf16[32,256]{1,0:T(8,128)(2,1)S(1)} %pad_maximum_fusion.2), channel_id=1, source_target_pairs={{0,8},{4,12},{8,0},{12,4},{16,24},{20,28},{24,16},{28,20},{1,9},{5... | collective-permute-start | bytes 49160 | tf_op jit(solution)/shard_map/ppermute | solution.py:172
  12.1 0.0 collective-permute-start.3
  12.1 0.0 collective-permute-done.4.refs_2_
  12.1 0.0 copy-start
  12.1 0.5 %collective-permute-start.5 = (bf16[2,128,512]{2,1,0:T(8,128)(2,1)S(1)}, bf16[2,128,512]{2,1,0:T(8,128)(2,1)S(1)}, u32[]{:S(2)}, u32[]{:S(2)}) collective-permute-start(bf16[2,128,512]{2,1,0:T(8,128)(2,1)S(1)} %collective-permute-done.4.refs_2_), channel_id=1, source_target_pairs={{0,1},{1,0},{2,3},{3,2},{4,5},{5,4},{6,7},{7,6},{8,9},{9,8},{10,11... | collective-permute-start | bytes 786440 | tf_op jit(solution)/shard_map/ppermute | solution.py:172
  12.6 1.6 %collective-permute-done.1 = bf16[32,256]{1,0:T(8,128)(2,1)S(1)} collective-permute-done((bf16[32,256]{1,0:T(8,128)(2,1)S(1)}, bf16[32,256]{1,0:T(8,128)(2,1)S(1)}, u32[]{:S(2)}, u32[]{:S(2)}) %collective-permute-start.1) | collective-permute-done | bytes 16416 | tf_op jit(solution)/shard_map/ppermute | solution.py:172
  14.3 0.0 copy-done.3
  14.3 2.6 %collective-permute-start.2 = (bf16[64,256]{1,0:T(8,128)(2,1)S(1)}, bf16[64,256]{1,0:T(8,128)(2,1)S(1)}, u32[]{:S(2)}, u32[]{:S(2)}) collective-permute-start(bf16[64,256]{1,0:T(8,128)(2,1)S(1)} %pad_maximum_fusion.1), channel_id=1, source_target_pairs={{0,16},{4,20},{8,24},{12,28},{16,0},{20,4},{24,8},{28,12},{1,17},{... | collective-permute-start | bytes 98312 | tf_op jit(solution)/shard_map/ppermute | solution.py:172
  16.9 2.2 %collective-permute-done.2 = bf16[64,256]{1,0:T(8,128)(2,1)S(1)} collective-permute-done((bf16[64,256]{1,0:T(8,128)(2,1)S(1)}, bf16[64,256]{1,0:T(8,128)(2,1)S(1)}, u32[]{:S(2)}, u32[]{:S(2)}) %collective-permute-start.2) | collective-permute-done | bytes 32800 | tf_op jit(solution)/shard_map/ppermute | solution.py:172
  19.1 0.6 %pad_maximum_fusion.gathered_ref = bf16[128,256]{1,0:T(8,128)(2,1)} fusion(bf16[64,256]{1,0:T(8,128)(2,1)S(1)} %collective-permute-done.2, bf16[32,256]{1,0:T(8,128)(2,1)S(1)} %collective-permute-done.1, bf16[16,256]{1,0:T(8,128)(2,1)S(1)} %collective-permute-done, bf16[16,256]{1,0:T(8,128)(2,1)S(1)} %copy-done.3), kind=kLoop, calls=%fused_computation | loop fusion | flops 262144 | bytes 131072 | tf_op jit(solution)/shard_map/concatenate | solution.py:347
  19.7 0.0 collective-permute-done.3.refs_1_
  19.7 0.0 copy-start.1
  19.7 0.0 collective-permute-done.5.refs_3_
  19.7 0.0 copy-done
  19.8 0.7 %copy-done.1 = bf16[2,128,512]{2,1,0:T(8,128)(2,1)} copy-done((bf16[2,128,512]{2,1,0:T(8,128)(2,1)}, bf16[2,128,512]{2,1,0:T(8,128)(2,1)S(1)}, u32[]{:S(2)}) %copy-start.1) | copy-done | bytes 262168
  20.4 0.0 copy-start.2
  20.4 0.7 %copy-done.2 = bf16[2,128,512]{2,1,0:T(8,128)(2,1)} copy-done((bf16[2,128,512]{2,1,0:T(8,128)(2,1)}, bf16[2,128,512]{2,1,0:T(8,128)(2,1)S(1)}, u32[]{:S(2)}) %copy-start.2) | copy-done | bytes 262168
  21.1 2.1 %shard_map.96.leaf_w_ref = f32[2,16,512]{2,1,0:T(8,128)} custom-call(s32[1]{0:T(128)S(6)} %copy.10.live_ref, f32[2,16,512]{2,1,0:T(8,128)} %leaf_rhs_ref.3, bf16[2,128,512]{2,1,0:T(8,128)(2,1)} %refs_0_.1, bf16[2,128,512]{2,1,0:T(8,128)(2,1)} %copy-done.1, bf16[2,128,512]{2,1,0:T(8,128)(2,1)} %copy-done, bf16[2,128,512]{2,1,0:T(8,128)(2,1)} %copy-done.2), custom_call_target="tpu_custom_call" | custom-call | flops 33554432 | bytes 1048576 | tf_op jit(solution)/shard_map/pallas_call | solution.py:185
  23.2 2.5 %shard_map.97 = (f32[2,16,512]{2,1,0:T(8,128)}, f32[2,3,8,16]{3,2,1,0:T(8,128)}) custom-call(s32[1]{0:T(128)S(6)} %copy.10.live_ref, s32[3,8]{1,0:T(4,128)} %targets_ref.1, bf16[128,256]{1,0:T(8,128)(2,1)} %pad_maximum_fusion.gathered_ref, f32[2,16,512]{2,1,0:T(8,128)} %shard_map.96.leaf_w_ref, bf16[2,8,512]{2,1,0:T(8,128)(2,1)} %bitcast.4), custom_call_target="tpu_custom_call" | custom-call | tf_op jit(solution)/shard_map/pallas_call | solution.py:349
  (1 shorter events, 0.0 us)
Async XLA Ops:
  0.6 11.5 %collective-permute-start.4 = (bf16[2,128,512]{2,1,0:T(8,128)(2,1)}, bf16[2,128,512]{2,1,0:T(8,128)(2,1)S(1)}, u32[]{:S(2)}, u32[]{:S(2)}) collective-permute-start(bf16[2,128,512]{2,1,0:T(8,128)(2,1)} %refs_0_.1), channel_id=1, source_target_pairs={{0,2},{1,3},{2,0},{3,1},{4,6},{5,7},{6,4},{7,5},{8,10},{9,11},{10,... | collective-permute-start | bytes 786440 | tf_op jit(solution)/shard_map/ppermute | solution.py:172
  6.0 8.3 %copy-start.3 = (bf16[16,256]{1,0:T(8,128)(2,1)S(1)}, bf16[16,256]{1,0:T(8,128)(2,1)}, u32[]{:S(2)}) copy-start(bf16[16,256]{1,0:T(8,128)(2,1)} %shard_map.95) | copy-start | bytes 24580
  6.0 3.9 %collective-permute-start = (bf16[16,256]{1,0:T(8,128)(2,1)}, bf16[16,256]{1,0:T(8,128)(2,1)S(1)}, u32[]{:S(2)}, u32[]{:S(2)}) collective-permute-start(bf16[16,256]{1,0:T(8,128)(2,1)} %shard_map.95), channel_id=1, source_target_pairs={{0,4},{4,0},{8,12},{12,8},{16,20},{20,16},{24,28},{28,24},{1,5},{5... | collective-permute-start | bytes 24584 | tf_op jit(solution)/shard_map/ppermute | solution.py:172
  10.5 3.7 %collective-permute-start.1 = (bf16[32,256]{1,0:T(8,128)(2,1)S(1)}, bf16[32,256]{1,0:T(8,128)(2,1)S(1)}, u32[]{:S(2)}, u32[]{:S(2)}) collective-permute-start(bf16[32,256]{1,0:T(8,128)(2,1)S(1)} %pad_maximum_fusion.2), channel_id=1, source_target_pairs={{0,8},{4,12},{8,0},{12,4},{16,24},{20,28},{24,16},{28,20},{1,9},{5... | collective-permute-start | bytes 49160 | tf_op jit(solution)/shard_map/ppermute | solution.py:172
  12.1 7.6 %collective-permute-start.3 = (bf16[2,128,512]{2,1,0:T(8,128)(2,1)}, bf16[2,128,512]{2,1,0:T(8,128)(2,1)S(1)}, u32[]{:S(2)}, u32[]{:S(2)}) collective-permute-start(bf16[2,128,512]{2,1,0:T(8,128)(2,1)} %refs_0_.1), channel_id=1, source_target_pairs={{0,1},{1,0},{2,3},{3,2},{4,5},{5,4},{6,7},{7,6},{8,9},{9,8},{10,11... | collective-permute-start | bytes 786440 | tf_op jit(solution)/shard_map/ppermute | solution.py:172
  12.1 7.6 %copy-start = (bf16[2,128,512]{2,1,0:T(8,128)(2,1)}, bf16[2,128,512]{2,1,0:T(8,128)(2,1)S(1)}, u32[]{:S(2)}) copy-start(bf16[2,128,512]{2,1,0:T(8,128)(2,1)S(1)} %collective-permute-done.4.refs_2_) | copy-start | bytes 786436
  12.1 7.6 %collective-permute-start.5 = (bf16[2,128,512]{2,1,0:T(8,128)(2,1)S(1)}, bf16[2,128,512]{2,1,0:T(8,128)(2,1)S(1)}, u32[]{:S(2)}, u32[]{:S(2)}) collective-permute-start(bf16[2,128,512]{2,1,0:T(8,128)(2,1)S(1)} %collective-permute-done.4.refs_2_), channel_id=1, source_target_pairs={{0,1},{1,0},{2,3},{3,2},{4,5},{5,4},{6,7},{7,6},{8,9},{9,8},{10,11... | collective-permute-start | bytes 786440 | tf_op jit(solution)/shard_map/ppermute | solution.py:172
  14.3 4.8 %collective-permute-start.2 = (bf16[64,256]{1,0:T(8,128)(2,1)S(1)}, bf16[64,256]{1,0:T(8,128)(2,1)S(1)}, u32[]{:S(2)}, u32[]{:S(2)}) collective-permute-start(bf16[64,256]{1,0:T(8,128)(2,1)S(1)} %pad_maximum_fusion.1), channel_id=1, source_target_pairs={{0,16},{4,20},{8,24},{12,28},{16,0},{20,4},{24,8},{28,12},{1,17},{... | collective-permute-start | bytes 98312 | tf_op jit(solution)/shard_map/ppermute | solution.py:172
  19.7 0.7 %copy-start.1 = (bf16[2,128,512]{2,1,0:T(8,128)(2,1)}, bf16[2,128,512]{2,1,0:T(8,128)(2,1)S(1)}, u32[]{:S(2)}) copy-start(bf16[2,128,512]{2,1,0:T(8,128)(2,1)S(1)} %collective-permute-done.3.refs_1_) | copy-start | bytes 786436
  20.4 0.7 %copy-start.2 = (bf16[2,128,512]{2,1,0:T(8,128)(2,1)}, bf16[2,128,512]{2,1,0:T(8,128)(2,1)S(1)}, u32[]{:S(2)}) copy-start(bf16[2,128,512]{2,1,0:T(8,128)(2,1)S(1)} %collective-permute-done.5.refs_3_) | copy-start | bytes 786436

commit v2 on v1

--- a/solution.py
+++ b/solution.py
@@ -141,64 +141,50 @@
     return leaf_x, jnp.stack(solved_x, axis=2)
 
 
-def masked_rows(leaf_rhs_ref, live_ref):
-    rows = leaf_rhs_ref.shape[2]
-    live = lax.broadcasted_iota(jnp.int32, (1, rows), 1) < live_ref[0] * 128
-    stacked = jnp.concatenate([leaf_rhs_ref[0], leaf_rhs_ref[1]], axis=0)
-    return jnp.where(live, stacked, 0.0).astype(jnp.bfloat16), live
-
-
-def leaf_product_kernel(parts, live_ref, leaf_rhs_ref, *refs):
-    inv_refs, out_ref, z_ref = refs[:parts], refs[parts], refs[parts + 1]
-    columns = leaf_rhs_ref.shape[1]
-    depth = inv_refs[0].shape[1]
-    leaf_z, live = masked_rows(leaf_rhs_ref, live_ref)
-    z_ref[...] = leaf_z
-    mine = lax.axis_index("rhs")
-    total = [None, None]
-    for step in range(parts):
-        owner = mine ^ step
-        piece = z_ref[:, pl.ds(pl.multiple_of(owner * depth, 128), depth)]
-        for part in range(2):
-            term = jnp.dot(piece, inv_refs[step][part], preferred_element_type=jnp.float32)
-            total[part] = term if step == 0 else total[part] + term
-    real_acc, imag_acc = total
-    out_ref[0] = jnp.where(live, real_acc[:columns] - imag_acc[columns:], 0.0)
-    out_ref[1] = jnp.where(live, imag_acc[:columns] + real_acc[columns:], 0.0)
-
-
 def xor_permute(values_in, axis, offset):
     count = lax.axis_size(axis)
     return lax.ppermute(values_in, axis, [(source, source ^ offset) for source in range(count)])
 
 
-def leaf_product(leaf_rhs, leaf_inv, leaf_live):
+def gather_pieces(own_piece, hold=lambda piece: piece):
     parts = lax.axis_size("rhs")
-    pieces = {0: leaf_inv}
+    pieces = {0: own_piece}
     offset = parts // 2
     while offset >= 1:
         for known in list(pieces):
-            pieces[known ^ offset] = xor_permute(pieces[known], "rhs", offset)
+            source = pieces[known] if known == 0 else hold(pieces[known])
+            pieces[known] = source
+            pieces[known ^ offset] = xor_permute(source, "rhs", offset)
         offset //= 2
-    ordered = [pieces[step] for step in range(parts)]
-    columns, rows = leaf_rhs.shape[1:]
-    return pl.pallas_call(
-        functools.partial(leaf_product_kernel, parts),
-        out_shape=jax.ShapeDtypeStruct((2, columns, rows), jnp.float32),
-        in_specs=[pl.BlockSpec(memory_space=SMEM)]
-        + [pl.BlockSpec(memory_space=VMEM)] * (1 + parts),
-        out_specs=pl.BlockSpec(memory_space=VMEM),
-        scratch_shapes=[pltpu.VMEM((2 * columns, rows), jnp.bfloat16)],
-        cost_estimate=pl.CostEstimate(
-            flops=8 * columns * rows * rows, bytes_accessed=4 * rows * rows, transcendentals=0
-        ),
-    )(leaf_live, leaf_rhs, *ordered)
-
-
-def pack_kernel(live_ref, leaf_rhs_ref, low_ref, rhs_ref, inv_ref, sep_low_ref, out_ref):
+    return [pieces[step] for step in range(parts)]
+
+
+def in_vmem(values_in):
+    return pltpu.with_memory_space_constraint(values_in, VMEM)
+
+
+def masked_rows(leaf_rhs, live_ref):
+    rows = leaf_rhs.shape[2]
+    live = lax.broadcasted_iota(jnp.int32, (1, rows), 1) < live_ref[0] * 128
+    stacked = jnp.concatenate([leaf_rhs[0], leaf_rhs[1]], axis=0)
+    return jnp.where(live, stacked, 0.0).astype(jnp.bfloat16), live
+
+
+def pack_kernel(live_ref, *refs):
+    sources, (out_ref, z_ref), places, sems = refs[:5], refs[5:7], refs[7:12], refs[12]
+    copies = [
+        pltpu.make_async_copy(source, place, sems.at[which])
+        for which, (source, place) in enumerate(zip(sources, places))
+    ]
+    for copy in copies:
+        copy.start()
+    for copy in copies:
+        copy.wait()
+    leaf_rhs_ref, low_ref, rhs_ref, inv_ref, sep_low_ref = places
     columns = leaf_rhs_ref.shape[1]
     depth = rhs_ref.shape[1]
-    leaf_z, _ = masked_rows(leaf_rhs_ref, live_ref)
+    leaf_z, _ = masked_rows(leaf_rhs_ref[...], live_ref)
+    z_ref[...] = leaf_z
     panel = jnp.concatenate([low_ref[0], low_ref[1]], axis=0)
     product = lax.dot_general(
         panel, leaf_z, (((1,), (1,)), ((), ())), preferred_element_type=jnp.float32
@@ -222,19 +208,84 @@
     out_ref[...] = jnp.concatenate(halves, axis=0).astype(jnp.bfloat16)
 
 
+def leaf_kernel(parts, live_ref, z_ref, *refs):
+    inv_refs, out_ref = refs[:parts], refs[parts]
+    columns = out_ref.shape[1]
+    depth = inv_refs[0].shape[1]
+    mine = lax.axis_index("rhs")
+    total = [None, None]
+    for step in range(parts):
+        owner = mine ^ step
+        piece = z_ref[:, pl.ds(pl.multiple_of(owner * depth, 128), depth)]
+        for part in range(2):
+            term = jnp.dot(piece, inv_refs[step][part], preferred_element_type=jnp.float32)
+            total[part] = term if step == 0 else total[part] + term
+    real_acc, imag_acc = total
+    live = lax.broadcasted_iota(jnp.int32, (1, z_ref.shape[1]), 1) < live_ref[0] * 128
+    out_ref[0] = jnp.where(live, real_acc[:columns] - imag_acc[columns:], 0.0)
+    out_ref[1] = jnp.where(live, imag_acc[:columns] + real_acc[columns:], 0.0)
+
+
+def prepare_kernel(low_start, live_ref, targets_ref, low_ref, panel_ref, pick_ref, kept_ref):
+    for level in range(targets_ref.shape[0]):
+        for block in range(targets_ref.shape[1]):
+            kept_ref[level, block] = targets_ref[level, block]
+    depth, devices = targets_ref.shape
+    width, leaf_rows = low_ref.shape[1:]
+    slab = 2 * width
+    device = lax.axis_index("leaf")
+    live = lax.broadcasted_iota(jnp.int32, (1, leaf_rows), 1) < live_ref[0] * 128
+    low = [jnp.where(live, low_ref[part].astype(jnp.float32), 0.0) for part in range(2)]
+    rows = jnp.concatenate(
+        [
+            jnp.concatenate([low[0], low[1]], axis=1),
+            jnp.concatenate([-low[1], low[0]], axis=1),
+        ],
+        axis=0,
+    ).astype(jnp.bfloat16)
+    panel_ref[...] = jnp.zeros_like(panel_ref)
+    panel_ref[pl.ds(pl.multiple_of(device * slab, slab), slab), :] = rows
+    size = devices * slab
+    row = lax.broadcasted_iota(jnp.int32, (size, size), 0)
+    lane_row = lax.broadcasted_iota(jnp.int32, (1, size), 1)
+    for level in range(1, depth + 1):
+        offset = width * (2**level - 2) + lane_row % width
+        target_lane = jnp.zeros((1, size), jnp.int32)
+        for block in range(devices):
+            target_lane = jnp.where(lane_row // slab == block, targets_ref[level - 1, block], target_lane)
+        pick_ref[level - 1] = jnp.where(row == offset + target_lane * width, 1.0, 0.0).astype(jnp.bfloat16)
+        if level < depth:
+            own_lane = (lane_row // slab) % 2**level
+            pick_ref[depth + level - 1] = jnp.where(
+                row == low_start + offset + own_lane * width, 1.0, 0.0
+            ).astype(jnp.bfloat16)
+
+
+def join_kernel(own_ref, other_ref, out_ref):
+    rows = own_ref.shape[0]
+    out_ref[:rows] = own_ref[...]
+    out_ref[rows:] = other_ref[...]
+
+
+def hold_kernel(piece_ref, _, out_ref):
+    pass
+
+
 def tree_kernel(
-    live_ref, targets_ref, gathered_ref, leaf_w_ref, low_ref, leaf_out_ref, sep_out_ref, panel_ref, turn_ref
+    targets_ref, near_ref, far_ref, leaf_w_ref, panel_ref, pick_ref, leaf_out_ref, sep_out_ref, all_ref, turn_ref
 ):
     depth, devices = targets_ref.shape
-    width = low_ref.shape[1]
+    size = panel_ref.shape[0]
+    slab = size // devices
+    width = slab // 2
     columns = leaf_w_ref.shape[1]
-    slab = 2 * width
-    size = devices * slab
     device = lax.axis_index("leaf")
     row = lax.broadcasted_iota(jnp.int32, (size, size), 0)
     lane = lax.broadcasted_iota(jnp.int32, (size, size), 1)
     lane_row = lax.broadcasted_iota(jnp.int32, (1, size), 1)
     row_part, lane_part = (row // width) % 2, (lane // width) % 2
+    all_ref[: size // 2, :] = near_ref[...]
+    all_ref[size // 2 :, :] = far_ref[...]
 
     def owner(level, block):
         if level == 0:
@@ -245,7 +296,7 @@
     def rows_of(level):
         return jnp.concatenate(
             [
-                gathered_ref[pl.ds(pl.multiple_of((owner(level, block) ^ device) * slab, slab), slab), :]
+                all_ref[pl.ds(pl.multiple_of((owner(level, block) ^ device) * slab, slab), slab), :]
                 for block in range(devices)
             ],
             axis=0,
@@ -260,9 +311,7 @@
         pick = jnp.where(pick_lane == pick_row + level * columns, 1.0, 0.0).astype(jnp.bfloat16)
         return lax.dot_general(pick, raw[level][:, :size], back, preferred_element_type=jnp.float32)
 
-    def spread_lanes(source, first_lane, level, column_of):
-        wanted = first_lane + column_of * width + lane_row % width
-        pick = jnp.where(row == wanted, 1.0, 0.0).astype(jnp.bfloat16)
+    def front_matrix(source, pick, level):
         plain = jnp.dot(source, pick, preferred_element_type=jnp.float32)
         swapped = plain.reshape(devices, 2, width, size)
         swapped = jnp.concatenate([swapped[:, 1:], swapped[:, :1]], axis=1).reshape(size, size)
@@ -271,17 +320,11 @@
         inside = row // (slab * 2**level) == lane // (slab * 2**level)
         return jnp.where(inside, full, 0.0).astype(jnp.bfloat16)
 
-    low_start = (1 + depth) * columns
     inverse, lower = [None], [None]
     for level in range(1, depth + 1):
-        offset = width * (2**level - 2)
-        target_lane = jnp.zeros((1, size), jnp.int32)
-        for block in range(devices):
-            target_lane = jnp.where(lane_row // slab == block, targets_ref[level - 1, block], target_lane)
-        inverse.append(spread_lanes(raw[level][:, size:], offset, level, target_lane))
+        inverse.append(front_matrix(raw[level][:, size:], pick_ref[level - 1], level))
         if level < depth:
-            own_lane = (lane_row // slab) % 2**level
-            lower.append(spread_lanes(raw[level][:, :size], low_start + offset, level, own_lane))
+            lower.append(front_matrix(raw[level][:, :size], pick_ref[depth + level - 1], level))
 
     arriving = side(0)
     partial = [None]
@@ -298,19 +341,12 @@
         product = lax.dot_general(parent, lower[level], back, preferred_element_type=jnp.float32)
         solved[level] = partial[level] - product * sign
 
-    leaf_rows = low_ref.shape[2]
-    panel_ref[...] = jnp.zeros_like(panel_ref)
-    first = jnp.concatenate([low_ref[0], -low_ref[1]], axis=0)
-    second = jnp.concatenate([low_ref[1], low_ref[0]], axis=0)
-    panel_ref[pl.ds(pl.multiple_of(device * slab, slab), slab), :] = jnp.concatenate([first, second], axis=1)
-    live = lax.broadcasted_iota(jnp.int32, (1, leaf_rows), 1) < live_ref[0] * 128
+    leaf_rows = leaf_w_ref.shape[2]
     product = jnp.dot(
         solved[1].astype(jnp.bfloat16), panel_ref[...], preferred_element_type=jnp.float32
     )
     for part in range(2):
-        leaf_out_ref[part] = jnp.where(
-            live, leaf_w_ref[part] - product[:, part * leaf_rows : (part + 1) * leaf_rows], 0.0
-        )
+        leaf_out_ref[part] = leaf_w_ref[part] - product[:, part * leaf_rows : (part + 1) * leaf_rows]
 
     stacked = jnp.concatenate(
         solved[1:] + [jnp.zeros((size - depth * columns, size), jnp.float32)], axis=0
@@ -327,53 +363,111 @@
             ]
 
 
-def gathered_tree(leaf_rhs, sep_rhs, leaf_w, leaf_low, sep_inv, sep_low, leaf_live, targets):
-    devices = lax.axis_size("leaf")
+def whole(space):
+    return pl.BlockSpec(memory_space=space)
+
+
+def body(leaf_rhs, sep_rhs, leaf_inv, leaf_low, sep_inv, sep_low, leaf_live, targets):
+    devices, parts = lax.axis_size("leaf"), lax.axis_size("rhs")
     columns, leaf_rows = leaf_rhs.shape[1:]
-    width = sep_inv.shape[1]
-    depth = sep_rhs.shape[2]
+    width, depth = sep_inv.shape[1], sep_rhs.shape[2]
     slab = 2 * width
     size = devices * slab
+    small_tree = (
+        size == 128 and (1 + depth) * columns + sep_low.shape[2] <= 128 and sep_inv.shape[2] <= 128
+    )
     panel = leaf_low.transpose(0, 2, 1)
     tree_rhs = sep_rhs.transpose(0, 2, 3, 1)
-    held = pl.pallas_call(
+
+    def leaf_w_of(leaf_z, pieces):
+        return pl.pallas_call(
+            functools.partial(leaf_kernel, parts),
+            out_shape=pltpu.VMEM((2, columns, leaf_rows), jnp.float32),
+            in_specs=[whole(SMEM)] + [whole(VMEM)] * (1 + parts),
+            out_specs=whole(VMEM),
+            cost_estimate=pl.CostEstimate(
+                flops=8 * columns * leaf_rows * leaf_rows,
+                bytes_accessed=4 * leaf_rows * leaf_rows,
+                transcendentals=0,
+            ),
+        )(leaf_live, *[in_vmem(ready) for ready in [leaf_z] + pieces])
+
+    if not small_tree:
+        live_mask = (jnp.arange(leaf_rows) < leaf_live[0] * 128).astype(jnp.float32)
+        leaf_z = (leaf_rhs * live_mask).astype(jnp.bfloat16).reshape(2 * columns, leaf_rows)
+        leaf_w = leaf_w_of(leaf_z, gather_pieces(leaf_inv))
+        return level_by_level(leaf_rhs, sep_rhs, leaf_w, leaf_low, sep_inv, sep_low, leaf_live, targets)
+
+    tree_parts = (leaf_rhs, panel, tree_rhs, sep_inv, sep_low)
+    held, leaf_z = pl.pallas_call(
         pack_kernel,
-        out_shape=jax.ShapeDtypeStruct((slab, 2 * size), jnp.bfloat16),
-        in_specs=[pl.BlockSpec(memory_space=SMEM)] + [pl.BlockSpec(memory_space=VMEM)] * 5,
-        out_specs=pl.BlockSpec(memory_space=VMEM),
-    )(leaf_live, leaf_rhs, panel, tree_rhs, sep_inv, sep_low)
+        out_shape=(
+            pltpu.VMEM((slab, 2 * size), jnp.bfloat16),
+            pltpu.VMEM((2 * columns, leaf_rows), jnp.bfloat16),
+        ),
+        in_specs=[whole(SMEM)] + [whole(pl.ANY)] * 5,
+        out_specs=(whole(VMEM),) * 2,
+        scratch_shapes=[pltpu.VMEM(part.shape, part.dtype) for part in tree_parts]
+        + [pltpu.SemaphoreType.DMA((5,))],
+    )(leaf_live, *tree_parts)
+    panel_rows, picks, kept_targets = pl.pallas_call(
+        functools.partial(prepare_kernel, (1 + depth) * columns),
+        out_shape=(
+            pltpu.VMEM((size, 2 * leaf_rows), jnp.bfloat16),
+            pltpu.VMEM((2 * depth - 1, size, size), jnp.bfloat16),
+            pltpu.SMEM(targets.shape, jnp.int32),
+        ),
+        in_specs=[whole(SMEM), whole(SMEM), whole(VMEM)],
+        out_specs=(whole(VMEM),) * 2 + (whole(SMEM),),
+        cost_estimate=pl.CostEstimate(flops=0, bytes_accessed=2 * 1024 * 1024, transcendentals=0),
+    )(leaf_live, targets, panel)
+
+    def join(own, other):
+        return pl.pallas_call(
+            join_kernel,
+            out_shape=pltpu.VMEM((2 * own.shape[0], own.shape[1]), own.dtype),
+            in_specs=[whole(VMEM)] * 2,
+            out_specs=whole(VMEM),
+            cost_estimate=pl.CostEstimate(
+                flops=0, bytes_accessed=32 * 1024 * 1024, transcendentals=0
+            ),
+        )(in_vmem(own), in_vmem(other))
+
+    rounds = [held]
     offset = 1
     while offset < devices:
-        held = jnp.concatenate([held, xor_permute(held, "leaf", offset)], axis=0)
+        rounds.append(xor_permute(held, "leaf", offset))
         offset *= 2
+        if offset < devices:
+            held = join(held, rounds[-1])
+
+    def hold(piece):
+        return pl.pallas_call(
+            hold_kernel,
+            out_shape=pltpu.VMEM(piece.shape, piece.dtype),
+            in_specs=[whole(VMEM)] * 2,
+            out_specs=whole(VMEM),
+            input_output_aliases={0: 0},
+        )(in_vmem(piece), in_vmem(held))
+
+    leaf_w = leaf_w_of(leaf_z, gather_pieces(leaf_inv, hold))
     leaf_x, sep_x = pl.pallas_call(
         tree_kernel,
         out_shape=(
             jax.ShapeDtypeStruct((2, columns, leaf_rows), jnp.float32),
             jax.ShapeDtypeStruct((2, depth, width, columns), jnp.float32),
         ),
-        in_specs=[pl.BlockSpec(memory_space=SMEM)] * 2 + [pl.BlockSpec(memory_space=VMEM)] * 3,
-        out_specs=(pl.BlockSpec(memory_space=VMEM), pl.BlockSpec(memory_space=VMEM)),
+        in_specs=[whole(SMEM)] + [whole(VMEM)] * 5,
+        out_specs=(whole(VMEM), whole(VMEM)),
         scratch_shapes=[
-            pltpu.VMEM((size, 2 * leaf_rows), jnp.bfloat16),
+            pltpu.VMEM((size, 2 * size), jnp.bfloat16),
             pltpu.VMEM((size, size), jnp.float32),
         ],
-    )(leaf_live, targets, held, leaf_w, panel)
+    )(
+        pltpu.with_memory_space_constraint(kept_targets, SMEM),
+        *[in_vmem(ready) for ready in (held, rounds[-1], leaf_w, panel_rows, picks)],
+    )
     return leaf_x, sep_x.transpose(0, 3, 1, 2)
-
-
-def body(leaf_rhs, sep_rhs, leaf_inv, leaf_low, sep_inv, sep_low, leaf_live, targets):
-    devices = lax.axis_size("leaf")
-    columns = leaf_rhs.shape[1]
-    width, depth = sep_inv.shape[1], sep_rhs.shape[2]
-    leaf_w = leaf_product(leaf_rhs, leaf_inv, leaf_live)
-    fits = (
-        devices * 2 * width == 128
-        and (1 + depth) * columns + sep_low.shape[2] <= 128
-        and sep_inv.shape[2] <= 128
-    )
-    solve = gathered_tree if fits else level_by_level
-    return solve(leaf_rhs, sep_rhs, leaf_w, leaf_low, sep_inv, sep_low, leaf_live, targets)
 
 
 def solution(mesh):

time: 26.1 us -> 19.7 us (0.75)
  Pallas kernels: 6.32 us -> 3.76 us
  local copies, waits for them, and re-layouts: 1.39 us -> 0.01 us
  other arithmetic: 1.34 us -> 0 us
  waiting for transfers between devices: 6.22 us -> 5.45 us
  starting transfers between devices: 9.2 us -> 8.89 us
    pallas_call x3 -> x7, Pallas kernels: 6.32 us -> 3.76 us  [the longest x1 1.64 us: body(): pl.pallas_call(tree_kernel, out_shape=(jax.ShapeDtypeStruct((2, columns,...]
    unnamed x8 -> x2, local copies, waits for them, and re-layouts: 1.39 us -> 0.01 us
    concatenate x3 -> x0, other arithmetic: 1.34 us -> none  [gathered_tree(): held = jnp.concatenate([held, xor_permute(held, 'leaf', offset)], axis=0)]
    ppermute x6, waiting for transfers between devices: 6.22 us -> 5.45 us  [xor_permute(): lax.ppermute(values_in, axis, [(source, source ^ offset) for source in ra...]
    ppermute x6, starting transfers between devices: 9.2 us -> 8.89 us  [xor_permute(): lax.ppermute(values_in, axis, [(source, source ^ offset) for source in ra...]
  transfers between devices with their start and end apart: 6 -> 6, of which waited for: 3 -> 3; matrix products, arithmetic and copies ran while one was open for 5% -> 0% of each run, Pallas kernels for 7% -> 11%
where the time goes in v2:
time: 19.7 us; the launch traced here: 19.5 us
  starting transfers between devices  8.89 us (45%)
  waiting for transfers between devices  5.45 us (28%)
  Pallas kernels  3.76 us (19%)
  between operations  1.36 us (7%)
    ppermute x6, starting transfers between devices, xor_permute(): lax.ppermute(values_in, axis, [(source, source ^ offset) for source in ra...  8.89 us
    ppermute x6, waiting for transfers between devices, xor_permute(): lax.ppermute(values_in, axis, [(source, source ^ offset) for source in ra...  5.45 us
    pallas_call x1, Pallas kernels, body(): pl.pallas_call(tree_kernel, out_shape=(jax.ShapeDtypeStruct((2, columns,...  1.64 us
    pallas_call x1, Pallas kernels, body(): pl.pallas_call(pack_kernel, out_shape=(pltpu.VMEM((slab, 2 * size), jnp.b...  1.09 us
    pallas_call x1, Pallas kernels, body(): pl.pallas_call(functools.partial(prepare_kernel, (1 + depth) * columns),...  0.78 us
  transfers between devices with their start and end apart: 6, of which 3 were waited for; matrix products, arithmetic and copies ran while one was open for 0% of the time, Pallas kernels for 11%

profile of v2, /device:TPU:0, one launch (start us, length us, event | category | flops | bytes accessed | tf_op | source)
XLA Modules:
  0.0 19.5 jit_solution(8758986132935881435)
XLA Ops:
  0.6 3.0 %collective-permute-start.4 = (bf16[2,128,512]{2,1,0:T(8,128)(2,1)}, bf16[2,128,512]{2,1,0:T(8,128)(2,1)S(1)}, u32[]{:S(2)}, u32[]{:S(2)}) collective-permute-start(bf16[2,128,512]{2,1,0:T(8,128)(2,1)} %refs_0_.3), channel_id=1, source_target_pairs={{0,2},{1,3},{2,0},{3,1},{4,6},{5,7},{6,4},{7,5},{8,10},{9,11},{10,... | collective-permute-start | bytes 786440 | tf_op jit(solution)/shard_map/ppermute | solution.py:146
  4.3 1.1 %shard_map.96 = (bf16[16,256]{1,0:T(8,128)(2,1)S(1)}, bf16[32,512]{1,0:T(8,128)(2,1)S(1)}) custom-call(s32[1]{0:T(128)S(6)} %copy.12.live_ref, f32[2,16,512]{2,1,0:T(8,128)} %refs_0_.2, bf16[2,8,512]{2,1,0:T(8,128)(2,1)} %bitcast.3, f32[2,3,8,16]{3,2,1,0:T(8,128)} %bitcast.5, bf16[2,8,112]{2,1,0:T(8,128)(2,1)} %refs_3_.1, bf16[2,8,48]{2,1,0:T(8,128)(2,1)} %refs_4_.1), custom_call_target="tpu_custom_call" | custom-call | tf_op jit(solution)/shard_map/pallas_call | solution.py:402
  5.4 1.6 %collective-permute-start = (bf16[16,256]{1,0:T(8,128)(2,1)S(1)}, bf16[16,256]{1,0:T(8,128)(2,1)S(1)}, u32[]{:S(2)}, u32[]{:S(2)}) collective-permute-start(bf16[16,256]{1,0:T(8,128)(2,1)S(1)} %get-tuple-element.10.own_ref), channel_id=1, source_target_pairs={{0,4},{4,0},{8,12},{12,8},{16,20},{20,16},{24,28},{28,24},{1,5},{5... | collective-permute-start | bytes 24584 | tf_op jit(solution)/shard_map/ppermute | solution.py:146
  7.0 2.1 %collective-permute-done.other_ref = bf16[16,256]{1,0:T(8,128)(2,1)S(1)} collective-permute-done((bf16[16,256]{1,0:T(8,128)(2,1)S(1)}, bf16[16,256]{1,0:T(8,128)(2,1)S(1)}, u32[]{:S(2)}, u32[]{:S(2)}) %collective-permute-start) | collective-permute-done | bytes 8224 | tf_op jit(solution)/shard_map/ppermute | solution.py:146
  9.1 1.6 %collective-permute-start.1 = (bf16[32,256]{1,0:T(8,128)(2,1)S(1)}, bf16[32,256]{1,0:T(8,128)(2,1)S(1)}, u32[]{:S(2)}, u32[]{:S(2)}) collective-permute-start(bf16[32,256]{1,0:T(8,128)(2,1)S(1)} %shard_map.97.own_ref), channel_id=1, source_target_pairs={{0,8},{4,12},{8,0},{12,4},{16,24},{20,28},{24,16},{28,20},{1,9},{5... | collective-permute-start | bytes 49160 | tf_op jit(solution)/shard_map/ppermute | solution.py:146
  10.7 0.0 collective-permute-start.3
  10.7 2.2 %collective-permute-done.1.other_ref = bf16[32,256]{1,0:T(8,128)(2,1)S(1)} collective-permute-done((bf16[32,256]{1,0:T(8,128)(2,1)S(1)}, bf16[32,256]{1,0:T(8,128)(2,1)S(1)}, u32[]{:S(2)}, u32[]{:S(2)}) %collective-permute-start.1) | collective-permute-done | bytes 16416 | tf_op jit(solution)/shard_map/ppermute | solution.py:146
  12.9 0.0 copy-start
  12.9 0.0 collective-permute-done.4.piece_ref
  12.9 0.1 collective-permute-start.5
  12.9 2.7 %collective-permute-start.2 = (bf16[64,256]{1,0:T(8,128)(2,1)S(1)}, bf16[64,256]{1,0:T(8,128)(2,1)S(1)}, u32[]{:S(2)}, u32[]{:S(2)}) collective-permute-start(bf16[64,256]{1,0:T(8,128)(2,1)S(1)} %shard_map.98._.near_ref), channel_id=1, source_target_pairs={{0,16},{4,20},{8,24},{12,28},{16,0},{20,4},{24,8},{28,12},{1,17},{... | collective-permute-start | bytes 98312 | tf_op jit(solution)/shard_map/ppermute | solution.py:146
  15.6 0.8 %shard_map.95 = (bf16[128,1024]{1,0:T(8,128)(2,1)S(1)}, bf16[5,128,128]{2,1,0:T(8,128)(2,1)S(1)}, s32[3,8]{1,0:T(4,128)S(4)}) custom-call(s32[1]{0:T(128)S(6)} %copy.12.live_ref, s32[3,8]{1,0:T(4,128)} %targets_ref.1, bf16[2,8,512]{2,1,0:T(8,128)(2,1)} %bitcast.4), custom_call_target="tpu_custom_call" | custom-call | bytes 2097152 | tf_op jit(solution)/shard_map/pallas_call | solution.py:413
  16.4 0.0 collective-permute-done.3.refs_1_
  16.4 0.0 collective-permute-done.5.refs_3_
  16.4 0.0 copy-done
  16.4 0.2 %shard_map.100.leaf_w_ref = f32[2,16,512]{2,1,0:T(8,128)S(1)} custom-call(s32[1]{0:T(128)S(6)} %copy.12.live_ref, bf16[32,512]{1,0:T(8,128)(2,1)S(1)} %get-tuple-element.11.z_ref, bf16[2,128,512]{2,1,0:T(8,128)(2,1)S(1)} %copy-done, bf16[2,128,512]{2,1,0:T(8,128)(2,1)S(1)} %collective-permute-done.3.refs_1_, bf16[2,128,512]{2,1,0:T(8,128)(2,1)S(1)} %shard_map.99.refs_2_, ...), custom_call_target="tpu_custom_call" | custom-call | flops 33554432 | bytes 1048576 | tf_op jit(solution)/shard_map/pallas_call | solution.py:383
  16.7 1.2 %collective-permute-done.2.far_ref = bf16[64,256]{1,0:T(8,128)(2,1)S(1)} collective-permute-done((bf16[64,256]{1,0:T(8,128)(2,1)S(1)}, bf16[64,256]{1,0:T(8,128)(2,1)S(1)}, u32[]{:S(2)}, u32[]{:S(2)}) %collective-permute-start.2) | collective-permute-done | bytes 32800 | tf_op jit(solution)/shard_map/ppermute | solution.py:146
  17.8 1.6 %shard_map.101 = (f32[2,16,512]{2,1,0:T(8,128)}, f32[2,3,8,16]{3,2,1,0:T(8,128)}) custom-call(s32[3,8]{1,0:T(4,128)S(4)} %get-tuple-element.9.targets_ref, bf16[64,256]{1,0:T(8,128)(2,1)S(1)} %shard_map.98._.near_ref, bf16[64,256]{1,0:T(8,128)(2,1)S(1)} %collective-permute-done.2.far_ref, f32[2,16,512]{2,1,0:T(8,128)S(1)} %shard_map.100.leaf_w_ref, ...), custom_call_target="tpu_custom_call" | custom-call | tf_op jit(solution)/shard_map/pallas_call | solution.py:454
  (3 shorter events, 0.0 us)
Async XLA Ops:
  0.6 12.2 %collective-permute-start.4 = (bf16[2,128,512]{2,1,0:T(8,128)(2,1)}, bf16[2,128,512]{2,1,0:T(8,128)(2,1)S(1)}, u32[]{:S(2)}, u32[]{:S(2)}) collective-permute-start(bf16[2,128,512]{2,1,0:T(8,128)(2,1)} %refs_0_.3), channel_id=1, source_target_pairs={{0,2},{1,3},{2,0},{3,1},{4,6},{5,7},{6,4},{7,5},{8,10},{9,11},{10,... | collective-permute-start | bytes 786440 | tf_op jit(solution)/shard_map/ppermute | solution.py:146
  5.4 3.7 %collective-permute-start = (bf16[16,256]{1,0:T(8,128)(2,1)S(1)}, bf16[16,256]{1,0:T(8,128)(2,1)S(1)}, u32[]{:S(2)}, u32[]{:S(2)}) collective-permute-start(bf16[16,256]{1,0:T(8,128)(2,1)S(1)} %get-tuple-element.10.own_ref), channel_id=1, source_target_pairs={{0,4},{4,0},{8,12},{12,8},{16,20},{20,16},{24,28},{28,24},{1,5},{5... | collective-permute-start | bytes 24584 | tf_op jit(solution)/shard_map/ppermute | solution.py:146
  9.1 3.7 %collective-permute-start.1 = (bf16[32,256]{1,0:T(8,128)(2,1)S(1)}, bf16[32,256]{1,0:T(8,128)(2,1)S(1)}, u32[]{:S(2)}, u32[]{:S(2)}) collective-permute-start(bf16[32,256]{1,0:T(8,128)(2,1)S(1)} %shard_map.97.own_ref), channel_id=1, source_target_pairs={{0,8},{4,12},{8,0},{12,4},{16,24},{20,28},{24,16},{28,20},{1,9},{5... | collective-permute-start | bytes 49160 | tf_op jit(solution)/shard_map/ppermute | solution.py:146
  10.7 5.7 %collective-permute-start.3 = (bf16[2,128,512]{2,1,0:T(8,128)(2,1)}, bf16[2,128,512]{2,1,0:T(8,128)(2,1)S(1)}, u32[]{:S(2)}, u32[]{:S(2)}) collective-permute-start(bf16[2,128,512]{2,1,0:T(8,128)(2,1)} %refs_0_.3), channel_id=1, source_target_pairs={{0,1},{1,0},{2,3},{3,2},{4,5},{5,4},{6,7},{7,6},{8,9},{9,8},{10,11... | collective-permute-start | bytes 786440 | tf_op jit(solution)/shard_map/ppermute | solution.py:146
  12.9 3.6 %copy-start = (bf16[2,128,512]{2,1,0:T(8,128)(2,1)S(1)}, bf16[2,128,512]{2,1,0:T(8,128)(2,1)}, u32[]{:S(2)}) copy-start(bf16[2,128,512]{2,1,0:T(8,128)(2,1)} %refs_0_.3) | copy-start | bytes 786436
  12.9 3.5 %collective-permute-start.5 = (bf16[2,128,512]{2,1,0:T(8,128)(2,1)S(1)}, bf16[2,128,512]{2,1,0:T(8,128)(2,1)S(1)}, u32[]{:S(2)}, u32[]{:S(2)}) collective-permute-start(bf16[2,128,512]{2,1,0:T(8,128)(2,1)S(1)} %shard_map.99.refs_2_), channel_id=1, source_target_pairs={{0,1},{1,0},{2,3},{3,2},{4,5},{5,4},{6,7},{7,6},{8,9},{9,8},{10,11... | collective-permute-start | bytes 786440 | tf_op jit(solution)/shard_map/ppermute | solution.py:146
  12.9 4.9 %collective-permute-start.2 = (bf16[64,256]{1,0:T(8,128)(2,1)S(1)}, bf16[64,256]{1,0:T(8,128)(2,1)S(1)}, u32[]{:S(2)}, u32[]{:S(2)}) collective-permute-start(bf16[64,256]{1,0:T(8,128)(2,1)S(1)} %shard_map.98._.near_ref), channel_id=1, source_target_pairs={{0,16},{4,20},{8,24},{12,28},{16,0},{20,4},{24,8},{28,12},{1,17},{... | collective-permute-start | bytes 98312 | tf_op jit(solution)/shard_map/ppermute | solution.py:146

commit v3 on v2

--- a/solution.py
+++ b/solution.py
@@ -170,17 +170,11 @@
     return jnp.where(live, stacked, 0.0).astype(jnp.bfloat16), live
 
 
-def pack_kernel(live_ref, *refs):
-    sources, (out_ref, z_ref), places, sems = refs[:5], refs[5:7], refs[7:12], refs[12]
-    copies = [
-        pltpu.make_async_copy(source, place, sems.at[which])
-        for which, (source, place) in enumerate(zip(sources, places))
-    ]
-    for copy in copies:
-        copy.start()
-    for copy in copies:
-        copy.wait()
-    leaf_rhs_ref, low_ref, rhs_ref, inv_ref, sep_low_ref = places
+def first_kernel(out_ref):
+    out_ref[...] = jnp.zeros_like(out_ref)
+
+
+def pack_kernel(live_ref, _, leaf_rhs_ref, low_ref, rhs_ref, inv_ref, sep_low_ref, out_ref, z_ref):
     columns = leaf_rhs_ref.shape[1]
     depth = rhs_ref.shape[1]
     leaf_z, _ = masked_rows(leaf_rhs_ref[...], live_ref)
@@ -226,7 +220,7 @@
     out_ref[1] = jnp.where(live, imag_acc[:columns] + real_acc[columns:], 0.0)
 
 
-def prepare_kernel(low_start, live_ref, targets_ref, low_ref, panel_ref, pick_ref, kept_ref):
+def prepare_kernel(low_start, live_ref, targets_ref, low_ref, _, panel_ref, pick_ref, kept_ref):
     for level in range(targets_ref.shape[0]):
         for block in range(targets_ref.shape[1]):
             kept_ref[level, block] = targets_ref[level, block]
@@ -399,17 +393,41 @@
         return level_by_level(leaf_rhs, sep_rhs, leaf_w, leaf_low, sep_inv, sep_low, leaf_live, targets)
 
     tree_parts = (leaf_rhs, panel, tree_rhs, sep_inv, sep_low)
+    first = pl.pallas_call(
+        first_kernel,
+        out_shape=pltpu.VMEM((8, 128), jnp.float32),
+        out_specs=whole(VMEM),
+        cost_estimate=pl.CostEstimate(flops=10**9, bytes_accessed=0, transcendentals=0),
+    )()
     held, leaf_z = pl.pallas_call(
         pack_kernel,
         out_shape=(
             pltpu.VMEM((slab, 2 * size), jnp.bfloat16),
             pltpu.VMEM((2 * columns, leaf_rows), jnp.bfloat16),
         ),
-        in_specs=[whole(SMEM)] + [whole(pl.ANY)] * 5,
+        in_specs=[whole(SMEM)] + [whole(VMEM)] * 6,
         out_specs=(whole(VMEM),) * 2,
-        scratch_shapes=[pltpu.VMEM(part.shape, part.dtype) for part in tree_parts]
-        + [pltpu.SemaphoreType.DMA((5,))],
-    )(leaf_live, *tree_parts)
+    )(leaf_live, *[in_vmem(part) for part in (first,) + tree_parts])
+
+    def join(own, other, flops):
+        return pl.pallas_call(
+            join_kernel,
+            out_shape=pltpu.VMEM((2 * own.shape[0], own.shape[1]), own.dtype),
+            in_specs=[whole(VMEM)] * 2,
+            out_specs=whole(VMEM),
+            cost_estimate=pl.CostEstimate(
+                flops=flops, bytes_accessed=0, transcendentals=0
+            ),
+        )(in_vmem(own), in_vmem(other))
+
+    rounds = [held]
+    offset = 1
+    while offset < devices:
+        rounds.append(xor_permute(held, "leaf", offset))
+        offset *= 2
+        if offset < devices:
+            held = join(held, rounds[-1], 10**11 if offset == 2 else 0)
+
     panel_rows, picks, kept_targets = pl.pallas_call(
         functools.partial(prepare_kernel, (1 + depth) * columns),
         out_shape=(
@@ -417,29 +435,10 @@
             pltpu.VMEM((2 * depth - 1, size, size), jnp.bfloat16),
             pltpu.SMEM(targets.shape, jnp.int32),
         ),
-        in_specs=[whole(SMEM), whole(SMEM), whole(VMEM)],
+        in_specs=[whole(SMEM), whole(SMEM), whole(VMEM), whole(VMEM)],
         out_specs=(whole(VMEM),) * 2 + (whole(SMEM),),
-        cost_estimate=pl.CostEstimate(flops=0, bytes_accessed=2 * 1024 * 1024, transcendentals=0),
-    )(leaf_live, targets, panel)
-
-    def join(own, other):
-        return pl.pallas_call(
-            join_kernel,
-            out_shape=pltpu.VMEM((2 * own.shape[0], own.shape[1]), own.dtype),
-            in_specs=[whole(VMEM)] * 2,
-            out_specs=whole(VMEM),
-            cost_estimate=pl.CostEstimate(
-                flops=0, bytes_accessed=32 * 1024 * 1024, transcendentals=0
-            ),
-        )(in_vmem(own), in_vmem(other))
-
-    rounds = [held]
-    offset = 1
-    while offset < devices:
-        rounds.append(xor_permute(held, "leaf", offset))
-        offset *= 2
-        if offset < devices:
-            held = join(held, rounds[-1])
+        cost_estimate=pl.CostEstimate(flops=10**11, bytes_accessed=0, transcendentals=0),
+    )(leaf_live, targets, panel, in_vmem(held))
 
     def hold(piece):
         return pl.pallas_call(

time: 19.7 us -> 16.9 us (0.86)
  waiting for transfers between devices: 5.45 us -> 2.68 us
  Pallas kernels: 3.76 us -> 2.87 us
  starting transfers between devices: 8.89 us -> 9.58 us
    ppermute x6, waiting for transfers between devices: 5.45 us -> 2.68 us  [xor_permute(): lax.ppermute(values_in, axis, [(source, source ^ offset) for source in ra...]
    pallas_call x1, Pallas kernels: 1.09 us -> 0.2 us  [body(): pl.pallas_call(pack_kernel, out_shape=(pltpu.VMEM((slab, 2 * size), jnp.b...]
    ppermute x6, starting transfers between devices: 8.89 us -> 9.58 us  [xor_permute(): lax.ppermute(values_in, axis, [(source, source ^ offset) for source in ra...]
  transfers between devices with their start and end apart: 6 -> 6, of which waited for: 3 -> 4; matrix products, arithmetic and copies ran while one was open for 0% -> 0% of each run, Pallas kernels for 11% -> 6%
where the time goes in v3:
time: 16.9 us; the launch traced here: 16.7 us
  starting transfers between devices  9.58 us (57%)
  Pallas kernels  2.87 us (17%)
  waiting for transfers between devices  2.68 us (16%)
  between operations  1.42 us (8%)
    ppermute x6, starting transfers between devices, xor_permute(): lax.ppermute(values_in, axis, [(source, source ^ offset) for source in ra...  9.58 us
    ppermute x6, waiting for transfers between devices, xor_permute(): lax.ppermute(values_in, axis, [(source, source ^ offset) for source in ra...  2.68 us
    pallas_call x1, Pallas kernels, body(): pl.pallas_call(tree_kernel, out_shape=(jax.ShapeDtypeStruct((2, columns,...  1.64 us
    pallas_call x1, Pallas kernels, body(): pl.pallas_call(functools.partial(prepare_kernel, (1 + depth) * columns),...  0.78 us
  transfers between devices with their start and end apart: 6, of which 4 were waited for; matrix products, arithmetic and copies ran while one was open for 0% of the time, Pallas kernels for 6%

profile of v3, /device:TPU:0, one launch (start us, length us, event | category | flops | bytes accessed | tf_op | source)
XLA Modules:
  0.0 16.7 jit_solution(5008088965550265835)
XLA Ops:
  0.6 0.0 copy-start.2
  0.6 0.0 copy-start.1
  0.7 0.0 copy-start
  0.7 0.0 copy-start.3
  0.7 0.0 copy-start.5
  0.7 0.0 copy-start.4
  1.4 0.0 copy-done.2
  1.4 0.1 copy-done.1
  1.5 0.0 copy-done.3
  1.5 0.0 copy-done.5
  1.5 0.0 copy-done.4
  1.5 0.2 %shard_map.96 = (bf16[16,256]{1,0:T(8,128)(2,1)S(1)}, bf16[32,512]{1,0:T(8,128)(2,1)S(1)}) custom-call(s32[1]{0:T(128)S(6)} %copy.12.live_ref, f32[8,128]{1,0:T(8,128)S(1)} %shard_map.95._, f32[2,16,512]{2,1,0:T(8,128)S(1)} %copy-done.1, bf16[2,8,512]{2,1,0:T(8,128)(2,1)S(1)} %bitcast.5, f32[2,3,8,16]{3,2,1,0:T(8,128)S(1)} %bitcast.3, ...), custom_call_target="tpu_custom_call" | custom-call | tf_op jit(solution)/shard_map/pallas_call | solution.py:402
  1.7 3.0 %collective-permute-start = (bf16[16,256]{1,0:T(8,128)(2,1)S(1)}, bf16[16,256]{1,0:T(8,128)(2,1)S(1)}, u32[]{:S(2)}, u32[]{:S(2)}) collective-permute-start(bf16[16,256]{1,0:T(8,128)(2,1)S(1)} %get-tuple-element.9.own_ref), channel_id=1, source_target_pairs={{0,4},{4,0},{8,12},{12,8},{16,20},{20,16},{24,28},{28,24},{1,5},{5... | collective-permute-start | bytes 24584 | tf_op jit(solution)/shard_map/ppermute | solution.py:146
  4.7 0.0 copy-done
  4.7 1.5 %collective-permute-start.4 = (bf16[2,128,512]{2,1,0:T(8,128)(2,1)S(1)}, bf16[2,128,512]{2,1,0:T(8,128)(2,1)S(1)}, u32[]{:S(2)}, u32[]{:S(2)}) collective-permute-start(bf16[2,128,512]{2,1,0:T(8,128)(2,1)S(1)} %copy-done), channel_id=1, source_target_pairs={{0,2},{1,3},{2,0},{3,1},{4,6},{5,7},{6,4},{7,5},{8,10},{9,11},{10,... | collective-permute-start | bytes 786440 | tf_op jit(solution)/shard_map/ppermute | solution.py:146
  6.2 0.1 collective-permute-done.other_ref
  6.3 2.1 %collective-permute-start.1 = (bf16[32,256]{1,0:T(8,128)(2,1)S(1)}, bf16[32,256]{1,0:T(8,128)(2,1)S(1)}, u32[]{:S(2)}, u32[]{:S(2)}) collective-permute-start(bf16[32,256]{1,0:T(8,128)(2,1)S(1)} %shard_map.97.own_ref), channel_id=1, source_target_pairs={{0,8},{4,12},{8,0},{12,4},{16,24},{20,28},{24,16},{28,20},{1,9},{5... | collective-permute-start | bytes 49160 | tf_op jit(solution)/shard_map/ppermute | solution.py:146
  8.4 0.0 collective-permute-start.3
  8.4 1.7 %collective-permute-done.1.other_ref = bf16[32,256]{1,0:T(8,128)(2,1)S(1)} collective-permute-done((bf16[32,256]{1,0:T(8,128)(2,1)S(1)}, bf16[32,256]{1,0:T(8,128)(2,1)S(1)}, u32[]{:S(2)}, u32[]{:S(2)}) %collective-permute-start.1) | collective-permute-done | bytes 16416 | tf_op jit(solution)/shard_map/ppermute | solution.py:146
  10.1 3.0 %collective-permute-start.2 = (bf16[64,256]{1,0:T(8,128)(2,1)S(1)}, bf16[64,256]{1,0:T(8,128)(2,1)S(1)}, u32[]{:S(2)}, u32[]{:S(2)}) collective-permute-start(bf16[64,256]{1,0:T(8,128)(2,1)S(1)} %shard_map.98._.near_ref), channel_id=1, source_target_pairs={{0,16},{4,20},{8,24},{12,28},{16,0},{20,4},{24,8},{28,12},{1,17},{... | collective-permute-start | bytes 98312 | tf_op jit(solution)/shard_map/ppermute | solution.py:146
  13.1 0.0 collective-permute-done.4.piece_ref
  13.1 0.0 collective-permute-start.5
  13.1 0.8 %shard_map.99 = (bf16[128,1024]{1,0:T(8,128)(2,1)S(1)}, bf16[5,128,128]{2,1,0:T(8,128)(2,1)S(1)}, s32[3,8]{1,0:T(4,128)S(4)}) custom-call(s32[1]{0:T(128)S(6)} %copy.12.live_ref, s32[3,8]{1,0:T(4,128)} %targets_ref.1, bf16[2,8,512]{2,1,0:T(8,128)(2,1)} %bitcast.4, bf16[64,256]{1,0:T(8,128)(2,1)S(1)} %shard_map.98._.near_ref), custom_call_target="tpu_custom_call" | custom-call | flops 99999997952 | tf_op jit(solution)/shard_map/pallas_call | solution.py:431
  13.9 0.0 collective-permute-done.3.refs_1_
  13.9 0.7 %collective-permute-done.5.refs_3_ = bf16[2,128,512]{2,1,0:T(8,128)(2,1)S(1)} collective-permute-done((bf16[2,128,512]{2,1,0:T(8,128)(2,1)S(1)}, bf16[2,128,512]{2,1,0:T(8,128)(2,1)S(1)}, u32[]{:S(2)}, u32[]{:S(2)}) %collective-permute-start.5) | collective-permute-done | bytes 262176 | tf_op jit(solution)/shard_map/ppermute | solution.py:146
  14.7 0.2 %shard_map.101.leaf_w_ref = f32[2,16,512]{2,1,0:T(8,128)S(1)} custom-call(s32[1]{0:T(128)S(6)} %copy.12.live_ref, bf16[32,512]{1,0:T(8,128)(2,1)S(1)} %get-tuple-element.11.z_ref, bf16[2,128,512]{2,1,0:T(8,128)(2,1)S(1)} %copy-done, bf16[2,128,512]{2,1,0:T(8,128)(2,1)S(1)} %collective-permute-done.3.refs_1_, bf16[2,128,512]{2,1,0:T(8,128)(2,1)S(1)} %shard_map.100.refs_2_, ...), custom_call_target="tpu_custom_call" | custom-call | flops 33554432 | bytes 1048576 | tf_op jit(solution)/shard_map/pallas_call | solution.py:377
  14.9 0.1 collective-permute-done.2.far_ref
  15.0 1.6 %shard_map.102 = (f32[2,16,512]{2,1,0:T(8,128)}, f32[2,3,8,16]{3,2,1,0:T(8,128)}) custom-call(s32[3,8]{1,0:T(4,128)S(4)} %get-tuple-element.10.targets_ref, bf16[64,256]{1,0:T(8,128)(2,1)S(1)} %shard_map.98._.near_ref, bf16[64,256]{1,0:T(8,128)(2,1)S(1)} %collective-permute-done.2.far_ref, f32[2,16,512]{2,1,0:T(8,128)S(1)} %shard_map.101.leaf_w_ref, ...), custom_call_target="tpu_custom_call" | custom-call | tf_op jit(solution)/shard_map/pallas_call | solution.py:453
  (4 shorter events, 0.0 us)
Async XLA Ops:
  0.6 0.8 %copy-start.2 = (f32[2,16,3,8]{1,3,2,0:T(8,128)S(1)}, f32[2,16,3,8]{1,3,2,0:T(8,128)}, u32[]{:S(2)}) copy-start(f32[2,16,3,8]{1,3,2,0:T(8,128)} %param.9) | copy-start | bytes 9220
  0.6 0.8 %copy-start.1 = (f32[2,16,512]{2,1,0:T(8,128)S(1)}, f32[2,16,512]{2,1,0:T(8,128)}, u32[]{:S(2)}) copy-start(f32[2,16,512]{2,1,0:T(8,128)} %leaf_rhs_ref.1) | copy-start | bytes 196612
  0.7 4.0 %copy-start = (bf16[2,128,512]{2,1,0:T(8,128)(2,1)S(1)}, bf16[2,128,512]{2,1,0:T(8,128)(2,1)}, u32[]{:S(2)}) copy-start(bf16[2,128,512]{2,1,0:T(8,128)(2,1)} %refs_0_.1) | copy-start | bytes 786436
  0.7 0.8 %copy-start.3 = (bf16[2,512,8]{1,2,0:T(8,128)(2,1)S(1)}, bf16[2,512,8]{1,2,0:T(8,128)(2,1)}, u32[]{:S(2)}) copy-start(bf16[2,512,8]{1,2,0:T(8,128)(2,1)} %param.11) | copy-start | bytes 49156
  0.7 0.8 %copy-start.5 = (bf16[2,8,48]{2,1,0:T(8,128)(2,1)S(1)}, bf16[2,8,48]{2,1,0:T(8,128)(2,1)}, u32[]{:S(2)}) copy-start(bf16[2,8,48]{2,1,0:T(8,128)(2,1)} %sep_low_ref.1) | copy-start | bytes 4612
  0.7 0.8 %copy-start.4 = (bf16[2,8,112]{2,1,0:T(8,128)(2,1)S(1)}, bf16[2,8,112]{2,1,0:T(8,128)(2,1)}, u32[]{:S(2)}) copy-start(bf16[2,8,112]{2,1,0:T(8,128)(2,1)} %inv_ref.1) | copy-start | bytes 10756
  1.7 4.6 %collective-permute-start = (bf16[16,256]{1,0:T(8,128)(2,1)S(1)}, bf16[16,256]{1,0:T(8,128)(2,1)S(1)}, u32[]{:S(2)}, u32[]{:S(2)}) collective-permute-start(bf16[16,256]{1,0:T(8,128)(2,1)S(1)} %get-tuple-element.9.own_ref), channel_id=1, source_target_pairs={{0,4},{4,0},{8,12},{12,8},{16,20},{20,16},{24,28},{28,24},{1,5},{5... | collective-permute-start | bytes 24584 | tf_op jit(solution)/shard_map/ppermute | solution.py:146
  4.7 8.5 %collective-permute-start.4 = (bf16[2,128,512]{2,1,0:T(8,128)(2,1)S(1)}, bf16[2,128,512]{2,1,0:T(8,128)(2,1)S(1)}, u32[]{:S(2)}, u32[]{:S(2)}) collective-permute-start(bf16[2,128,512]{2,1,0:T(8,128)(2,1)S(1)} %copy-done), channel_id=1, source_target_pairs={{0,2},{1,3},{2,0},{3,1},{4,6},{5,7},{6,4},{7,5},{8,10},{9,11},{10,... | collective-permute-start | bytes 786440 | tf_op jit(solution)/shard_map/ppermute | solution.py:146
  6.3 3.8 %collective-permute-start.1 = (bf16[32,256]{1,0:T(8,128)(2,1)S(1)}, bf16[32,256]{1,0:T(8,128)(2,1)S(1)}, u32[]{:S(2)}, u32[]{:S(2)}) collective-permute-start(bf16[32,256]{1,0:T(8,128)(2,1)S(1)} %shard_map.97.own_ref), channel_id=1, source_target_pairs={{0,8},{4,12},{8,0},{12,4},{16,24},{20,28},{24,16},{28,20},{1,9},{5... | collective-permute-start | bytes 49160 | tf_op jit(solution)/shard_map/ppermute | solution.py:146
  8.4 5.6 %collective-permute-start.3 = (bf16[2,128,512]{2,1,0:T(8,128)(2,1)S(1)}, bf16[2,128,512]{2,1,0:T(8,128)(2,1)S(1)}, u32[]{:S(2)}, u32[]{:S(2)}) collective-permute-start(bf16[2,128,512]{2,1,0:T(8,128)(2,1)S(1)} %copy-done), channel_id=1, source_target_pairs={{0,1},{1,0},{2,3},{3,2},{4,5},{5,4},{6,7},{7,6},{8,9},{9,8},{10,11... | collective-permute-start | bytes 786440 | tf_op jit(solution)/shard_map/ppermute | solution.py:146
  10.1 4.9 %collective-permute-start.2 = (bf16[64,256]{1,0:T(8,128)(2,1)S(1)}, bf16[64,256]{1,0:T(8,128)(2,1)S(1)}, u32[]{:S(2)}, u32[]{:S(2)}) collective-permute-start(bf16[64,256]{1,0:T(8,128)(2,1)S(1)} %shard_map.98._.near_ref), channel_id=1, source_target_pairs={{0,16},{4,20},{8,24},{12,28},{16,0},{20,4},{24,8},{28,12},{1,17},{... | collective-permute-start | bytes 98312 | tf_op jit(solution)/shard_map/ppermute | solution.py:146
  13.1 1.5 %collective-permute-start.5 = (bf16[2,128,512]{2,1,0:T(8,128)(2,1)S(1)}, bf16[2,128,512]{2,1,0:T(8,128)(2,1)S(1)}, u32[]{:S(2)}, u32[]{:S(2)}) collective-permute-start(bf16[2,128,512]{2,1,0:T(8,128)(2,1)S(1)} %shard_map.100.refs_2_), channel_id=1, source_target_pairs={{0,1},{1,0},{2,3},{3,2},{4,5},{5,4},{6,7},{7,6},{8,9},{9,8},{10,11... | collective-permute-start | bytes 786440 | tf_op jit(solution)/shard_map/ppermute | solution.py:146

commit v4 on v3

--- a/solution.py
+++ b/solution.py
@@ -146,19 +146,6 @@
     return lax.ppermute(values_in, axis, [(source, source ^ offset) for source in range(count)])
 
 
-def gather_pieces(own_piece, hold=lambda piece: piece):
-    parts = lax.axis_size("rhs")
-    pieces = {0: own_piece}
-    offset = parts // 2
-    while offset >= 1:
-        for known in list(pieces):
-            source = pieces[known] if known == 0 else hold(pieces[known])
-            pieces[known] = source
-            pieces[known ^ offset] = xor_permute(source, "rhs", offset)
-        offset //= 2
-    return [pieces[step] for step in range(parts)]
-
-
 def in_vmem(values_in):
     return pltpu.with_memory_space_constraint(values_in, VMEM)
 
@@ -174,7 +161,7 @@
     out_ref[...] = jnp.zeros_like(out_ref)
 
 
-def pack_kernel(live_ref, _, leaf_rhs_ref, low_ref, rhs_ref, inv_ref, sep_low_ref, out_ref, z_ref):
+def pack_kernel(live_ref, _, leaf_rhs_ref, low_ref, rhs_ref, inv_ref, sep_low_ref, out_ref, tile_ref, z_ref):
     columns = leaf_rhs_ref.shape[1]
     depth = rhs_ref.shape[1]
     leaf_z, _ = masked_rows(leaf_rhs_ref[...], live_ref)
@@ -199,25 +186,26 @@
         if inv_ref.shape[2] < 128:
             pieces.append(jnp.zeros((width, 128 - inv_ref.shape[2]), jnp.float32))
         halves.append(jnp.concatenate(pieces, axis=1))
-    out_ref[...] = jnp.concatenate(halves, axis=0).astype(jnp.bfloat16)
-
-
-def leaf_kernel(parts, live_ref, z_ref, *refs):
-    inv_refs, out_ref = refs[:parts], refs[parts]
-    columns = out_ref.shape[1]
-    depth = inv_refs[0].shape[1]
-    mine = lax.axis_index("rhs")
-    total = [None, None]
-    for step in range(parts):
-        owner = mine ^ step
-        piece = z_ref[:, pl.ds(pl.multiple_of(owner * depth, 128), depth)]
-        for part in range(2):
-            term = jnp.dot(piece, inv_refs[step][part], preferred_element_type=jnp.float32)
-            total[part] = term if step == 0 else total[part] + term
-    real_acc, imag_acc = total
-    live = lax.broadcasted_iota(jnp.int32, (1, z_ref.shape[1]), 1) < live_ref[0] * 128
-    out_ref[0] = jnp.where(live, real_acc[:columns] - imag_acc[columns:], 0.0)
-    out_ref[1] = jnp.where(live, imag_acc[:columns] + real_acc[columns:], 0.0)
+    packed = jnp.concatenate(halves, axis=0).astype(jnp.bfloat16)
+    out_ref[...] = packed
+    tile_ref[...] = packed[:, : tile_ref.shape[1]]
+
+
+def piece_product(step, z_ref, piece_ref):
+    columns = z_ref.shape[0] // 2
+    depth = piece_ref.shape[1]
+    owner = lax.axis_index("rhs") ^ step
+    rows = z_ref[:, pl.ds(pl.multiple_of(owner * depth, 128), depth)]
+    real_acc = jnp.dot(rows, piece_ref[0], preferred_element_type=jnp.float32)
+    imag_acc = jnp.dot(rows, piece_ref[1], preferred_element_type=jnp.float32)
+    return real_acc[:columns] - imag_acc[columns:], imag_acc[:columns] + real_acc[columns:]
+
+
+def leaf_kernel(steps, z_ref, *refs):
+    out_ref = refs[-1]
+    products = [piece_product(step, z_ref, piece_ref) for step, piece_ref in zip(steps, refs[:-1])]
+    for part in range(2):
+        out_ref[part] = sum(product[part] for product in products)
 
 
 def prepare_kernel(low_start, live_ref, targets_ref, low_ref, _, panel_ref, pick_ref, kept_ref):
@@ -255,24 +243,44 @@
             ).astype(jnp.bfloat16)
 
 
-def join_kernel(own_ref, other_ref, out_ref):
-    rows = own_ref.shape[0]
-    out_ref[:rows] = own_ref[...]
-    out_ref[rows:] = other_ref[...]
+def join_first_kernel(own_ref, received_ref, pair_ref, out_ref, tile_ref):
+    rows, lanes = own_ref.shape
+    tile = pair_ref.shape[1]
+    out_ref[:rows, :lanes] = own_ref[...]
+    out_ref[rows:, :lanes] = received_ref[...]
+    out_ref[:rows, lanes:] = pair_ref[...]
+    out_ref[rows:, lanes:] = pair_ref[...]
+    tile_ref[...] = received_ref[:, :tile]
+
+
+def join_second_kernel(side_lanes, own_ref, first_ref, pair_ref, second_ref, _, out_ref):
+    rows, lanes = own_ref.shape
+    tile = pair_ref.shape[1]
+    out_ref[:rows, :] = own_ref[...]
+    out_ref[rows : 2 * rows, :tile] = pair_ref[...]
+    out_ref[rows : 2 * rows, tile:] = first_ref[:, tile:]
+    lane = lax.broadcasted_iota(jnp.int32, (rows, tile), 1)
+    merged = jnp.where(
+        lane < side_lanes,
+        second_ref[:rows, lanes:].astype(jnp.float32),
+        second_ref[:rows, :tile].astype(jnp.float32),
+    )
+    out_ref[2 * rows : 3 * rows, :tile] = merged.astype(jnp.bfloat16)
+    out_ref[2 * rows : 3 * rows, tile:] = second_ref[:rows, tile:lanes]
+    out_ref[3 * rows :, :] = second_ref[rows:, :lanes]
 
 
 def hold_kernel(piece_ref, _, out_ref):
-    pass
+    out_ref[...] = piece_ref[...]
 
 
 def tree_kernel(
-    targets_ref, near_ref, far_ref, leaf_w_ref, panel_ref, pick_ref, leaf_out_ref, sep_out_ref, all_ref, turn_ref
+    targets_ref, near_ref, far_ref, pick_ref, _, parent_ref, sep_out_ref, all_ref, turn_ref
 ):
     depth, devices = targets_ref.shape
-    size = panel_ref.shape[0]
+    columns, size = parent_ref.shape
     slab = size // devices
     width = slab // 2
-    columns = leaf_w_ref.shape[1]
     device = lax.axis_index("leaf")
     row = lax.broadcasted_iota(jnp.int32, (size, size), 0)
     lane = lax.broadcasted_iota(jnp.int32, (size, size), 1)
@@ -335,13 +343,7 @@
         product = lax.dot_general(parent, lower[level], back, preferred_element_type=jnp.float32)
         solved[level] = partial[level] - product * sign
 
-    leaf_rows = leaf_w_ref.shape[2]
-    product = jnp.dot(
-        solved[1].astype(jnp.bfloat16), panel_ref[...], preferred_element_type=jnp.float32
-    )
-    for part in range(2):
-        leaf_out_ref[part] = leaf_w_ref[part] - product[:, part * leaf_rows : (part + 1) * leaf_rows]
-
+    parent_ref[...] = solved[1].astype(jnp.bfloat16)
     stacked = jnp.concatenate(
         solved[1:] + [jnp.zeros((size - depth * columns, size), jnp.float32)], axis=0
     )
@@ -357,6 +359,20 @@
             ]
 
 
+def finish_kernel(steps, live_ref, z_ref, partial_ref, parent_ref, panel_ref, sep_ref, *refs):
+    leaf_out_ref, sep_out_ref = refs[-2:]
+    leaf_rows = leaf_out_ref.shape[2]
+    live = lax.broadcasted_iota(jnp.int32, (1, leaf_rows), 1) < live_ref[0] * 128
+    products = [piece_product(step, z_ref, piece_ref) for step, piece_ref in zip(steps, refs[:-2])]
+    from_tree = jnp.dot(parent_ref[...], panel_ref[...], preferred_element_type=jnp.float32)
+    for part in range(2):
+        leaf_w = partial_ref[part] + sum(product[part] for product in products)
+        leaf_out_ref[part] = (
+            jnp.where(live, leaf_w, 0.0) - from_tree[:, part * leaf_rows : (part + 1) * leaf_rows]
+        )
+    sep_out_ref[...] = sep_ref[...]
+
+
 def whole(space):
     return pl.BlockSpec(memory_space=space)
 
@@ -368,28 +384,15 @@
     slab = 2 * width
     size = devices * slab
     small_tree = (
-        size == 128 and (1 + depth) * columns + sep_low.shape[2] <= 128 and sep_inv.shape[2] <= 128
+        devices == 8 and parts % 2 == 0 and size == 128 and (1 + depth) * columns + sep_low.shape[2] <= 128 and sep_inv.shape[2] <= 128
     )
     panel = leaf_low.transpose(0, 2, 1)
     tree_rhs = sep_rhs.transpose(0, 2, 3, 1)
 
-    def leaf_w_of(leaf_z, pieces):
-        return pl.pallas_call(
-            functools.partial(leaf_kernel, parts),
-            out_shape=pltpu.VMEM((2, columns, leaf_rows), jnp.float32),
-            in_specs=[whole(SMEM)] + [whole(VMEM)] * (1 + parts),
-            out_specs=whole(VMEM),
-            cost_estimate=pl.CostEstimate(
-                flops=8 * columns * leaf_rows * leaf_rows,
-                bytes_accessed=4 * leaf_rows * leaf_rows,
-                transcendentals=0,
-            ),
-        )(leaf_live, *[in_vmem(ready) for ready in [leaf_z] + pieces])
-
     if not small_tree:
         live_mask = (jnp.arange(leaf_rows) < leaf_live[0] * 128).astype(jnp.float32)
-        leaf_z = (leaf_rhs * live_mask).astype(jnp.bfloat16).reshape(2 * columns, leaf_rows)
-        leaf_w = leaf_w_of(leaf_z, gather_pieces(leaf_inv))
+        leaf_z = (leaf_rhs * live_mask).astype(jnp.bfloat16)
+        leaf_w = complex_dot(leaf_z, lax.all_gather(leaf_inv, "rhs", axis=1, tiled=True)) * live_mask
         return level_by_level(leaf_rhs, sep_rhs, leaf_w, leaf_low, sep_inv, sep_low, leaf_live, targets)
 
     tree_parts = (leaf_rhs, panel, tree_rhs, sep_inv, sep_low)
@@ -399,35 +402,38 @@
         out_specs=whole(VMEM),
         cost_estimate=pl.CostEstimate(flops=10**9, bytes_accessed=0, transcendentals=0),
     )()
-    held, leaf_z = pl.pallas_call(
+    held, own_tile, leaf_z = pl.pallas_call(
         pack_kernel,
         out_shape=(
             pltpu.VMEM((slab, 2 * size), jnp.bfloat16),
+            pltpu.VMEM((slab, size), jnp.bfloat16),
             pltpu.VMEM((2 * columns, leaf_rows), jnp.bfloat16),
         ),
         in_specs=[whole(SMEM)] + [whole(VMEM)] * 6,
+        out_specs=(whole(VMEM),) * 3,
+    )(leaf_live, *[in_vmem(part) for part in (first,) + tree_parts])
+
+    def exchange(values_in, offset, flip):
+        partners = [
+            (source * parts + part, (source ^ offset) * parts + (part ^ flip))
+            for source in range(devices)
+            for part in range(parts)
+        ]
+        return lax.ppermute(values_in, ("leaf", "rhs"), partners)
+
+    first_round = exchange(held, 1, 1)
+    pair_tile = xor_permute(own_tile, "rhs", 1)
+    second_part, first_tile = pl.pallas_call(
+        join_first_kernel,
+        out_shape=(
+            pltpu.VMEM((2 * slab, 3 * size), jnp.bfloat16),
+            pltpu.VMEM((slab, size), jnp.bfloat16),
+        ),
+        in_specs=[whole(VMEM)] * 3,
         out_specs=(whole(VMEM),) * 2,
-    )(leaf_live, *[in_vmem(part) for part in (first,) + tree_parts])
-
-    def join(own, other, flops):
-        return pl.pallas_call(
-            join_kernel,
-            out_shape=pltpu.VMEM((2 * own.shape[0], own.shape[1]), own.dtype),
-            in_specs=[whole(VMEM)] * 2,
-            out_specs=whole(VMEM),
-            cost_estimate=pl.CostEstimate(
-                flops=flops, bytes_accessed=0, transcendentals=0
-            ),
-        )(in_vmem(own), in_vmem(other))
-
-    rounds = [held]
-    offset = 1
-    while offset < devices:
-        rounds.append(xor_permute(held, "leaf", offset))
-        offset *= 2
-        if offset < devices:
-            held = join(held, rounds[-1], 10**11 if offset == 2 else 0)
-
+        cost_estimate=pl.CostEstimate(flops=10**11, bytes_accessed=0, transcendentals=0),
+    )(in_vmem(held), in_vmem(first_round), in_vmem(pair_tile))
+    second_round = exchange(second_part, 2, 1)
     panel_rows, picks, kept_targets = pl.pallas_call(
         functools.partial(prepare_kernel, (1 + depth) * columns),
         out_shape=(
@@ -437,8 +443,18 @@
         ),
         in_specs=[whole(SMEM), whole(SMEM), whole(VMEM), whole(VMEM)],
         out_specs=(whole(VMEM),) * 2 + (whole(SMEM),),
-        cost_estimate=pl.CostEstimate(flops=10**11, bytes_accessed=0, transcendentals=0),
-    )(leaf_live, targets, panel, in_vmem(held))
+        cost_estimate=pl.CostEstimate(flops=0, bytes_accessed=0, transcendentals=0),
+    )(leaf_live, targets, panel, in_vmem(first_tile))
+
+    pair_first = xor_permute(first_tile, "rhs", 1)
+    held = pl.pallas_call(
+        functools.partial(join_second_kernel, (1 + depth) * columns),
+        out_shape=pltpu.VMEM((4 * slab, 2 * size), jnp.bfloat16),
+        in_specs=[whole(VMEM)] * 5,
+        out_specs=whole(VMEM),
+        cost_estimate=pl.CostEstimate(flops=0, bytes_accessed=0, transcendentals=0),
+    )(*[in_vmem(ready) for ready in (held, first_round, pair_first, second_round, picks)])
+    far = exchange(held, 4, 0)
 
     def hold(piece):
         return pl.pallas_call(
@@ -446,25 +462,45 @@
             out_shape=pltpu.VMEM(piece.shape, piece.dtype),
             in_specs=[whole(VMEM)] * 2,
             out_specs=whole(VMEM),
-            input_output_aliases={0: 0},
         )(in_vmem(piece), in_vmem(held))
 
-    leaf_w = leaf_w_of(leaf_z, gather_pieces(leaf_inv, hold))
+    far_piece = hold(xor_permute(leaf_inv, "rhs", 3))
+    partial = pl.pallas_call(
+        functools.partial(leaf_kernel, (0, 3)),
+        out_shape=pltpu.VMEM((2, columns, leaf_rows), jnp.float32),
+        in_specs=[whole(VMEM)] * 3,
+        out_specs=whole(VMEM),
+        cost_estimate=pl.CostEstimate(flops=0, bytes_accessed=0, transcendentals=0),
+    )(*[in_vmem(ready) for ready in (leaf_z, leaf_inv, far_piece)])
+    parent_x, tree_sep = pl.pallas_call(
+        tree_kernel,
+        out_shape=(
+            pltpu.VMEM((columns, size), jnp.bfloat16),
+            pltpu.VMEM((2, depth, width, columns), jnp.float32),
+        ),
+        in_specs=[whole(SMEM)] + [whole(VMEM)] * 4,
+        out_specs=(whole(VMEM),) * 2,
+        scratch_shapes=[
+            pltpu.VMEM((size, 2 * size), jnp.bfloat16),
+            pltpu.VMEM((size, size), jnp.float32),
+        ],
+        cost_estimate=pl.CostEstimate(flops=3*10**9, bytes_accessed=0, transcendentals=0),
+    )(
+        pltpu.with_memory_space_constraint(kept_targets, SMEM),
+        *[in_vmem(ready) for ready in (held, far, picks, partial)],
+    )
+    pair_pieces = (xor_permute(leaf_inv, "rhs", 1), xor_permute(far_piece, "rhs", 1))
     leaf_x, sep_x = pl.pallas_call(
-        tree_kernel,
+        functools.partial(finish_kernel, (1, 2)),
         out_shape=(
             jax.ShapeDtypeStruct((2, columns, leaf_rows), jnp.float32),
             jax.ShapeDtypeStruct((2, depth, width, columns), jnp.float32),
         ),
-        in_specs=[whole(SMEM)] + [whole(VMEM)] * 5,
-        out_specs=(whole(VMEM), whole(VMEM)),
-        scratch_shapes=[
-            pltpu.VMEM((size, 2 * size), jnp.bfloat16),
-            pltpu.VMEM((size, size), jnp.float32),
-        ],
+        in_specs=[whole(SMEM)] + [whole(VMEM)] * 7,
+        out_specs=(whole(VMEM),) * 2,
     )(
-        pltpu.with_memory_space_constraint(kept_targets, SMEM),
-        *[in_vmem(ready) for ready in (held, rounds[-1], leaf_w, panel_rows, picks)],
+        leaf_live,
+        *[in_vmem(ready) for ready in (leaf_z, partial, parent_x, panel_rows, tree_sep) + pair_pieces],
     )
     return leaf_x, sep_x.transpose(0, 3, 1, 2)
 

time: 16.9 us -> 16.3 us (0.964)
  waiting for transfers between devices: 2.68 us -> 2.02 us
  Pallas kernels: 2.87 us -> 3.06 us
    ppermute x6 -> x5, starting transfers between devices: 9.58 us -> 2.48 us  [xor_permute(): lax.ppermute(values_in, axis, [(source, source ^ offset) for source in ra...]
    ppermute x0 -> x3, starting transfers between devices: none -> 7.03 us  [exchange(): return lax.ppermute(values_in, ('leaf', 'rhs'), partners)]
    ppermute x6 -> x5, waiting for transfers between devices: 2.68 us -> 0.99 us  [xor_permute(): lax.ppermute(values_in, axis, [(source, source ^ offset) for source in ra...]
    ppermute x0 -> x3, waiting for transfers between devices: none -> 1.03 us  [exchange(): return lax.ppermute(values_in, ('leaf', 'rhs'), partners)]
    pallas_call x4 -> x5, Pallas kernels: 1.89 us -> 2.07 us  [the longest x1 1.02 us: body(): pl.pallas_call(tree_kernel, out_shape=(pltpu.VMEM((columns, size), jnp.bf...]
  transfers between devices with their start and end apart: 6 -> 8, of which waited for: 4 -> 4; matrix products, arithmetic and copies ran while one was open for 0% -> 0% of each run, Pallas kernels for 6% -> 12%
where the time goes in v4:
time: 16.3 us; the launch traced here: 16.1 us
  starting transfers between devices  9.51 us (58%)
  Pallas kernels  3.06 us (19%)
  waiting for transfers between devices  2.02 us (12%)
  between operations  1.42 us (9%)
    ppermute x3, starting transfers between devices, exchange(): return lax.ppermute(values_in, ('leaf', 'rhs'), partners)  7.03 us
    ppermute x5, starting transfers between devices, xor_permute(): lax.ppermute(values_in, axis, [(source, source ^ offset) for source in ra...  2.48 us
    ppermute x3, waiting for transfers between devices, exchange(): return lax.ppermute(values_in, ('leaf', 'rhs'), partners)  1.03 us
    pallas_call x1, Pallas kernels, body(): pl.pallas_call(tree_kernel, out_shape=(pltpu.VMEM((columns, size), jnp.bf...  1.02 us
    ppermute x5, waiting for transfers between devices, xor_permute(): lax.ppermute(values_in, axis, [(source, source ^ offset) for source in ra...  0.99 us
    pallas_call x1, Pallas kernels, body(): pl.pallas_call(functools.partial(finish_kernel, (1, 2)), out_shape=(jax.S...  0.87 us
    pallas_call x1, Pallas kernels, body(): pl.pallas_call(functools.partial(prepare_kernel, (1 + depth) * columns),...  0.78 us
  transfers between devices with their start and end apart: 8, of which 4 were waited for; matrix products, arithmetic and copies ran while one was open for 0% of the time, Pallas kernels for 12%

profile of v4, /device:TPU:0, one launch (start us, length us, event | category | flops | bytes accessed | tf_op | source)
XLA Modules:
  0.0 16.1 jit_solution(5799221143325287084)
XLA Ops:
  0.6 0.0 copy-start.3
  0.6 0.0 copy-start.1
  0.7 0.0 copy-start
  0.7 0.0 copy-start.2
  0.7 0.0 copy-start.5
  0.7 0.0 copy-start.4
  1.4 0.0 copy-done.3
  1.4 0.1 copy-done.1
  1.5 0.0 copy-done.2
  1.5 0.0 copy-done.5
  1.5 0.0 copy-done.4
  1.5 0.2 %shard_map.96 = (bf16[16,256]{1,0:T(8,128)(2,1)S(1)}, bf16[16,128]{1,0:T(8,128)(2,1)S(1)}, bf16[32,512]{1,0:T(8,128)(2,1)S(1)}) custom-call(s32[1]{0:T(128)S(6)} %copy.10.live_ref, f32[8,128]{1,0:T(8,128)S(1)} %shard_map.95._, f32[2,16,512]{2,1,0:T(8,128)S(1)} %copy-done.1, bf16[2,8,512]{2,1,0:T(8,128)(2,1)S(1)} %bitcast.4, f32[2,3,8,16]{3,2,1,0:T(8,128)S(1)} %bitcast.5, ...), custom_call_target="tpu_custom_call" | custom-call | tf_op jit(solution)/shard_map/pallas_call | solution.py:405
  1.7 2.4 %collective-permute-start.1 = (bf16[16,256]{1,0:T(8,128)(2,1)S(1)}, bf16[16,256]{1,0:T(8,128)(2,1)S(1)}, u32[]{:S(2)}, u32[]{:S(2)}) collective-permute-start(bf16[16,256]{1,0:T(8,128)(2,1)S(1)} %get-tuple-element.15.own_ref), channel_id=1, source_target_pairs={{0,5},{1,4},{2,7},{3,6},{4,1},{5,0},{6,3},{7,2},{8,13},{9,12},{10,... | collective-permute-start | bytes 24584 | tf_op jit(solution)/shard_map/ppermute | solution.py:422
  4.1 0.7 %collective-permute-start.2 = (bf16[16,128]{1,0:T(8,128)(2,1)S(1)}, bf16[16,128]{1,0:T(8,128)(2,1)S(1)}, u32[]{:S(2)}, u32[]{:S(2)}) collective-permute-start(bf16[16,128]{1,0:T(8,128)(2,1)S(1)} %get-tuple-element.16), channel_id=1, source_target_pairs={{0,1},{1,0},{2,3},{3,2},{4,5},{5,4},{6,7},{7,6},{8,9},{9,8},{10,11... | collective-permute-start | bytes 12296 | tf_op jit(solution)/shard_map/ppermute | solution.py:146
  4.8 0.0 copy-done
  4.8 1.1 %collective-permute-start = (bf16[2,128,512]{2,1,0:T(8,128)(2,1)S(1)}, bf16[2,128,512]{2,1,0:T(8,128)(2,1)S(1)}, u32[]{:S(2)}, u32[]{:S(2)}) collective-permute-start(bf16[2,128,512]{2,1,0:T(8,128)(2,1)S(1)} %copy-done), channel_id=1, source_target_pairs={{0,3},{1,2},{2,1},{3,0},{4,7},{5,6},{6,5},{7,4},{8,11},{9,10},{10,... | collective-permute-start | bytes 786440 | tf_op jit(solution)/shard_map/ppermute | solution.py:146
  5.9 0.0 collective-permute-done.2.pair_ref
  5.9 0.0 collective-permute-done.1.received_ref.first_ref
  5.9 1.8 %collective-permute-start.4 = (bf16[32,384]{1,0:T(8,128)(2,1)S(1)}, bf16[32,384]{1,0:T(8,128)(2,1)S(1)}, u32[]{:S(2)}, u32[]{:S(2)}) collective-permute-start(bf16[32,384]{1,0:T(8,128)(2,1)S(1)} %get-tuple-element.18), channel_id=1, source_target_pairs={{0,9},{1,8},{2,11},{3,10},{4,13},{5,12},{6,15},{7,14},{8,1},{9,0},... | collective-permute-start | bytes 73736 | tf_op jit(solution)/shard_map/ppermute | solution.py:422
  7.7 0.3 %collective-permute-start.3 = (bf16[16,128]{1,0:T(8,128)(2,1)S(1)}, bf16[16,128]{1,0:T(8,128)(2,1)S(1)}, u32[]{:S(2)}, u32[]{:S(2)}) collective-permute-start(bf16[16,128]{1,0:T(8,128)(2,1)S(1)} %get-tuple-element.17._), channel_id=1, source_target_pairs={{0,1},{1,0},{2,3},{3,2},{4,5},{5,4},{6,7},{7,6},{8,9},{9,8},{10,11... | collective-permute-start | bytes 12296 | tf_op jit(solution)/shard_map/ppermute | solution.py:146
  7.9 0.8 %shard_map.98 = (bf16[128,1024]{1,0:T(8,128)(2,1)S(1)}, bf16[5,128,128]{2,1,0:T(8,128)(2,1)S(1)}, s32[3,8]{1,0:T(4,128)S(4)}) custom-call(s32[1]{0:T(128)S(6)} %copy.10.live_ref, s32[3,8]{1,0:T(4,128)} %targets_ref.1, bf16[2,8,512]{2,1,0:T(8,128)(2,1)} %bitcast.3, bf16[16,128]{1,0:T(8,128)(2,1)S(1)} %get-tuple-element.17._), custom_call_target="tpu_custom_call" | custom-call | tf_op jit(solution)/shard_map/pallas_call | solution.py:437
  8.7 0.1 collective-permute-done.3.pair_ref
  8.8 0.4 %collective-permute-done.4.second_ref = bf16[32,384]{1,0:T(8,128)(2,1)S(1)} collective-permute-done((bf16[32,384]{1,0:T(8,128)(2,1)S(1)}, bf16[32,384]{1,0:T(8,128)(2,1)S(1)}, u32[]{:S(2)}, u32[]{:S(2)}) %collective-permute-start.4) | collective-permute-done | bytes 24608 | tf_op jit(solution)/shard_map/ppermute | solution.py:422
  9.2 2.9 %collective-permute-start.5 = (bf16[64,256]{1,0:T(8,128)(2,1)S(1)}, bf16[64,256]{1,0:T(8,128)(2,1)S(1)}, u32[]{:S(2)}, u32[]{:S(2)}) collective-permute-start(bf16[64,256]{1,0:T(8,128)(2,1)S(1)} %shard_map.99._.near_ref), channel_id=1, source_target_pairs={{0,16},{1,17},{2,18},{3,19},{4,20},{5,21},{6,22},{7,23},{8,24},{9,... | collective-permute-start | bytes 98312 | tf_op jit(solution)/shard_map/ppermute | solution.py:422
  12.1 0.2 %collective-permute-start.6 = (bf16[2,128,512]{2,1,0:T(8,128)(2,1)S(1)}, bf16[2,128,512]{2,1,0:T(8,128)(2,1)S(1)}, u32[]{:S(2)}, u32[]{:S(2)}) collective-permute-start(bf16[2,128,512]{2,1,0:T(8,128)(2,1)S(1)} %copy-done), channel_id=1, source_target_pairs={{0,1},{1,0},{2,3},{3,2},{4,5},{5,4},{6,7},{7,6},{8,9},{9,8},{10,11... | collective-permute-start | bytes 786440 | tf_op jit(solution)/shard_map/ppermute | solution.py:146
  12.3 0.9 %collective-permute-done.piece_ref = bf16[2,128,512]{2,1,0:T(8,128)(2,1)S(1)} collective-permute-done((bf16[2,128,512]{2,1,0:T(8,128)(2,1)S(1)}, bf16[2,128,512]{2,1,0:T(8,128)(2,1)S(1)}, u32[]{:S(2)}, u32[]{:S(2)}) %collective-permute-start) | collective-permute-done | bytes 262176 | tf_op jit(solution)/shard_map/ppermute | solution.py:146
  13.2 0.2 %collective-permute-start.7 = (bf16[2,128,512]{2,1,0:T(8,128)(2,1)S(1)}, bf16[2,128,512]{2,1,0:T(8,128)(2,1)S(1)}, u32[]{:S(2)}, u32[]{:S(2)}) collective-permute-start(bf16[2,128,512]{2,1,0:T(8,128)(2,1)S(1)} %shard_map.100.refs_1_), channel_id=1, source_target_pairs={{0,1},{1,0},{2,3},{3,2},{4,5},{5,4},{6,7},{7,6},{8,9},{9,8},{10,11... | collective-permute-start | bytes 786440 | tf_op jit(solution)/shard_map/ppermute | solution.py:146
  13.4 0.2 %shard_map.101._.partial_ref = f32[2,16,512]{2,1,0:T(8,128)S(1)} custom-call(bf16[32,512]{1,0:T(8,128)(2,1)S(1)} %get-tuple-element.14.z_ref, bf16[2,128,512]{2,1,0:T(8,128)(2,1)S(1)} %copy-done, bf16[2,128,512]{2,1,0:T(8,128)(2,1)S(1)} %shard_map.100.refs_1_), custom_call_target="tpu_custom_call" | custom-call | tf_op jit(solution)/shard_map/pallas_call | solution.py:468
  13.6 0.6 %collective-permute-done.5.far_ref = bf16[64,256]{1,0:T(8,128)(2,1)S(1)} collective-permute-done((bf16[64,256]{1,0:T(8,128)(2,1)S(1)}, bf16[64,256]{1,0:T(8,128)(2,1)S(1)}, u32[]{:S(2)}, u32[]{:S(2)}) %collective-permute-start.5) | collective-permute-done | bytes 32800 | tf_op jit(solution)/shard_map/ppermute | solution.py:422
  14.2 1.0 %shard_map.102 = (bf16[16,128]{1,0:T(8,128)(2,1)S(1)}, f32[2,3,8,16]{3,2,1,0:T(8,128)S(1)}) custom-call(s32[3,8]{1,0:T(4,128)S(4)} %get-tuple-element.20.targets_ref, bf16[64,256]{1,0:T(8,128)(2,1)S(1)} %shard_map.99._.near_ref, bf16[64,256]{1,0:T(8,128)(2,1)S(1)} %collective-permute-done.5.far_ref, bf16[5,128,128]{2,1,0:T(8,128)(2,1)S(1)} %get-tuple-element.19._.pick_ref, ...), custom_call_target="tpu_custom_call" | custom-call | flops 3000000000 | tf_op jit(solution)/shard_map/pallas_call | solution.py:475
  15.2 0.0 collective-permute-done.6.refs_0_
  15.2 0.0 collective-permute-done.7.refs_1_
  15.3 0.9 %shard_map.103 = (f32[2,16,512]{2,1,0:T(8,128)}, f32[2,3,8,16]{3,2,1,0:T(8,128)}) custom-call(s32[1]{0:T(128)S(6)} %copy.10.live_ref, bf16[32,512]{1,0:T(8,128)(2,1)S(1)} %get-tuple-element.14.z_ref, f32[2,16,512]{2,1,0:T(8,128)S(1)} %shard_map.101._.partial_ref, bf16[16,128]{1,0:T(8,128)(2,1)S(1)} %get-tuple-element.21.parent_ref, ...), custom_call_target="tpu_custom_call" | custom-call | tf_op jit(solution)/shard_map/pallas_call | solution.py:493
  (4 shorter events, 0.0 us)
Async XLA Ops:
  0.6 0.8 %copy-start.3 = (f32[2,16,3,8]{1,3,2,0:T(8,128)S(1)}, f32[2,16,3,8]{1,3,2,0:T(8,128)}, u32[]{:S(2)}) copy-start(f32[2,16,3,8]{1,3,2,0:T(8,128)} %param.9) | copy-start | bytes 9220
  0.6 0.8 %copy-start.1 = (f32[2,16,512]{2,1,0:T(8,128)S(1)}, f32[2,16,512]{2,1,0:T(8,128)}, u32[]{:S(2)}) copy-start(f32[2,16,512]{2,1,0:T(8,128)} %leaf_rhs_ref.1) | copy-start | bytes 196612
  0.7 4.1 %copy-start = (bf16[2,128,512]{2,1,0:T(8,128)(2,1)S(1)}, bf16[2,128,512]{2,1,0:T(8,128)(2,1)}, u32[]{:S(2)}) copy-start(bf16[2,128,512]{2,1,0:T(8,128)(2,1)} %refs_0_.1) | copy-start | bytes 786436
  0.7 0.8 %copy-start.2 = (bf16[2,512,8]{1,2,0:T(8,128)(2,1)S(1)}, bf16[2,512,8]{1,2,0:T(8,128)(2,1)}, u32[]{:S(2)}) copy-start(bf16[2,512,8]{1,2,0:T(8,128)(2,1)} %param.11) | copy-start | bytes 49156
  0.7 0.8 %copy-start.5 = (bf16[2,8,48]{2,1,0:T(8,128)(2,1)S(1)}, bf16[2,8,48]{2,1,0:T(8,128)(2,1)}, u32[]{:S(2)}) copy-start(bf16[2,8,48]{2,1,0:T(8,128)(2,1)} %sep_low_ref.1) | copy-start | bytes 4612
  0.7 0.8 %copy-start.4 = (bf16[2,8,112]{2,1,0:T(8,128)(2,1)S(1)}, bf16[2,8,112]{2,1,0:T(8,128)(2,1)}, u32[]{:S(2)}) copy-start(bf16[2,8,112]{2,1,0:T(8,128)(2,1)} %inv_ref.1) | copy-start | bytes 10756
  1.7 4.2 %collective-permute-start.1 = (bf16[16,256]{1,0:T(8,128)(2,1)S(1)}, bf16[16,256]{1,0:T(8,128)(2,1)S(1)}, u32[]{:S(2)}, u32[]{:S(2)}) collective-permute-start(bf16[16,256]{1,0:T(8,128)(2,1)S(1)} %get-tuple-element.15.own_ref), channel_id=1, source_target_pairs={{0,5},{1,4},{2,7},{3,6},{4,1},{5,0},{6,3},{7,2},{8,13},{9,12},{10,... | collective-permute-start | bytes 24584 | tf_op jit(solution)/shard_map/ppermute | solution.py:422
  4.1 1.8 %collective-permute-start.2 = (bf16[16,128]{1,0:T(8,128)(2,1)S(1)}, bf16[16,128]{1,0:T(8,128)(2,1)S(1)}, u32[]{:S(2)}, u32[]{:S(2)}) collective-permute-start(bf16[16,128]{1,0:T(8,128)(2,1)S(1)} %get-tuple-element.16), channel_id=1, source_target_pairs={{0,1},{1,0},{2,3},{3,2},{4,5},{5,4},{6,7},{7,6},{8,9},{9,8},{10,11... | collective-permute-start | bytes 12296 | tf_op jit(solution)/shard_map/ppermute | solution.py:146
  4.8 8.4 %collective-permute-start = (bf16[2,128,512]{2,1,0:T(8,128)(2,1)S(1)}, bf16[2,128,512]{2,1,0:T(8,128)(2,1)S(1)}, u32[]{:S(2)}, u32[]{:S(2)}) collective-permute-start(bf16[2,128,512]{2,1,0:T(8,128)(2,1)S(1)} %copy-done), channel_id=1, source_target_pairs={{0,3},{1,2},{2,1},{3,0},{4,7},{5,6},{6,5},{7,4},{8,11},{9,10},{10,... | collective-permute-start | bytes 786440 | tf_op jit(solution)/shard_map/ppermute | solution.py:146
  5.9 3.3 %collective-permute-start.4 = (bf16[32,384]{1,0:T(8,128)(2,1)S(1)}, bf16[32,384]{1,0:T(8,128)(2,1)S(1)}, u32[]{:S(2)}, u32[]{:S(2)}) collective-permute-start(bf16[32,384]{1,0:T(8,128)(2,1)S(1)} %get-tuple-element.18), channel_id=1, source_target_pairs={{0,9},{1,8},{2,11},{3,10},{4,13},{5,12},{6,15},{7,14},{8,1},{9,0},... | collective-permute-start | bytes 73736 | tf_op jit(solution)/shard_map/ppermute | solution.py:422
  7.7 1.2 %collective-permute-start.3 = (bf16[16,128]{1,0:T(8,128)(2,1)S(1)}, bf16[16,128]{1,0:T(8,128)(2,1)S(1)}, u32[]{:S(2)}, u32[]{:S(2)}) collective-permute-start(bf16[16,128]{1,0:T(8,128)(2,1)S(1)} %get-tuple-element.17._), channel_id=1, source_target_pairs={{0,1},{1,0},{2,3},{3,2},{4,5},{5,4},{6,7},{7,6},{8,9},{9,8},{10,11... | collective-permute-start | bytes 12296 | tf_op jit(solution)/shard_map/ppermute | solution.py:146
  9.2 5.0 %collective-permute-start.5 = (bf16[64,256]{1,0:T(8,128)(2,1)S(1)}, bf16[64,256]{1,0:T(8,128)(2,1)S(1)}, u32[]{:S(2)}, u32[]{:S(2)}) collective-permute-start(bf16[64,256]{1,0:T(8,128)(2,1)S(1)} %shard_map.99._.near_ref), channel_id=1, source_target_pairs={{0,16},{1,17},{2,18},{3,19},{4,20},{5,21},{6,22},{7,23},{8,24},{9,... | collective-permute-start | bytes 98312 | tf_op jit(solution)/shard_map/ppermute | solution.py:422
  12.1 3.2 %collective-permute-start.6 = (bf16[2,128,512]{2,1,0:T(8,128)(2,1)S(1)}, bf16[2,128,512]{2,1,0:T(8,128)(2,1)S(1)}, u32[]{:S(2)}, u32[]{:S(2)}) collective-permute-start(bf16[2,128,512]{2,1,0:T(8,128)(2,1)S(1)} %copy-done), channel_id=1, source_target_pairs={{0,1},{1,0},{2,3},{3,2},{4,5},{5,4},{6,7},{7,6},{8,9},{9,8},{10,11... | collective-permute-start | bytes 786440 | tf_op jit(solution)/shard_map/ppermute | solution.py:146
  13.2 2.0 %collective-permute-start.7 = (bf16[2,128,512]{2,1,0:T(8,128)(2,1)S(1)}, bf16[2,128,512]{2,1,0:T(8,128)(2,1)S(1)}, u32[]{:S(2)}, u32[]{:S(2)}) collective-permute-start(bf16[2,128,512]{2,1,0:T(8,128)(2,1)S(1)} %shard_map.100.refs_1_), channel_id=1, source_target_pairs={{0,1},{1,0},{2,3},{3,2},{4,5},{5,4},{6,7},{7,6},{8,9},{9,8},{10,11... | collective-permute-start | bytes 786440 | tf_op jit(solution)/shard_map/ppermute | solution.py:146

commit v5 on v4

--- a/solution.py
+++ b/solution.py
@@ -221,7 +221,7 @@
     rows = jnp.concatenate(
         [
             jnp.concatenate([low[0], low[1]], axis=1),
-            jnp.concatenate([-low[1], low[0]], axis=1),
+            jnp.concatenate([low[1], -low[0]], axis=1),
         ],
         axis=0,
     ).astype(jnp.bfloat16)
@@ -274,103 +274,182 @@
     out_ref[...] = piece_ref[...]
 
 
-def tree_kernel(
-    targets_ref, near_ref, far_ref, pick_ref, _, parent_ref, sep_out_ref, all_ref, turn_ref
+def owner(targets_ref, level, block):
+    if level == 0:
+        return jnp.int32(block)
+    group = 2**level
+    return block // group * group + targets_ref[level - 1, block]
+
+
+def rows_of(targets_ref, level, source_ref, slab):
+    device = lax.axis_index("leaf")
+    return jnp.concatenate(
+        [
+            source_ref[
+                pl.ds(pl.multiple_of((owner(targets_ref, level, block) ^ device) * slab, slab), slab), :
+            ]
+            for block in range(targets_ref.shape[1])
+        ],
+        axis=0,
+    )
+
+
+def side_of(raw, level, columns):
+    size = raw.shape[0]
+    row = lax.broadcasted_iota(jnp.int32, (columns, size), 0)
+    lane = lax.broadcasted_iota(jnp.int32, (columns, size), 1)
+    pick = jnp.where(lane == row + level * columns, 1.0, 0.0).astype(jnp.bfloat16)
+    return times_transposed(pick, raw[:, :size])
+
+
+def times_transposed(left, right):
+    return lax.dot_general(left, right, (((1,), (1,)), ((), ())), preferred_element_type=jnp.float32)
+
+
+def front_matrix(source, pick, level, slab):
+    size, width = pick.shape[0], slab // 2
+    row = lax.broadcasted_iota(jnp.int32, (size, size), 0)
+    lane = lax.broadcasted_iota(jnp.int32, (size, size), 1)
+    plain = jnp.dot(source, pick, preferred_element_type=jnp.float32)
+    swapped = plain.reshape(size // slab, 2, width, size)
+    swapped = jnp.concatenate([swapped[:, 1:], swapped[:, :1]], axis=1).reshape(size, size)
+    signed = jnp.where((row // width) % 2 == 0, plain, -plain)
+    full = jnp.where((lane // width) % 2 == 0, signed, swapped)
+    inside = row // (slab * 2**level) == lane // (slab * 2**level)
+    return jnp.where(inside, full, 0.0).astype(jnp.bfloat16)
+
+
+def conjugate(values_in, width):
+    lane = lax.broadcasted_iota(jnp.int32, (1, values_in.shape[1]), 1)
+    return jnp.where((lane // width) % 2 == 0, values_in, -values_in)
+
+
+def near_kernel(
+    targets_ref,
+    near_ref,
+    pick_ref,
+    panel_ref,
+    update_ref,
+    solved_ref,
+    lower_ref,
+    leaf_ref,
+    operator_ref,
+    all_ref,
 ):
     depth, devices = targets_ref.shape
+    columns, size = update_ref.shape
+    slab = size // devices
+    width = slab // 2
+    top = depth - 1
+    all_ref[: size // 2, :] = near_ref[...]
+    all_ref[size // 2 :, :] = jnp.zeros_like(near_ref)
+    arriving = side_of(rows_of(targets_ref, 0, all_ref, slab), 0, columns)
+    partial, lower = [None], [None]
+    for level in range(1, depth):
+        raw = rows_of(targets_ref, level, all_ref, slab)
+        level_z = (side_of(raw, level, columns) - arriving).astype(jnp.bfloat16)
+        inverse = front_matrix(raw[:, size:], pick_ref[level - 1], level, slab)
+        lower.append(front_matrix(raw[:, :size], pick_ref[depth + level - 1], level, slab))
+        partial.append(jnp.dot(level_z, inverse, preferred_element_type=jnp.float32))
+        arriving = jnp.dot(level_z, lower[level], preferred_element_type=jnp.float32)
+    update_ref[...] = arriving
+    known, operator = partial[top], lower[top]
+    solved = {top: known}
+    lower_ref[top - 1] = operator
+    for level in range(top - 1, 0, -1):
+        parent = conjugate(known, width).astype(jnp.bfloat16)
+        known = partial[level] - conjugate(times_transposed(parent, lower[level]), width)
+        operator = -jnp.dot(lower[level], operator, preferred_element_type=jnp.float32)
+        operator = operator.astype(jnp.bfloat16)
+        solved[level] = known
+        lower_ref[level - 1] = operator
+    stacked = [solved[level] for level in range(1, depth)]
+    stacked.append(jnp.zeros((size - top * columns, size), jnp.float32))
+    solved_ref[...] = jnp.concatenate(stacked, axis=0).T
+    parent = conjugate(known, width).astype(jnp.bfloat16)
+    leaf_ref[...] = jnp.dot(parent, panel_ref[...], preferred_element_type=jnp.float32)
+    operator_ref[...] = lax.dot_general(
+        operator, panel_ref[...], (((0,), (0,)), ((), ())), preferred_element_type=jnp.float32
+    ).astype(jnp.bfloat16)
+
+
+def top_kernel(targets_ref, near_ref, far_ref, pick_ref, update_ref, _, parent_ref, solved_ref, half_ref, all_ref):
+    depth, devices = targets_ref.shape
+    columns, size = update_ref.shape
+    slab = size // devices
+    half_ref[: size // 2, :] = jnp.zeros_like(near_ref)
+    half_ref[size // 2 :, :] = far_ref[...]
+    all_ref[: size // 2, :] = near_ref[...]
+    all_ref[size // 2 :, :] = far_ref[...]
+    raw = rows_of(targets_ref, depth, all_ref, slab)
+    inverse = front_matrix(raw[:, size:], pick_ref[depth - 1], depth, slab)
+    waiting = side_of(raw, depth, columns) - update_ref[...]
+    arriving = side_of(rows_of(targets_ref, 0, half_ref, slab), 0, columns)
+    for level in range(1, depth):
+        raw = rows_of(targets_ref, level, half_ref, slab)
+        level_z = (side_of(raw, level, columns) - arriving).astype(jnp.bfloat16)
+        lower = front_matrix(raw[:, :size], pick_ref[depth + level - 1], level, slab)
+        arriving = jnp.dot(level_z, lower, preferred_element_type=jnp.float32)
+    level_z = (waiting - arriving).astype(jnp.bfloat16)
+    solved = jnp.dot(level_z, inverse, preferred_element_type=jnp.float32)
+    solved_ref[...] = lax.dot_general(
+        inverse, level_z, (((0,), (1,)), ((), ())), preferred_element_type=jnp.float32
+    )
+    parent_ref[...] = conjugate(solved, slab // 2).astype(jnp.bfloat16)
+
+
+def finish_kernel(
+    steps,
+    live_ref,
+    targets_ref,
+    z_ref,
+    partial_ref,
+    parent_ref,
+    top_ref,
+    solved_ref,
+    lower_ref,
+    leaf_ref,
+    operator_ref,
+    *refs,
+):
+    piece_refs, (leaf_out_ref, sep_out_ref) = refs[: len(steps)], refs[len(steps) : len(steps) + 2]
+    leaf_place, sep_place, sems = refs[len(steps) + 2 :]
+    depth, devices = targets_ref.shape
     columns, size = parent_ref.shape
+    leaf_rows = leaf_place.shape[2]
     slab = size // devices
     width = slab // 2
     device = lax.axis_index("leaf")
-    row = lax.broadcasted_iota(jnp.int32, (size, size), 0)
-    lane = lax.broadcasted_iota(jnp.int32, (size, size), 1)
-    lane_row = lax.broadcasted_iota(jnp.int32, (1, size), 1)
-    row_part, lane_part = (row // width) % 2, (lane // width) % 2
-    all_ref[: size // 2, :] = near_ref[...]
-    all_ref[size // 2 :, :] = far_ref[...]
-
-    def owner(level, block):
-        if level == 0:
-            return jnp.int32(block)
-        group = 2**level
-        return block // group * group + targets_ref[level - 1, block]
-
-    def rows_of(level):
-        return jnp.concatenate(
-            [
-                all_ref[pl.ds(pl.multiple_of((owner(level, block) ^ device) * slab, slab), slab), :]
-                for block in range(devices)
-            ],
-            axis=0,
-        )
-
-    raw = [rows_of(level) for level in range(depth + 1)]
-    pick_row = lax.broadcasted_iota(jnp.int32, (columns, size), 0)
-    pick_lane = lax.broadcasted_iota(jnp.int32, (columns, size), 1)
-    back = (((1,), (1,)), ((), ()))
-
-    def side(level):
-        pick = jnp.where(pick_lane == pick_row + level * columns, 1.0, 0.0).astype(jnp.bfloat16)
-        return lax.dot_general(pick, raw[level][:, :size], back, preferred_element_type=jnp.float32)
-
-    def front_matrix(source, pick, level):
-        plain = jnp.dot(source, pick, preferred_element_type=jnp.float32)
-        swapped = plain.reshape(devices, 2, width, size)
-        swapped = jnp.concatenate([swapped[:, 1:], swapped[:, :1]], axis=1).reshape(size, size)
-        signed = jnp.where(row_part == 0, plain, -plain)
-        full = jnp.where(lane_part == 0, signed, swapped)
-        inside = row // (slab * 2**level) == lane // (slab * 2**level)
-        return jnp.where(inside, full, 0.0).astype(jnp.bfloat16)
-
-    inverse, lower = [None], [None]
-    for level in range(1, depth + 1):
-        inverse.append(front_matrix(raw[level][:, size:], pick_ref[level - 1], level))
-        if level < depth:
-            lower.append(front_matrix(raw[level][:, :size], pick_ref[depth + level - 1], level))
-
-    arriving = side(0)
-    partial = [None]
-    for level in range(1, depth + 1):
-        level_z = (side(level) - arriving).astype(jnp.bfloat16)
-        partial.append(jnp.dot(level_z, inverse[level], preferred_element_type=jnp.float32))
-        if level < depth:
-            arriving = jnp.dot(level_z, lower[level], preferred_element_type=jnp.float32)
-
-    sign = jnp.where((lane_row // width) % 2 == 0, 1.0, -1.0)
-    solved = list(partial)
-    for level in range(depth - 1, 0, -1):
-        parent = (solved[level + 1] * sign).astype(jnp.bfloat16)
-        product = lax.dot_general(parent, lower[level], back, preferred_element_type=jnp.float32)
-        solved[level] = partial[level] - product * sign
-
-    parent_ref[...] = solved[1].astype(jnp.bfloat16)
-    stacked = jnp.concatenate(
-        solved[1:] + [jnp.zeros((size - depth * columns, size), jnp.float32)], axis=0
-    )
-    turn_ref[...] = stacked.T
+    live = lax.broadcasted_iota(jnp.int32, (1, leaf_rows), 1) < live_ref[0] * 128
+    parent = parent_ref[...]
     for level in range(1, depth + 1):
         place = jnp.int32(0)
         for block in range(devices):
-            place = jnp.where(owner(level, block) == device, block, place)
-        block_rows = turn_ref[pl.ds(pl.multiple_of(place * slab, slab), slab), :]
+            place = jnp.where(owner(targets_ref, level, block) == device, block, place)
+        rows = pl.ds(pl.multiple_of(place * slab, slab), slab)
+        if level < depth:
+            known = solved_ref[rows, :][:, (level - 1) * columns : level * columns]
+            change = times_transposed(lower_ref[level - 1, rows, :], parent)
+            halves = known[:width] - change[:width], known[width:] + change[width:]
+        else:
+            solved = top_ref[rows, :]
+            halves = solved[:width], solved[width:]
         for part in range(2):
-            sep_out_ref[part, level - 1] = block_rows[
-                part * width : (part + 1) * width, (level - 1) * columns : level * columns
-            ]
-
-
-def finish_kernel(steps, live_ref, z_ref, partial_ref, parent_ref, panel_ref, sep_ref, *refs):
-    leaf_out_ref, sep_out_ref = refs[-2:]
-    leaf_rows = leaf_out_ref.shape[2]
-    live = lax.broadcasted_iota(jnp.int32, (1, leaf_rows), 1) < live_ref[0] * 128
-    products = [piece_product(step, z_ref, piece_ref) for step, piece_ref in zip(steps, refs[:-2])]
-    from_tree = jnp.dot(parent_ref[...], panel_ref[...], preferred_element_type=jnp.float32)
+            sep_place[part, level - 1] = halves[part]
+    from_tree = leaf_ref[...] - jnp.dot(parent, operator_ref[...], preferred_element_type=jnp.float32)
+    products = [piece_product(step, z_ref, piece_ref) for step, piece_ref in zip(steps, piece_refs)]
+    copies = []
     for part in range(2):
         leaf_w = partial_ref[part] + sum(product[part] for product in products)
-        leaf_out_ref[part] = (
+        leaf_place[part] = (
             jnp.where(live, leaf_w, 0.0) - from_tree[:, part * leaf_rows : (part + 1) * leaf_rows]
         )
-    sep_out_ref[...] = sep_ref[...]
+        copies.append(pltpu.make_async_copy(leaf_place.at[part], leaf_out_ref.at[part], sems.at[part]))
+        copies[-1].start()
+    copies.append(pltpu.make_async_copy(sep_place, sep_out_ref, sems.at[2]))
+    copies[-1].start()
+    for copy in copies:
+        copy.wait()
 
 
 def whole(space):
@@ -472,23 +551,32 @@
         out_specs=whole(VMEM),
         cost_estimate=pl.CostEstimate(flops=0, bytes_accessed=0, transcendentals=0),
     )(*[in_vmem(ready) for ready in (leaf_z, leaf_inv, far_piece)])
-    parent_x, tree_sep = pl.pallas_call(
-        tree_kernel,
+    kept_targets = pltpu.with_memory_space_constraint(kept_targets, SMEM)
+    update, known, lower, known_leaf, operator = pl.pallas_call(
+        near_kernel,
+        out_shape=(
+            pltpu.VMEM((columns, size), jnp.float32),
+            pltpu.VMEM((size, size), jnp.float32),
+            pltpu.VMEM((depth - 1, size, size), jnp.bfloat16),
+            pltpu.VMEM((columns, 2 * leaf_rows), jnp.float32),
+            pltpu.VMEM((size, 2 * leaf_rows), jnp.bfloat16),
+        ),
+        in_specs=[whole(SMEM)] + [whole(VMEM)] * 3,
+        out_specs=(whole(VMEM),) * 5,
+        scratch_shapes=[pltpu.VMEM((size, 2 * size), jnp.bfloat16)],
+        cost_estimate=pl.CostEstimate(flops=0, bytes_accessed=0, transcendentals=0),
+    )(kept_targets, *[in_vmem(ready) for ready in (held, picks, panel_rows)])
+    parent_x, top_x = pl.pallas_call(
+        top_kernel,
         out_shape=(
             pltpu.VMEM((columns, size), jnp.bfloat16),
-            pltpu.VMEM((2, depth, width, columns), jnp.float32),
+            pltpu.VMEM((size, columns), jnp.float32),
         ),
-        in_specs=[whole(SMEM)] + [whole(VMEM)] * 4,
+        in_specs=[whole(SMEM)] + [whole(VMEM)] * 5,
         out_specs=(whole(VMEM),) * 2,
-        scratch_shapes=[
-            pltpu.VMEM((size, 2 * size), jnp.bfloat16),
-            pltpu.VMEM((size, size), jnp.float32),
-        ],
-        cost_estimate=pl.CostEstimate(flops=3*10**9, bytes_accessed=0, transcendentals=0),
-    )(
-        pltpu.with_memory_space_constraint(kept_targets, SMEM),
-        *[in_vmem(ready) for ready in (held, far, picks, partial)],
-    )
+        scratch_shapes=[pltpu.VMEM((size, 2 * size), jnp.bfloat16)] * 2,
+        cost_estimate=pl.CostEstimate(flops=3 * 10**9, bytes_accessed=0, transcendentals=0),
+    )(kept_targets, *[in_vmem(ready) for ready in (held, far, picks, update, partial)])
     pair_pieces = (xor_permute(leaf_inv, "rhs", 1), xor_permute(far_piece, "rhs", 1))
     leaf_x, sep_x = pl.pallas_call(
         functools.partial(finish_kernel, (1, 2)),
@@ -496,11 +584,20 @@
             jax.ShapeDtypeStruct((2, columns, leaf_rows), jnp.float32),
             jax.ShapeDtypeStruct((2, depth, width, columns), jnp.float32),
         ),
-        in_specs=[whole(SMEM)] + [whole(VMEM)] * 7,
-        out_specs=(whole(VMEM),) * 2,
+        in_specs=[whole(SMEM)] * 2 + [whole(VMEM)] * 10,
+        out_specs=(whole(pl.ANY),) * 2,
+        scratch_shapes=[
+            pltpu.VMEM((2, columns, leaf_rows), jnp.float32),
+            pltpu.VMEM((2, depth, width, columns), jnp.float32),
+            pltpu.SemaphoreType.DMA((3,)),
+        ],
     )(
         leaf_live,
-        *[in_vmem(ready) for ready in (leaf_z, partial, parent_x, panel_rows, tree_sep) + pair_pieces],
+        kept_targets,
+        *[
+            in_vmem(ready)
+            for ready in (leaf_z, partial, parent_x, top_x, known, lower, known_leaf, operator) + pair_pieces
+        ],
     )
     return leaf_x, sep_x.transpose(0, 3, 1, 2)
 

time: 16.3 us -> 15.9 us (0.975)
  waiting for transfers between devices: 2.02 us -> 1.06 us
  Pallas kernels: 3.06 us -> 3.51 us
    ppermute x5, waiting for transfers between devices: 0.99 us -> 0.15 us  [xor_permute(): lax.ppermute(values_in, axis, [(source, source ^ offset) for source in ra...]
    pallas_call x1 -> x2, Pallas kernels: 1.02 us -> 1.41 us  [the longest x1 0.82 us: body(): pl.pallas_call(near_kernel, out_shape=(pltpu.VMEM((columns, size), jnp.fl...]
  transfers between devices with their start and end apart: 8 -> 8, of which waited for: 4 -> 3; matrix products, arithmetic and copies ran while one was open for 0% -> 0% of each run, Pallas kernels for 12% -> 15%
where the time goes in v5:
time: 15.9 us; the launch traced here: 15.8 us
  starting transfers between devices  9.63 us (61%)
  Pallas kernels  3.51 us (22%)
  between operations  1.45 us (9%)
  waiting for transfers between devices  1.06 us (7%)
    ppermute x3, starting transfers between devices, exchange(): return lax.ppermute(values_in, ('leaf', 'rhs'), partners)  7.03 us
    ppermute x5, starting transfers between devices, xor_permute(): lax.ppermute(values_in, axis, [(source, source ^ offset) for source in ra...  2.6 us
    pallas_call x1, Pallas kernels, body(): pl.pallas_call(functools.partial(finish_kernel, (1, 2)), out_shape=(jax.S...  0.92 us
    ppermute x3, waiting for transfers between devices, exchange(): return lax.ppermute(values_in, ('leaf', 'rhs'), partners)  0.9 us
    pallas_call x1, Pallas kernels, body(): pl.pallas_call(near_kernel, out_shape=(pltpu.VMEM((columns, size), jnp.fl...  0.82 us
    pallas_call x1, Pallas kernels, body(): pl.pallas_call(functools.partial(prepare_kernel, (1 + depth) * columns),...  0.78 us
    pallas_call x1, Pallas kernels, body(): pl.pallas_call(top_kernel, out_shape=(pltpu.VMEM((columns, size), jnp.bfl...  0.59 us
  transfers between devices with their start and end apart: 8, of which 3 were waited for; matrix products, arithmetic and copies ran while one was open for 0% of the time, Pallas kernels for 15%

profile of v5, /device:TPU:0, one launch (start us, length us, event | category | flops | bytes accessed | tf_op | source)
XLA Modules:
  0.0 15.8 jit_solution(1066171663650477066)
XLA Ops:
  0.6 0.0 copy-start.3
  0.6 0.0 copy-start.1
  0.7 0.0 copy-start
  0.7 0.0 copy-start.2
  0.7 0.0 copy-start.5
  0.7 0.0 copy-start.4
  1.4 0.0 copy-done.3
  1.4 0.1 copy-done.1
  1.5 0.0 copy-done.2
  1.5 0.0 copy-done.5
  1.5 0.0 copy-done.4
  1.5 0.2 %shard_map.96 = (bf16[16,256]{1,0:T(8,128)(2,1)S(1)}, bf16[16,128]{1,0:T(8,128)(2,1)S(1)}, bf16[32,512]{1,0:T(8,128)(2,1)S(1)}) custom-call(s32[1]{0:T(128)S(6)} %copy.10.live_ref, f32[8,128]{1,0:T(8,128)S(1)} %shard_map.95._, f32[2,16,512]{2,1,0:T(8,128)S(1)} %copy-done.1, bf16[2,8,512]{2,1,0:T(8,128)(2,1)S(1)} %bitcast.4, f32[2,3,8,16]{3,2,1,0:T(8,128)S(1)} %bitcast.5, ...), custom_call_target="tpu_custom_call" | custom-call | tf_op jit(solution)/shard_map/pallas_call | solution.py:484
  1.7 2.4 %collective-permute-start = (bf16[16,256]{1,0:T(8,128)(2,1)S(1)}, bf16[16,256]{1,0:T(8,128)(2,1)S(1)}, u32[]{:S(2)}, u32[]{:S(2)}) collective-permute-start(bf16[16,256]{1,0:T(8,128)(2,1)S(1)} %get-tuple-element.19.own_ref), channel_id=1, source_target_pairs={{0,5},{1,4},{2,7},{3,6},{4,1},{5,0},{6,3},{7,2},{8,13},{9,12},{10,... | collective-permute-start | bytes 24584 | tf_op jit(solution)/shard_map/ppermute | solution.py:501
  4.1 0.7 %collective-permute-start.1 = (bf16[16,128]{1,0:T(8,128)(2,1)S(1)}, bf16[16,128]{1,0:T(8,128)(2,1)S(1)}, u32[]{:S(2)}, u32[]{:S(2)}) collective-permute-start(bf16[16,128]{1,0:T(8,128)(2,1)S(1)} %get-tuple-element.20), channel_id=1, source_target_pairs={{0,1},{1,0},{2,3},{3,2},{4,5},{5,4},{6,7},{7,6},{8,9},{9,8},{10,11... | collective-permute-start | bytes 12296 | tf_op jit(solution)/shard_map/ppermute | solution.py:146
  4.8 0.0 copy-done
  4.8 1.1 %collective-permute-start.2 = (bf16[2,128,512]{2,1,0:T(8,128)(2,1)S(1)}, bf16[2,128,512]{2,1,0:T(8,128)(2,1)S(1)}, u32[]{:S(2)}, u32[]{:S(2)}) collective-permute-start(bf16[2,128,512]{2,1,0:T(8,128)(2,1)S(1)} %copy-done), channel_id=1, source_target_pairs={{0,3},{1,2},{2,1},{3,0},{4,7},{5,6},{6,5},{7,4},{8,11},{9,10},{10,... | collective-permute-start | bytes 786440 | tf_op jit(solution)/shard_map/ppermute | solution.py:146
  5.9 0.0 collective-permute-done.1.pair_ref
  5.9 0.0 collective-permute-done.received_ref.first_ref
  5.9 1.8 %collective-permute-start.4 = (bf16[32,384]{1,0:T(8,128)(2,1)S(1)}, bf16[32,384]{1,0:T(8,128)(2,1)S(1)}, u32[]{:S(2)}, u32[]{:S(2)}) collective-permute-start(bf16[32,384]{1,0:T(8,128)(2,1)S(1)} %get-tuple-element.24), channel_id=1, source_target_pairs={{0,9},{1,8},{2,11},{3,10},{4,13},{5,12},{6,15},{7,14},{8,1},{9,0},... | collective-permute-start | bytes 73736 | tf_op jit(solution)/shard_map/ppermute | solution.py:501
  7.7 0.3 %collective-permute-start.3 = (bf16[16,128]{1,0:T(8,128)(2,1)S(1)}, bf16[16,128]{1,0:T(8,128)(2,1)S(1)}, u32[]{:S(2)}, u32[]{:S(2)}) collective-permute-start(bf16[16,128]{1,0:T(8,128)(2,1)S(1)} %get-tuple-element.21._), channel_id=1, source_target_pairs={{0,1},{1,0},{2,3},{3,2},{4,5},{5,4},{6,7},{7,6},{8,9},{9,8},{10,11... | collective-permute-start | bytes 12296 | tf_op jit(solution)/shard_map/ppermute | solution.py:146
  7.9 0.8 %shard_map.98 = (bf16[128,1024]{1,0:T(8,128)(2,1)S(1)}, bf16[5,128,128]{2,1,0:T(8,128)(2,1)S(1)}, s32[3,8]{1,0:T(4,128)S(4)}) custom-call(s32[1]{0:T(128)S(6)} %copy.10.live_ref, s32[3,8]{1,0:T(4,128)} %targets_ref.1, bf16[2,8,512]{2,1,0:T(8,128)(2,1)} %bitcast.3, bf16[16,128]{1,0:T(8,128)(2,1)S(1)} %get-tuple-element.21._), custom_call_target="tpu_custom_call" | custom-call | tf_op jit(solution)/shard_map/pallas_call | solution.py:516
  8.7 0.1 collective-permute-done.3.pair_ref
  8.8 0.4 %collective-permute-done.4.second_ref = bf16[32,384]{1,0:T(8,128)(2,1)S(1)} collective-permute-done((bf16[32,384]{1,0:T(8,128)(2,1)S(1)}, bf16[32,384]{1,0:T(8,128)(2,1)S(1)}, u32[]{:S(2)}, u32[]{:S(2)}) %collective-permute-start.4) | collective-permute-done | bytes 24608 | tf_op jit(solution)/shard_map/ppermute | solution.py:501
  9.2 2.9 %collective-permute-start.5 = (bf16[64,256]{1,0:T(8,128)(2,1)S(1)}, bf16[64,256]{1,0:T(8,128)(2,1)S(1)}, u32[]{:S(2)}, u32[]{:S(2)}) collective-permute-start(bf16[64,256]{1,0:T(8,128)(2,1)S(1)} %shard_map.99._.near_ref), channel_id=1, source_target_pairs={{0,16},{1,17},{2,18},{3,19},{4,20},{5,21},{6,22},{7,23},{8,24},{9,... | collective-permute-start | bytes 98312 | tf_op jit(solution)/shard_map/ppermute | solution.py:501
  12.1 0.2 %collective-permute-start.6 = (bf16[2,128,512]{2,1,0:T(8,128)(2,1)S(1)}, bf16[2,128,512]{2,1,0:T(8,128)(2,1)S(1)}, u32[]{:S(2)}, u32[]{:S(2)}) collective-permute-start(bf16[2,128,512]{2,1,0:T(8,128)(2,1)S(1)} %copy-done), channel_id=1, source_target_pairs={{0,1},{1,0},{2,3},{3,2},{4,5},{5,4},{6,7},{7,6},{8,9},{9,8},{10,11... | collective-permute-start | bytes 786440 | tf_op jit(solution)/shard_map/ppermute | solution.py:146
  12.3 0.8 %shard_map.102 = (f32[16,128]{1,0:T(8,128)S(1)}, f32[128,128]{1,0:T(8,128)S(1)}, bf16[2,128,128]{2,1,0:T(8,128)(2,1)S(1)}, f32[16,1024]{1,0:T(8,128)S(1)}, bf16[128,1024]{1,0:T(8,128)(2,1)S(1)}) custom-call(s32[3,8]{1,0:T(4,128)S(4)} %get-tuple-element.22.targets_ref, bf16[64,256]{1,0:T(8,128)(2,1)S(1)} %shard_map.99._.near_ref, ...), custom_call_target="tpu_custom_call" | custom-call | tf_op jit(solution)/shard_map/pallas_call | solution.py:555
  13.2 0.0 collective-permute-done.2.piece_ref
  13.2 0.3 %collective-permute-start.7 = (bf16[2,128,512]{2,1,0:T(8,128)(2,1)S(1)}, bf16[2,128,512]{2,1,0:T(8,128)(2,1)S(1)}, u32[]{:S(2)}, u32[]{:S(2)}) collective-permute-start(bf16[2,128,512]{2,1,0:T(8,128)(2,1)S(1)} %shard_map.100.refs_1_), channel_id=1, source_target_pairs={{0,1},{1,0},{2,3},{3,2},{4,5},{5,4},{6,7},{7,6},{8,9},{9,8},{10,11... | collective-permute-start | bytes 786440 | tf_op jit(solution)/shard_map/ppermute | solution.py:146
  13.5 0.2 %shard_map.101._.partial_ref = f32[2,16,512]{2,1,0:T(8,128)S(1)} custom-call(bf16[32,512]{1,0:T(8,128)(2,1)S(1)} %get-tuple-element.23.z_ref, bf16[2,128,512]{2,1,0:T(8,128)(2,1)S(1)} %copy-done, bf16[2,128,512]{2,1,0:T(8,128)(2,1)S(1)} %shard_map.100.refs_1_), custom_call_target="tpu_custom_call" | custom-call | tf_op jit(solution)/shard_map/pallas_call | solution.py:547
  13.7 0.5 %collective-permute-done.5.far_ref = bf16[64,256]{1,0:T(8,128)(2,1)S(1)} collective-permute-done((bf16[64,256]{1,0:T(8,128)(2,1)S(1)}, bf16[64,256]{1,0:T(8,128)(2,1)S(1)}, u32[]{:S(2)}, u32[]{:S(2)}) %collective-permute-start.5) | collective-permute-done | bytes 32800 | tf_op jit(solution)/shard_map/ppermute | solution.py:501
  14.2 0.6 %shard_map.103 = (bf16[16,128]{1,0:T(8,128)(2,1)S(1)}, f32[128,16]{1,0:T(8,128)S(1)}) custom-call(s32[3,8]{1,0:T(4,128)S(4)} %get-tuple-element.22.targets_ref, bf16[64,256]{1,0:T(8,128)(2,1)S(1)} %shard_map.99._.near_ref, bf16[64,256]{1,0:T(8,128)(2,1)S(1)} %collective-permute-done.5.far_ref, bf16[5,128,128]{2,1,0:T(8,128)(2,1)S(1)} %get-tuple-element.25._.pick_ref, ...), custom_call_target="tpu_custom_call" | custom-call | flops 3000000000 | tf_op jit(solution)/shard_map/pallas_call | solution.py:569
  14.8 0.0 collective-permute-done.6.refs_0_
  14.8 0.0 collective-permute-done.7.refs_1_
  14.8 0.9 %shard_map.104 = (f32[2,16,512]{2,1,0:T(8,128)}, f32[2,3,8,16]{3,2,1,0:T(8,128)}) custom-call(s32[1]{0:T(128)S(6)} %copy.10.live_ref, s32[3,8]{1,0:T(4,128)S(4)} %get-tuple-element.22.targets_ref, bf16[32,512]{1,0:T(8,128)(2,1)S(1)} %get-tuple-element.23.z_ref, f32[2,16,512]{2,1,0:T(8,128)S(1)} %shard_map.101._.partial_ref, ...), custom_call_target="tpu_custom_call" | custom-call | tf_op jit(solution)/shard_map/pallas_call | solution.py:581
  (4 shorter events, 0.0 us)
Async XLA Ops:
  0.6 0.8 %copy-start.3 = (f32[2,16,3,8]{1,3,2,0:T(8,128)S(1)}, f32[2,16,3,8]{1,3,2,0:T(8,128)}, u32[]{:S(2)}) copy-start(f32[2,16,3,8]{1,3,2,0:T(8,128)} %param.9) | copy-start | bytes 9220
  0.6 0.8 %copy-start.1 = (f32[2,16,512]{2,1,0:T(8,128)S(1)}, f32[2,16,512]{2,1,0:T(8,128)}, u32[]{:S(2)}) copy-start(f32[2,16,512]{2,1,0:T(8,128)} %leaf_rhs_ref.1) | copy-start | bytes 196612
  0.7 4.1 %copy-start = (bf16[2,128,512]{2,1,0:T(8,128)(2,1)S(1)}, bf16[2,128,512]{2,1,0:T(8,128)(2,1)}, u32[]{:S(2)}) copy-start(bf16[2,128,512]{2,1,0:T(8,128)(2,1)} %refs_0_.1) | copy-start | bytes 786436
  0.7 0.8 %copy-start.2 = (bf16[2,512,8]{1,2,0:T(8,128)(2,1)S(1)}, bf16[2,512,8]{1,2,0:T(8,128)(2,1)}, u32[]{:S(2)}) copy-start(bf16[2,512,8]{1,2,0:T(8,128)(2,1)} %param.11) | copy-start | bytes 49156
  0.7 0.8 %copy-start.5 = (bf16[2,8,48]{2,1,0:T(8,128)(2,1)S(1)}, bf16[2,8,48]{2,1,0:T(8,128)(2,1)}, u32[]{:S(2)}) copy-start(bf16[2,8,48]{2,1,0:T(8,128)(2,1)} %sep_low_ref.1) | copy-start | bytes 4612
  0.7 0.8 %copy-start.4 = (bf16[2,8,112]{2,1,0:T(8,128)(2,1)S(1)}, bf16[2,8,112]{2,1,0:T(8,128)(2,1)}, u32[]{:S(2)}) copy-start(bf16[2,8,112]{2,1,0:T(8,128)(2,1)} %inv_ref.1) | copy-start | bytes 10756
  1.7 4.2 %collective-permute-start = (bf16[16,256]{1,0:T(8,128)(2,1)S(1)}, bf16[16,256]{1,0:T(8,128)(2,1)S(1)}, u32[]{:S(2)}, u32[]{:S(2)}) collective-permute-start(bf16[16,256]{1,0:T(8,128)(2,1)S(1)} %get-tuple-element.19.own_ref), channel_id=1, source_target_pairs={{0,5},{1,4},{2,7},{3,6},{4,1},{5,0},{6,3},{7,2},{8,13},{9,12},{10,... | collective-permute-start | bytes 24584 | tf_op jit(solution)/shard_map/ppermute | solution.py:501
  4.1 1.8 %collective-permute-start.1 = (bf16[16,128]{1,0:T(8,128)(2,1)S(1)}, bf16[16,128]{1,0:T(8,128)(2,1)S(1)}, u32[]{:S(2)}, u32[]{:S(2)}) collective-permute-start(bf16[16,128]{1,0:T(8,128)(2,1)S(1)} %get-tuple-element.20), channel_id=1, source_target_pairs={{0,1},{1,0},{2,3},{3,2},{4,5},{5,4},{6,7},{7,6},{8,9},{9,8},{10,11... | collective-permute-start | bytes 12296 | tf_op jit(solution)/shard_map/ppermute | solution.py:146
  4.8 8.4 %collective-permute-start.2 = (bf16[2,128,512]{2,1,0:T(8,128)(2,1)S(1)}, bf16[2,128,512]{2,1,0:T(8,128)(2,1)S(1)}, u32[]{:S(2)}, u32[]{:S(2)}) collective-permute-start(bf16[2,128,512]{2,1,0:T(8,128)(2,1)S(1)} %copy-done), channel_id=1, source_target_pairs={{0,3},{1,2},{2,1},{3,0},{4,7},{5,6},{6,5},{7,4},{8,11},{9,10},{10,... | collective-permute-start | bytes 786440 | tf_op jit(solution)/shard_map/ppermute | solution.py:146
  5.9 3.3 %collective-permute-start.4 = (bf16[32,384]{1,0:T(8,128)(2,1)S(1)}, bf16[32,384]{1,0:T(8,128)(2,1)S(1)}, u32[]{:S(2)}, u32[]{:S(2)}) collective-permute-start(bf16[32,384]{1,0:T(8,128)(2,1)S(1)} %get-tuple-element.24), channel_id=1, source_target_pairs={{0,9},{1,8},{2,11},{3,10},{4,13},{5,12},{6,15},{7,14},{8,1},{9,0},... | collective-permute-start | bytes 73736 | tf_op jit(solution)/shard_map/ppermute | solution.py:501
  7.7 1.2 %collective-permute-start.3 = (bf16[16,128]{1,0:T(8,128)(2,1)S(1)}, bf16[16,128]{1,0:T(8,128)(2,1)S(1)}, u32[]{:S(2)}, u32[]{:S(2)}) collective-permute-start(bf16[16,128]{1,0:T(8,128)(2,1)S(1)} %get-tuple-element.21._), channel_id=1, source_target_pairs={{0,1},{1,0},{2,3},{3,2},{4,5},{5,4},{6,7},{7,6},{8,9},{9,8},{10,11... | collective-permute-start | bytes 12296 | tf_op jit(solution)/shard_map/ppermute | solution.py:146
  9.2 5.0 %collective-permute-start.5 = (bf16[64,256]{1,0:T(8,128)(2,1)S(1)}, bf16[64,256]{1,0:T(8,128)(2,1)S(1)}, u32[]{:S(2)}, u32[]{:S(2)}) collective-permute-start(bf16[64,256]{1,0:T(8,128)(2,1)S(1)} %shard_map.99._.near_ref), channel_id=1, source_target_pairs={{0,16},{1,17},{2,18},{3,19},{4,20},{5,21},{6,22},{7,23},{8,24},{9,... | collective-permute-start | bytes 98312 | tf_op jit(solution)/shard_map/ppermute | solution.py:501
  12.1 2.7 %collective-permute-start.6 = (bf16[2,128,512]{2,1,0:T(8,128)(2,1)S(1)}, bf16[2,128,512]{2,1,0:T(8,128)(2,1)S(1)}, u32[]{:S(2)}, u32[]{:S(2)}) collective-permute-start(bf16[2,128,512]{2,1,0:T(8,128)(2,1)S(1)} %copy-done), channel_id=1, source_target_pairs={{0,1},{1,0},{2,3},{3,2},{4,5},{5,4},{6,7},{7,6},{8,9},{9,8},{10,11... | collective-permute-start | bytes 786440 | tf_op jit(solution)/shard_map/ppermute | solution.py:146
  13.2 1.6 %collective-permute-start.7 = (bf16[2,128,512]{2,1,0:T(8,128)(2,1)S(1)}, bf16[2,128,512]{2,1,0:T(8,128)(2,1)S(1)}, u32[]{:S(2)}, u32[]{:S(2)}) collective-permute-start(bf16[2,128,512]{2,1,0:T(8,128)(2,1)S(1)} %shard_map.100.refs_1_), channel_id=1, source_target_pairs={{0,1},{1,0},{2,3},{3,2},{4,5},{5,4},{6,7},{7,6},{8,9},{9,8},{10,11... | collective-permute-start | bytes 786440 | tf_op jit(solution)/shard_map/ppermute | solution.py:146

commit v6 on v5

--- a/solution.py
+++ b/solution.py
@@ -324,46 +324,38 @@
     return jnp.where((lane // width) % 2 == 0, values_in, -values_in)
 
 
-def near_kernel(
-    targets_ref,
-    near_ref,
-    pick_ref,
-    panel_ref,
-    update_ref,
-    solved_ref,
-    lower_ref,
-    leaf_ref,
-    operator_ref,
-    all_ref,
-):
+def near_kernel(targets_ref, near_ref, pick_ref, update_ref, partial_ref, lower_ref, all_ref):
     depth, devices = targets_ref.shape
     columns, size = update_ref.shape
     slab = size // devices
-    width = slab // 2
-    top = depth - 1
     all_ref[: size // 2, :] = near_ref[...]
     all_ref[size // 2 :, :] = jnp.zeros_like(near_ref)
     arriving = side_of(rows_of(targets_ref, 0, all_ref, slab), 0, columns)
-    partial, lower = [None], [None]
     for level in range(1, depth):
         raw = rows_of(targets_ref, level, all_ref, slab)
         level_z = (side_of(raw, level, columns) - arriving).astype(jnp.bfloat16)
         inverse = front_matrix(raw[:, size:], pick_ref[level - 1], level, slab)
-        lower.append(front_matrix(raw[:, :size], pick_ref[depth + level - 1], level, slab))
-        partial.append(jnp.dot(level_z, inverse, preferred_element_type=jnp.float32))
-        arriving = jnp.dot(level_z, lower[level], preferred_element_type=jnp.float32)
+        lower = front_matrix(raw[:, :size], pick_ref[depth + level - 1], level, slab)
+        lower_ref[level - 1] = lower
+        partial_ref[level - 1] = jnp.dot(level_z, inverse, preferred_element_type=jnp.float32)
+        arriving = jnp.dot(level_z, lower, preferred_element_type=jnp.float32)
     update_ref[...] = arriving
-    known, operator = partial[top], lower[top]
+
+
+def operator_kernel(partial_ref, lower_ref, panel_ref, _, solved_ref, back_ref, leaf_ref, operator_ref):
+    top, columns, size = partial_ref.shape
+    width = size // 16
+    known, operator = partial_ref[top - 1], lower_ref[top - 1]
     solved = {top: known}
-    lower_ref[top - 1] = operator
+    back_ref[top - 1] = operator
     for level in range(top - 1, 0, -1):
         parent = conjugate(known, width).astype(jnp.bfloat16)
-        known = partial[level] - conjugate(times_transposed(parent, lower[level]), width)
-        operator = -jnp.dot(lower[level], operator, preferred_element_type=jnp.float32)
+        known = partial_ref[level - 1] - conjugate(times_transposed(parent, lower_ref[level - 1]), width)
+        operator = -jnp.dot(lower_ref[level - 1], operator, preferred_element_type=jnp.float32)
         operator = operator.astype(jnp.bfloat16)
         solved[level] = known
-        lower_ref[level - 1] = operator
-    stacked = [solved[level] for level in range(1, depth)]
+        back_ref[level - 1] = operator
+    stacked = [solved[level] for level in range(1, top + 1)]
     stacked.append(jnp.zeros((size - top * columns, size), jnp.float32))
     solved_ref[...] = jnp.concatenate(stacked, axis=0).T
     parent = conjugate(known, width).astype(jnp.bfloat16)
@@ -373,7 +365,9 @@
     ).astype(jnp.bfloat16)
 
 
-def top_kernel(targets_ref, near_ref, far_ref, pick_ref, update_ref, _, parent_ref, solved_ref, half_ref, all_ref):
+def top_kernel(
+    targets_ref, near_ref, far_ref, pick_ref, update_ref, _, __, parent_ref, solved_ref, half_ref, all_ref
+):
     depth, devices = targets_ref.shape
     columns, size = update_ref.shape
     slab = size // devices
@@ -535,15 +529,37 @@
     )(*[in_vmem(ready) for ready in (held, first_round, pair_first, second_round, picks)])
     far = exchange(held, 4, 0)
 
-    def hold(piece):
-        return pl.pallas_call(
-            hold_kernel,
-            out_shape=pltpu.VMEM(piece.shape, piece.dtype),
-            in_specs=[whole(VMEM)] * 2,
-            out_specs=whole(VMEM),
-        )(in_vmem(piece), in_vmem(held))
-
-    far_piece = hold(xor_permute(leaf_inv, "rhs", 3))
+    kept_targets = pltpu.with_memory_space_constraint(kept_targets, SMEM)
+    update, partial_x, lower = pl.pallas_call(
+        near_kernel,
+        out_shape=(
+            pltpu.VMEM((columns, size), jnp.float32),
+            pltpu.VMEM((depth - 1, columns, size), jnp.float32),
+            pltpu.VMEM((depth - 1, size, size), jnp.bfloat16),
+        ),
+        in_specs=[whole(SMEM)] + [whole(VMEM)] * 2,
+        out_specs=(whole(VMEM),) * 3,
+        scratch_shapes=[pltpu.VMEM((size, 2 * size), jnp.bfloat16)],
+        cost_estimate=pl.CostEstimate(flops=0, bytes_accessed=0, transcendentals=0),
+    )(kept_targets, *[in_vmem(ready) for ready in (held, picks)])
+    far_piece = pl.pallas_call(
+        hold_kernel,
+        out_shape=pltpu.VMEM(leaf_inv.shape, leaf_inv.dtype),
+        in_specs=[whole(VMEM)] * 2,
+        out_specs=whole(VMEM),
+    )(in_vmem(xor_permute(leaf_inv, "rhs", 3)), in_vmem(update))
+    known, back, known_leaf, operator = pl.pallas_call(
+        operator_kernel,
+        out_shape=(
+            pltpu.VMEM((size, size), jnp.float32),
+            pltpu.VMEM((depth - 1, size, size), jnp.bfloat16),
+            pltpu.VMEM((columns, 2 * leaf_rows), jnp.float32),
+            pltpu.VMEM((size, 2 * leaf_rows), jnp.bfloat16),
+        ),
+        in_specs=[whole(VMEM)] * 4,
+        out_specs=(whole(VMEM),) * 4,
+        cost_estimate=pl.CostEstimate(flops=0, bytes_accessed=0, transcendentals=0),
+    )(*[in_vmem(ready) for ready in (partial_x, lower, panel_rows, far_piece)])
     partial = pl.pallas_call(
         functools.partial(leaf_kernel, (0, 3)),
         out_shape=pltpu.VMEM((2, columns, leaf_rows), jnp.float32),
@@ -551,32 +567,20 @@
         out_specs=whole(VMEM),
         cost_estimate=pl.CostEstimate(flops=0, bytes_accessed=0, transcendentals=0),
     )(*[in_vmem(ready) for ready in (leaf_z, leaf_inv, far_piece)])
-    kept_targets = pltpu.with_memory_space_constraint(kept_targets, SMEM)
-    update, known, lower, known_leaf, operator = pl.pallas_call(
-        near_kernel,
-        out_shape=(
-            pltpu.VMEM((columns, size), jnp.float32),
-            pltpu.VMEM((size, size), jnp.float32),
-            pltpu.VMEM((depth - 1, size, size), jnp.bfloat16),
-            pltpu.VMEM((columns, 2 * leaf_rows), jnp.float32),
-            pltpu.VMEM((size, 2 * leaf_rows), jnp.bfloat16),
-        ),
-        in_specs=[whole(SMEM)] + [whole(VMEM)] * 3,
-        out_specs=(whole(VMEM),) * 5,
-        scratch_shapes=[pltpu.VMEM((size, 2 * size), jnp.bfloat16)],
-        cost_estimate=pl.CostEstimate(flops=0, bytes_accessed=0, transcendentals=0),
-    )(kept_targets, *[in_vmem(ready) for ready in (held, picks, panel_rows)])
     parent_x, top_x = pl.pallas_call(
         top_kernel,
         out_shape=(
             pltpu.VMEM((columns, size), jnp.bfloat16),
             pltpu.VMEM((size, columns), jnp.float32),
         ),
-        in_specs=[whole(SMEM)] + [whole(VMEM)] * 5,
+        in_specs=[whole(SMEM)] + [whole(VMEM)] * 6,
         out_specs=(whole(VMEM),) * 2,
-        scratch_shapes=[pltpu.VMEM((size, 2 * size), jnp.bfloat16)] * 2,
+        scratch_shapes=[
+            pltpu.VMEM((size, 2 * size), jnp.bfloat16),
+            pltpu.VMEM((size, 2 * size), jnp.bfloat16),
+        ],
         cost_estimate=pl.CostEstimate(flops=3 * 10**9, bytes_accessed=0, transcendentals=0),
-    )(kept_targets, *[in_vmem(ready) for ready in (held, far, picks, update, partial)])
+    )(kept_targets, *[in_vmem(ready) for ready in (held, far, picks, update, partial, known_leaf)])
     pair_pieces = (xor_permute(leaf_inv, "rhs", 1), xor_permute(far_piece, "rhs", 1))
     leaf_x, sep_x = pl.pallas_call(
         functools.partial(finish_kernel, (1, 2)),
@@ -596,7 +600,7 @@
         kept_targets,
         *[
             in_vmem(ready)
-            for ready in (leaf_z, partial, parent_x, top_x, known, lower, known_leaf, operator) + pair_pieces
+            for ready in (leaf_z, partial, parent_x, top_x, known, back, known_leaf, operator) + pair_pieces
         ],
     )
     return leaf_x, sep_x.transpose(0, 3, 1, 2)

time: 15.9 us -> 15.9 us (level)
    pallas_call x1 -> x2, Pallas kernels: 0.02 us -> 0.44 us  [the longest x1 0.42 us: body(): pl.pallas_call(operator_kernel, out_shape=(pltpu.VMEM((size, size), jnp.f...]
    ppermute x5, waiting for transfers between devices: 0.15 us -> 0.51 us  [xor_permute(): lax.ppermute(values_in, axis, [(source, source ^ offset) for source in ra...]
    pallas_call x1, Pallas kernels: 0.82 us -> 0.47 us  [body(): pl.pallas_call(near_kernel, out_shape=(pltpu.VMEM((columns, size), jnp.fl...]
    ppermute x3, waiting for transfers between devices: 0.9 us -> 0.6 us  [exchange(): return lax.ppermute(values_in, ('leaf', 'rhs'), partners)]
  transfers between devices with their start and end apart: 8 -> 8, of which waited for: 3 -> 4; matrix products, arithmetic and copies ran while one was open for 0% -> 0% of each run, Pallas kernels for 15% -> 16%
where the time goes in v6:
time: 15.9 us; the launch traced here: 15.8 us
  starting transfers between devices  9.51 us (60%)
  Pallas kernels  3.58 us (23%)
  between operations  1.44 us (9%)
  waiting for transfers between devices  1.12 us (7%)
    ppermute x3, starting transfers between devices, exchange(): return lax.ppermute(values_in, ('leaf', 'rhs'), partners)  7.03 us
    ppermute x5, starting transfers between devices, xor_permute(): lax.ppermute(values_in, axis, [(source, source ^ offset) for source in ra...  2.48 us
    pallas_call x1, Pallas kernels, body(): pl.pallas_call(functools.partial(finish_kernel, (1, 2)), out_shape=(jax.S...  0.92 us
    pallas_call x1, Pallas kernels, body(): pl.pallas_call(functools.partial(prepare_kernel, (1 + depth) * columns),...  0.78 us
    ppermute x3, waiting for transfers between devices, exchange(): return lax.ppermute(values_in, ('leaf', 'rhs'), partners)  0.6 us
    pallas_call x1, Pallas kernels, body(): pl.pallas_call(top_kernel, out_shape=(pltpu.VMEM((columns, size), jnp.bfl...  0.59 us
    ppermute x5, waiting for transfers between devices, xor_permute(): lax.ppermute(values_in, axis, [(source, source ^ offset) for source in ra...  0.51 us
    pallas_call x1, Pallas kernels, body(): pl.pallas_call(near_kernel, out_shape=(pltpu.VMEM((columns, size), jnp.fl...  0.47 us
  transfers between devices with their start and end apart: 8, of which 4 were waited for; matrix products, arithmetic and copies ran while one was open for 0% of the time, Pallas kernels for 16%

profile of v6, /device:TPU:0, one launch (start us, length us, event | category | flops | bytes accessed | tf_op | source)
XLA Modules:
  0.0 15.8 jit_solution(17630333608260783413)
XLA Ops:
  0.6 0.0 copy-start.3
  0.6 0.0 copy-start.1
  0.7 0.0 copy-start
  0.7 0.0 copy-start.2
  0.7 0.0 copy-start.5
  0.7 0.0 copy-start.4
  1.4 0.0 copy-done.3
  1.4 0.1 copy-done.1
  1.5 0.0 copy-done.2
  1.5 0.0 copy-done.5
  1.5 0.0 copy-done.4
  1.5 0.2 %shard_map.96 = (bf16[16,256]{1,0:T(8,128)(2,1)S(1)}, bf16[16,128]{1,0:T(8,128)(2,1)S(1)}, bf16[32,512]{1,0:T(8,128)(2,1)S(1)}) custom-call(s32[1]{0:T(128)S(6)} %copy.10.live_ref, f32[8,128]{1,0:T(8,128)S(1)} %shard_map.95._, f32[2,16,512]{2,1,0:T(8,128)S(1)} %copy-done.1, bf16[2,8,512]{2,1,0:T(8,128)(2,1)S(1)} %bitcast.4, f32[2,3,8,16]{3,2,1,0:T(8,128)S(1)} %bitcast.5, ...), custom_call_target="tpu_custom_call" | custom-call | tf_op jit(solution)/shard_map/pallas_call | solution.py:478
  1.7 2.4 %collective-permute-start = (bf16[16,256]{1,0:T(8,128)(2,1)S(1)}, bf16[16,256]{1,0:T(8,128)(2,1)S(1)}, u32[]{:S(2)}, u32[]{:S(2)}) collective-permute-start(bf16[16,256]{1,0:T(8,128)(2,1)S(1)} %get-tuple-element.21.own_ref), channel_id=1, source_target_pairs={{0,5},{1,4},{2,7},{3,6},{4,1},{5,0},{6,3},{7,2},{8,13},{9,12},{10,... | collective-permute-start | bytes 24584 | tf_op jit(solution)/shard_map/ppermute | solution.py:495
  4.1 0.7 %collective-permute-start.1 = (bf16[16,128]{1,0:T(8,128)(2,1)S(1)}, bf16[16,128]{1,0:T(8,128)(2,1)S(1)}, u32[]{:S(2)}, u32[]{:S(2)}) collective-permute-start(bf16[16,128]{1,0:T(8,128)(2,1)S(1)} %get-tuple-element.22), channel_id=1, source_target_pairs={{0,1},{1,0},{2,3},{3,2},{4,5},{5,4},{6,7},{7,6},{8,9},{9,8},{10,11... | collective-permute-start | bytes 12296 | tf_op jit(solution)/shard_map/ppermute | solution.py:146
  4.8 0.0 copy-done
  4.8 1.1 %collective-permute-start.2 = (bf16[2,128,512]{2,1,0:T(8,128)(2,1)S(1)}, bf16[2,128,512]{2,1,0:T(8,128)(2,1)S(1)}, u32[]{:S(2)}, u32[]{:S(2)}) collective-permute-start(bf16[2,128,512]{2,1,0:T(8,128)(2,1)S(1)} %copy-done), channel_id=1, source_target_pairs={{0,3},{1,2},{2,1},{3,0},{4,7},{5,6},{6,5},{7,4},{8,11},{9,10},{10,... | collective-permute-start | bytes 786440 | tf_op jit(solution)/shard_map/ppermute | solution.py:146
  5.9 0.0 collective-permute-done.1.pair_ref
  5.9 0.0 collective-permute-done.received_ref.first_ref
  5.9 1.8 %collective-permute-start.4 = (bf16[32,384]{1,0:T(8,128)(2,1)S(1)}, bf16[32,384]{1,0:T(8,128)(2,1)S(1)}, u32[]{:S(2)}, u32[]{:S(2)}) collective-permute-start(bf16[32,384]{1,0:T(8,128)(2,1)S(1)} %get-tuple-element.26), channel_id=1, source_target_pairs={{0,9},{1,8},{2,11},{3,10},{4,13},{5,12},{6,15},{7,14},{8,1},{9,0},... | collective-permute-start | bytes 73736 | tf_op jit(solution)/shard_map/ppermute | solution.py:495
  7.7 0.3 %collective-permute-start.3 = (bf16[16,128]{1,0:T(8,128)(2,1)S(1)}, bf16[16,128]{1,0:T(8,128)(2,1)S(1)}, u32[]{:S(2)}, u32[]{:S(2)}) collective-permute-start(bf16[16,128]{1,0:T(8,128)(2,1)S(1)} %get-tuple-element.23._), channel_id=1, source_target_pairs={{0,1},{1,0},{2,3},{3,2},{4,5},{5,4},{6,7},{7,6},{8,9},{9,8},{10,11... | collective-permute-start | bytes 12296 | tf_op jit(solution)/shard_map/ppermute | solution.py:146
  7.9 0.8 %shard_map.98 = (bf16[128,1024]{1,0:T(8,128)(2,1)S(1)}, bf16[5,128,128]{2,1,0:T(8,128)(2,1)S(1)}, s32[3,8]{1,0:T(4,128)S(4)}) custom-call(s32[1]{0:T(128)S(6)} %copy.10.live_ref, s32[3,8]{1,0:T(4,128)} %targets_ref.1, bf16[2,8,512]{2,1,0:T(8,128)(2,1)} %bitcast.3, bf16[16,128]{1,0:T(8,128)(2,1)S(1)} %get-tuple-element.23._), custom_call_target="tpu_custom_call" | custom-call | tf_op jit(solution)/shard_map/pallas_call | solution.py:510
  8.7 0.1 collective-permute-done.3.pair_ref
  8.8 0.4 %collective-permute-done.4.second_ref = bf16[32,384]{1,0:T(8,128)(2,1)S(1)} collective-permute-done((bf16[32,384]{1,0:T(8,128)(2,1)S(1)}, bf16[32,384]{1,0:T(8,128)(2,1)S(1)}, u32[]{:S(2)}, u32[]{:S(2)}) %collective-permute-start.4) | collective-permute-done | bytes 24608 | tf_op jit(solution)/shard_map/ppermute | solution.py:495
  9.2 2.9 %collective-permute-start.5 = (bf16[64,256]{1,0:T(8,128)(2,1)S(1)}, bf16[64,256]{1,0:T(8,128)(2,1)S(1)}, u32[]{:S(2)}, u32[]{:S(2)}) collective-permute-start(bf16[64,256]{1,0:T(8,128)(2,1)S(1)} %shard_map.99.near_ref), channel_id=1, source_target_pairs={{0,16},{1,17},{2,18},{3,19},{4,20},{5,21},{6,22},{7,23},{8,24},{9,... | collective-permute-start | bytes 98312 | tf_op jit(solution)/shard_map/ppermute | solution.py:495
  12.1 0.2 %collective-permute-start.6 = (bf16[2,128,512]{2,1,0:T(8,128)(2,1)S(1)}, bf16[2,128,512]{2,1,0:T(8,128)(2,1)S(1)}, u32[]{:S(2)}, u32[]{:S(2)}) collective-permute-start(bf16[2,128,512]{2,1,0:T(8,128)(2,1)S(1)} %copy-done), channel_id=1, source_target_pairs={{0,1},{1,0},{2,3},{3,2},{4,5},{5,4},{6,7},{7,6},{8,9},{9,8},{10,11... | collective-permute-start | bytes 786440 | tf_op jit(solution)/shard_map/ppermute | solution.py:146
  12.3 0.5 %shard_map.100 = (f32[16,128]{1,0:T(8,128)S(1)}, f32[2,16,128]{2,1,0:T(8,128)S(1)}, bf16[2,128,128]{2,1,0:T(8,128)(2,1)S(1)}) custom-call(s32[3,8]{1,0:T(4,128)S(4)} %get-tuple-element.24.targets_ref, bf16[64,256]{1,0:T(8,128)(2,1)S(1)} %shard_map.99.near_ref, bf16[5,128,128]{2,1,0:T(8,128)(2,1)S(1)} %get-tuple-element.27._.pick_ref), custom_call_target="tpu_custom_call" | custom-call | tf_op jit(solution)/shard_map/pallas_call | solution.py:533
  12.8 0.4 %collective-permute-done.2.piece_ref = bf16[2,128,512]{2,1,0:T(8,128)(2,1)S(1)} collective-permute-done((bf16[2,128,512]{2,1,0:T(8,128)(2,1)S(1)}, bf16[2,128,512]{2,1,0:T(8,128)(2,1)S(1)}, u32[]{:S(2)}, u32[]{:S(2)}) %collective-permute-start.2) | collective-permute-done | bytes 262176 | tf_op jit(solution)/shard_map/ppermute | solution.py:146
  13.2 0.2 %collective-permute-start.7 = (bf16[2,128,512]{2,1,0:T(8,128)(2,1)S(1)}, bf16[2,128,512]{2,1,0:T(8,128)(2,1)S(1)}, u32[]{:S(2)}, u32[]{:S(2)}) collective-permute-start(bf16[2,128,512]{2,1,0:T(8,128)(2,1)S(1)} %shard_map.101.refs_1_._), channel_id=1, source_target_pairs={{0,1},{1,0},{2,3},{3,2},{4,5},{5,4},{6,7},{7,6},{8,9},{9,8},{10,11... | collective-permute-start | bytes 786440 | tf_op jit(solution)/shard_map/ppermute | solution.py:146
  13.4 0.2 %shard_map.102._.partial_ref = f32[2,16,512]{2,1,0:T(8,128)S(1)} custom-call(bf16[32,512]{1,0:T(8,128)(2,1)S(1)} %get-tuple-element.25.z_ref, bf16[2,128,512]{2,1,0:T(8,128)(2,1)S(1)} %copy-done, bf16[2,128,512]{2,1,0:T(8,128)(2,1)S(1)} %shard_map.101.refs_1_._), custom_call_target="tpu_custom_call" | custom-call | tf_op jit(solution)/shard_map/pallas_call | solution.py:563
  13.6 0.4 %shard_map.103 = (f32[128,128]{1,0:T(8,128)S(1)}, bf16[2,128,128]{2,1,0:T(8,128)(2,1)S(1)}, f32[16,1024]{1,0:T(8,128)S(1)}, bf16[128,1024]{1,0:T(8,128)(2,1)S(1)}) custom-call(f32[2,16,128]{2,1,0:T(8,128)S(1)} %get-tuple-element.29.partial_ref, bf16[2,128,128]{2,1,0:T(8,128)(2,1)S(1)} %get-tuple-element.30.lower_ref, ...), custom_call_target="tpu_custom_call" | custom-call | tf_op jit(solution)/shard_map/pallas_call | solution.py:551
  14.0 0.2 %collective-permute-done.5.far_ref = bf16[64,256]{1,0:T(8,128)(2,1)S(1)} collective-permute-done((bf16[64,256]{1,0:T(8,128)(2,1)S(1)}, bf16[64,256]{1,0:T(8,128)(2,1)S(1)}, u32[]{:S(2)}, u32[]{:S(2)}) %collective-permute-start.5) | collective-permute-done | bytes 32800 | tf_op jit(solution)/shard_map/ppermute | solution.py:495
  14.2 0.6 %shard_map.104 = (bf16[16,128]{1,0:T(8,128)(2,1)S(1)}, f32[128,16]{1,0:T(8,128)S(1)}) custom-call(s32[3,8]{1,0:T(4,128)S(4)} %get-tuple-element.24.targets_ref, bf16[64,256]{1,0:T(8,128)(2,1)S(1)} %shard_map.99.near_ref, bf16[64,256]{1,0:T(8,128)(2,1)S(1)} %collective-permute-done.5.far_ref, bf16[5,128,128]{2,1,0:T(8,128)(2,1)S(1)} %get-tuple-element.27._.pick_ref, ...), custom_call_target="tpu_custom_call" | custom-call | flops 3000000000 | tf_op jit(solution)/shard_map/pallas_call | solution.py:570
  14.8 0.0 collective-permute-done.6.refs_0_
  14.8 0.0 collective-permute-done.7.refs_1_
  14.8 0.9 %shard_map.105 = (f32[2,16,512]{2,1,0:T(8,128)}, f32[2,3,8,16]{3,2,1,0:T(8,128)}) custom-call(s32[1]{0:T(128)S(6)} %copy.10.live_ref, s32[3,8]{1,0:T(4,128)S(4)} %get-tuple-element.24.targets_ref, bf16[32,512]{1,0:T(8,128)(2,1)S(1)} %get-tuple-element.25.z_ref, f32[2,16,512]{2,1,0:T(8,128)S(1)} %shard_map.102._.partial_ref, ...), custom_call_target="tpu_custom_call" | custom-call | tf_op jit(solution)/shard_map/pallas_call | solution.py:585
  (4 shorter events, 0.0 us)
Async XLA Ops:
  0.6 0.8 %copy-start.3 = (f32[2,16,3,8]{1,3,2,0:T(8,128)S(1)}, f32[2,16,3,8]{1,3,2,0:T(8,128)}, u32[]{:S(2)}) copy-start(f32[2,16,3,8]{1,3,2,0:T(8,128)} %param.9) | copy-start | bytes 9220
  0.6 0.8 %copy-start.1 = (f32[2,16,512]{2,1,0:T(8,128)S(1)}, f32[2,16,512]{2,1,0:T(8,128)}, u32[]{:S(2)}) copy-start(f32[2,16,512]{2,1,0:T(8,128)} %leaf_rhs_ref.1) | copy-start | bytes 196612
  0.7 4.1 %copy-start = (bf16[2,128,512]{2,1,0:T(8,128)(2,1)S(1)}, bf16[2,128,512]{2,1,0:T(8,128)(2,1)}, u32[]{:S(2)}) copy-start(bf16[2,128,512]{2,1,0:T(8,128)(2,1)} %refs_0_.1) | copy-start | bytes 786436
  0.7 0.8 %copy-start.2 = (bf16[2,512,8]{1,2,0:T(8,128)(2,1)S(1)}, bf16[2,512,8]{1,2,0:T(8,128)(2,1)}, u32[]{:S(2)}) copy-start(bf16[2,512,8]{1,2,0:T(8,128)(2,1)} %param.11) | copy-start | bytes 49156
  0.7 0.8 %copy-start.5 = (bf16[2,8,48]{2,1,0:T(8,128)(2,1)S(1)}, bf16[2,8,48]{2,1,0:T(8,128)(2,1)}, u32[]{:S(2)}) copy-start(bf16[2,8,48]{2,1,0:T(8,128)(2,1)} %sep_low_ref.1) | copy-start | bytes 4612
  0.7 0.8 %copy-start.4 = (bf16[2,8,112]{2,1,0:T(8,128)(2,1)S(1)}, bf16[2,8,112]{2,1,0:T(8,128)(2,1)}, u32[]{:S(2)}) copy-start(bf16[2,8,112]{2,1,0:T(8,128)(2,1)} %inv_ref.1) | copy-start | bytes 10756
  1.7 4.2 %collective-permute-start = (bf16[16,256]{1,0:T(8,128)(2,1)S(1)}, bf16[16,256]{1,0:T(8,128)(2,1)S(1)}, u32[]{:S(2)}, u32[]{:S(2)}) collective-permute-start(bf16[16,256]{1,0:T(8,128)(2,1)S(1)} %get-tuple-element.21.own_ref), channel_id=1, source_target_pairs={{0,5},{1,4},{2,7},{3,6},{4,1},{5,0},{6,3},{7,2},{8,13},{9,12},{10,... | collective-permute-start | bytes 24584 | tf_op jit(solution)/shard_map/ppermute | solution.py:495
  4.1 1.8 %collective-permute-start.1 = (bf16[16,128]{1,0:T(8,128)(2,1)S(1)}, bf16[16,128]{1,0:T(8,128)(2,1)S(1)}, u32[]{:S(2)}, u32[]{:S(2)}) collective-permute-start(bf16[16,128]{1,0:T(8,128)(2,1)S(1)} %get-tuple-element.22), channel_id=1, source_target_pairs={{0,1},{1,0},{2,3},{3,2},{4,5},{5,4},{6,7},{7,6},{8,9},{9,8},{10,11... | collective-permute-start | bytes 12296 | tf_op jit(solution)/shard_map/ppermute | solution.py:146
  4.8 8.4 %collective-permute-start.2 = (bf16[2,128,512]{2,1,0:T(8,128)(2,1)S(1)}, bf16[2,128,512]{2,1,0:T(8,128)(2,1)S(1)}, u32[]{:S(2)}, u32[]{:S(2)}) collective-permute-start(bf16[2,128,512]{2,1,0:T(8,128)(2,1)S(1)} %copy-done), channel_id=1, source_target_pairs={{0,3},{1,2},{2,1},{3,0},{4,7},{5,6},{6,5},{7,4},{8,11},{9,10},{10,... | collective-permute-start | bytes 786440 | tf_op jit(solution)/shard_map/ppermute | solution.py:146
  5.9 3.3 %collective-permute-start.4 = (bf16[32,384]{1,0:T(8,128)(2,1)S(1)}, bf16[32,384]{1,0:T(8,128)(2,1)S(1)}, u32[]{:S(2)}, u32[]{:S(2)}) collective-permute-start(bf16[32,384]{1,0:T(8,128)(2,1)S(1)} %get-tuple-element.26), channel_id=1, source_target_pairs={{0,9},{1,8},{2,11},{3,10},{4,13},{5,12},{6,15},{7,14},{8,1},{9,0},... | collective-permute-start | bytes 73736 | tf_op jit(solution)/shard_map/ppermute | solution.py:495
  7.7 1.2 %collective-permute-start.3 = (bf16[16,128]{1,0:T(8,128)(2,1)S(1)}, bf16[16,128]{1,0:T(8,128)(2,1)S(1)}, u32[]{:S(2)}, u32[]{:S(2)}) collective-permute-start(bf16[16,128]{1,0:T(8,128)(2,1)S(1)} %get-tuple-element.23._), channel_id=1, source_target_pairs={{0,1},{1,0},{2,3},{3,2},{4,5},{5,4},{6,7},{7,6},{8,9},{9,8},{10,11... | collective-permute-start | bytes 12296 | tf_op jit(solution)/shard_map/ppermute | solution.py:146
  9.2 5.0 %collective-permute-start.5 = (bf16[64,256]{1,0:T(8,128)(2,1)S(1)}, bf16[64,256]{1,0:T(8,128)(2,1)S(1)}, u32[]{:S(2)}, u32[]{:S(2)}) collective-permute-start(bf16[64,256]{1,0:T(8,128)(2,1)S(1)} %shard_map.99.near_ref), channel_id=1, source_target_pairs={{0,16},{1,17},{2,18},{3,19},{4,20},{5,21},{6,22},{7,23},{8,24},{9,... | collective-permute-start | bytes 98312 | tf_op jit(solution)/shard_map/ppermute | solution.py:495
  12.1 2.7 %collective-permute-start.6 = (bf16[2,128,512]{2,1,0:T(8,128)(2,1)S(1)}, bf16[2,128,512]{2,1,0:T(8,128)(2,1)S(1)}, u32[]{:S(2)}, u32[]{:S(2)}) collective-permute-start(bf16[2,128,512]{2,1,0:T(8,128)(2,1)S(1)} %copy-done), channel_id=1, source_target_pairs={{0,1},{1,0},{2,3},{3,2},{4,5},{5,4},{6,7},{7,6},{8,9},{9,8},{10,11... | collective-permute-start | bytes 786440 | tf_op jit(solution)/shard_map/ppermute | solution.py:146
  13.2 1.6 %collective-permute-start.7 = (bf16[2,128,512]{2,1,0:T(8,128)(2,1)S(1)}, bf16[2,128,512]{2,1,0:T(8,128)(2,1)S(1)}, u32[]{:S(2)}, u32[]{:S(2)}) collective-permute-start(bf16[2,128,512]{2,1,0:T(8,128)(2,1)S(1)} %shard_map.101.refs_1_._), channel_id=1, source_target_pairs={{0,1},{1,0},{2,3},{3,2},{4,5},{5,4},{6,7},{7,6},{8,9},{9,8},{10,11... | collective-permute-start | bytes 786440 | tf_op jit(solution)/shard_map/ppermute | solution.py:146

commit v7 on v6

--- a/solution.py
+++ b/solution.py
@@ -161,7 +161,7 @@
     out_ref[...] = jnp.zeros_like(out_ref)
 
 
-def pack_kernel(live_ref, _, leaf_rhs_ref, low_ref, rhs_ref, inv_ref, sep_low_ref, out_ref, tile_ref, z_ref):
+def pack_kernel(live_ref, _, leaf_rhs_ref, low_ref, rhs_ref, inv_ref, sep_low_ref, out_ref, tile_ref, send_ref, z_ref):
     columns = leaf_rhs_ref.shape[1]
     depth = rhs_ref.shape[1]
     leaf_z, _ = masked_rows(leaf_rhs_ref[...], live_ref)
@@ -176,19 +176,23 @@
         product[width:, :columns] + product[:width, columns:],
     ]
     used = (1 + depth) * columns + sep_low_ref.shape[2]
-    halves = []
+    halves, turned = [], []
     for part in range(2):
         pieces = [update[part]] + [rhs_ref[part, level] for level in range(depth)]
         pieces.append(sep_low_ref[part].astype(jnp.float32))
         if used < 128:
             pieces.append(jnp.zeros((width, 128 - used), jnp.float32))
-        pieces.append(inv_ref[part].astype(jnp.float32))
-        if inv_ref.shape[2] < 128:
-            pieces.append(jnp.zeros((width, 128 - inv_ref.shape[2]), jnp.float32))
+        inverse = inv_ref[part].astype(jnp.float32)
+        below = width * (2**depth - 2)
+        gap = jnp.zeros((width, 128 - inverse.shape[1]), jnp.float32)
+        pieces += [inverse[:, below:], inverse[:, :below], gap]
+        turned.append(jnp.concatenate([inverse[:, :below], gap, inverse[:, below:]], axis=1))
         halves.append(jnp.concatenate(pieces, axis=1))
     packed = jnp.concatenate(halves, axis=0).astype(jnp.bfloat16)
     out_ref[...] = packed
     tile_ref[...] = packed[:, : tile_ref.shape[1]]
+    send_ref[:, : tile_ref.shape[1]] = packed[:, : tile_ref.shape[1]]
+    send_ref[:, tile_ref.shape[1] :] = jnp.concatenate(turned, axis=0).astype(jnp.bfloat16)
 
 
 def piece_product(step, z_ref, piece_ref):
@@ -232,10 +236,17 @@
     lane_row = lax.broadcasted_iota(jnp.int32, (1, size), 1)
     for level in range(1, depth + 1):
         offset = width * (2**level - 2) + lane_row % width
+        inverse_offset = lane_row % width if level == depth else offset + width * devices
         target_lane = jnp.zeros((1, size), jnp.int32)
         for block in range(devices):
             target_lane = jnp.where(lane_row // slab == block, targets_ref[level - 1, block], target_lane)
-        pick_ref[level - 1] = jnp.where(row == offset + target_lane * width, 1.0, 0.0).astype(jnp.bfloat16)
+        pick_ref[level - 1] = jnp.where(row == inverse_offset + target_lane * width, 1.0, 0.0).astype(
+            jnp.bfloat16
+        )
+        if level == depth:
+            pick_ref[2 * depth - 1] = jnp.where(
+                row == size // 2 + inverse_offset + target_lane * width, 1.0, 0.0
+            ).astype(jnp.bfloat16)
         if level < depth:
             own_lane = (lane_row // slab) % 2**level
             pick_ref[depth + level - 1] = jnp.where(
@@ -253,7 +264,7 @@
     tile_ref[...] = received_ref[:, :tile]
 
 
-def join_second_kernel(side_lanes, own_ref, first_ref, pair_ref, second_ref, _, out_ref):
+def join_second_kernel(side_lanes, own_ref, first_ref, pair_ref, second_ref, _, out_ref, send_ref):
     rows, lanes = own_ref.shape
     tile = pair_ref.shape[1]
     out_ref[:rows, :] = own_ref[...]
@@ -268,6 +279,15 @@
     out_ref[2 * rows : 3 * rows, :tile] = merged.astype(jnp.bfloat16)
     out_ref[2 * rows : 3 * rows, tile:] = second_ref[:rows, tile:lanes]
     out_ref[3 * rows :, :] = second_ref[rows:, :lanes]
+    half = tile // 2
+    send_ref[:rows, :] = own_ref[:, :tile]
+    send_ref[rows : 2 * rows, :] = pair_ref[...]
+    send_ref[2 * rows : 3 * rows, :] = merged.astype(jnp.bfloat16)
+    send_ref[3 * rows : 4 * rows, :] = second_ref[rows:, :tile]
+    send_ref[4 * rows : 5 * rows, :half] = own_ref[:, tile : tile + half]
+    send_ref[4 * rows : 5 * rows, half:] = first_ref[:, tile + half :]
+    send_ref[5 * rows :, :half] = second_ref[:rows, tile : tile + half]
+    send_ref[5 * rows :, half:] = second_ref[rows:, tile + half : 2 * tile]
 
 
 def hold_kernel(piece_ref, _, out_ref):
@@ -307,10 +327,13 @@
 
 
 def front_matrix(source, pick, level, slab):
-    size, width = pick.shape[0], slab // 2
+    return front_of(jnp.dot(source, pick, preferred_element_type=jnp.float32), level, slab)
+
+
+def front_of(plain, level, slab):
+    size, width = plain.shape[0], slab // 2
     row = lax.broadcasted_iota(jnp.int32, (size, size), 0)
     lane = lax.broadcasted_iota(jnp.int32, (size, size), 1)
-    plain = jnp.dot(source, pick, preferred_element_type=jnp.float32)
     swapped = plain.reshape(size // slab, 2, width, size)
     swapped = jnp.concatenate([swapped[:, 1:], swapped[:, :1]], axis=1).reshape(size, size)
     signed = jnp.where((row // width) % 2 == 0, plain, -plain)
@@ -324,12 +347,18 @@
     return jnp.where((lane // width) % 2 == 0, values_in, -values_in)
 
 
-def near_kernel(targets_ref, near_ref, pick_ref, update_ref, partial_ref, lower_ref, all_ref):
+def near_kernel(targets_ref, near_ref, pick_ref, update_ref, partial_ref, lower_ref, kept_ref, all_ref):
     depth, devices = targets_ref.shape
     columns, size = update_ref.shape
     slab = size // devices
-    all_ref[: size // 2, :] = near_ref[...]
-    all_ref[size // 2 :, :] = jnp.zeros_like(near_ref)
+    half = size // 2
+    for place_ref in (kept_ref, all_ref):
+        place_ref[:half, :] = near_ref[...]
+        for slot in range(1, devices // 2, 2):
+            rows = slice(slot * slab, (slot + 1) * slab)
+            turned = pltpu.roll(near_ref[rows, size:].astype(jnp.float32), half, 1)
+            place_ref[rows, size:] = turned.astype(jnp.bfloat16)
+    all_ref[half:, :] = jnp.zeros_like(near_ref)
     arriving = side_of(rows_of(targets_ref, 0, all_ref, slab), 0, columns)
     for level in range(1, depth):
         raw = rows_of(targets_ref, level, all_ref, slab)
@@ -371,18 +400,32 @@
     depth, devices = targets_ref.shape
     columns, size = update_ref.shape
     slab = size // devices
-    half_ref[: size // 2, :] = jnp.zeros_like(near_ref)
-    half_ref[size // 2 :, :] = far_ref[...]
-    all_ref[: size // 2, :] = near_ref[...]
-    all_ref[size // 2 :, :] = far_ref[...]
+    half = size // 2
+    half_ref[:half, :] = jnp.zeros((half, size), jnp.bfloat16)
+    half_ref[half:, :] = far_ref[:half]
+    all_ref[:half, :] = near_ref[...]
+    all_ref[half:, :size] = far_ref[:half]
+    for slot in range(devices // 2):
+        rows = slice(half + slot // 2 * slab, half + (slot // 2 + 1) * slab)
+        all_ref[half + slot * slab : half + (slot + 1) * slab, size:] = far_ref[rows]
     raw = rows_of(targets_ref, depth, all_ref, slab)
-    inverse = front_matrix(raw[:, size:], pick_ref[depth - 1], depth, slab)
+    row_block = lax.broadcasted_iota(jnp.int32, (size, size), 0) // slab
+    upper = jnp.zeros((size, size), jnp.int32)
+    for block in range(devices):
+        slot = owner(targets_ref, depth, block) ^ lax.axis_index("leaf")
+        upper = jnp.where(row_block == block, slot, upper)
+    plain = jnp.where(
+        (upper >= devices // 2) & (upper % 2 == 1),
+        jnp.dot(raw[:, size:], pick_ref[2 * depth - 1], preferred_element_type=jnp.float32),
+        jnp.dot(raw[:, size:], pick_ref[depth - 1], preferred_element_type=jnp.float32),
+    )
+    inverse = front_of(plain, depth, slab)
     waiting = side_of(raw, depth, columns) - update_ref[...]
     arriving = side_of(rows_of(targets_ref, 0, half_ref, slab), 0, columns)
     for level in range(1, depth):
         raw = rows_of(targets_ref, level, half_ref, slab)
         level_z = (side_of(raw, level, columns) - arriving).astype(jnp.bfloat16)
-        lower = front_matrix(raw[:, :size], pick_ref[depth + level - 1], level, slab)
+        lower = front_matrix(raw, pick_ref[depth + level - 1], level, slab)
         arriving = jnp.dot(level_z, lower, preferred_element_type=jnp.float32)
     level_z = (waiting - arriving).astype(jnp.bfloat16)
     solved = jnp.dot(level_z, inverse, preferred_element_type=jnp.float32)
@@ -475,15 +518,16 @@
         out_specs=whole(VMEM),
         cost_estimate=pl.CostEstimate(flops=10**9, bytes_accessed=0, transcendentals=0),
     )()
-    held, own_tile, leaf_z = pl.pallas_call(
+    held, own_tile, sent, leaf_z = pl.pallas_call(
         pack_kernel,
         out_shape=(
             pltpu.VMEM((slab, 2 * size), jnp.bfloat16),
             pltpu.VMEM((slab, size), jnp.bfloat16),
+            pltpu.VMEM((slab, 2 * size), jnp.bfloat16),
             pltpu.VMEM((2 * columns, leaf_rows), jnp.bfloat16),
         ),
         in_specs=[whole(SMEM)] + [whole(VMEM)] * 6,
-        out_specs=(whole(VMEM),) * 3,
+        out_specs=(whole(VMEM),) * 4,
     )(leaf_live, *[in_vmem(part) for part in (first,) + tree_parts])
 
     def exchange(values_in, offset, flip):
@@ -494,7 +538,7 @@
         ]
         return lax.ppermute(values_in, ("leaf", "rhs"), partners)
 
-    first_round = exchange(held, 1, 1)
+    first_round = exchange(sent, 1, 1)
     pair_tile = xor_permute(own_tile, "rhs", 1)
     second_part, first_tile = pl.pallas_call(
         join_first_kernel,
@@ -505,13 +549,13 @@
         in_specs=[whole(VMEM)] * 3,
         out_specs=(whole(VMEM),) * 2,
         cost_estimate=pl.CostEstimate(flops=10**11, bytes_accessed=0, transcendentals=0),
-    )(in_vmem(held), in_vmem(first_round), in_vmem(pair_tile))
+    )(*[in_vmem(ready) for ready in (held, first_round, pair_tile)])
     second_round = exchange(second_part, 2, 1)
     panel_rows, picks, kept_targets = pl.pallas_call(
         functools.partial(prepare_kernel, (1 + depth) * columns),
         out_shape=(
             pltpu.VMEM((size, 2 * leaf_rows), jnp.bfloat16),
-            pltpu.VMEM((2 * depth - 1, size, size), jnp.bfloat16),
+            pltpu.VMEM((2 * depth, size, size), jnp.bfloat16),
             pltpu.SMEM(targets.shape, jnp.int32),
         ),
         in_specs=[whole(SMEM), whole(SMEM), whole(VMEM), whole(VMEM)],
@@ -520,25 +564,29 @@
     )(leaf_live, targets, panel, in_vmem(first_tile))
 
     pair_first = xor_permute(first_tile, "rhs", 1)
-    held = pl.pallas_call(
+    held, sent = pl.pallas_call(
         functools.partial(join_second_kernel, (1 + depth) * columns),
-        out_shape=pltpu.VMEM((4 * slab, 2 * size), jnp.bfloat16),
+        out_shape=(
+            pltpu.VMEM((4 * slab, 2 * size), jnp.bfloat16),
+            pltpu.VMEM((6 * slab, size), jnp.bfloat16),
+        ),
         in_specs=[whole(VMEM)] * 5,
-        out_specs=whole(VMEM),
+        out_specs=(whole(VMEM),) * 2,
         cost_estimate=pl.CostEstimate(flops=0, bytes_accessed=0, transcendentals=0),
     )(*[in_vmem(ready) for ready in (held, first_round, pair_first, second_round, picks)])
-    far = exchange(held, 4, 0)
+    far = exchange(sent, 4, 0)
 
     kept_targets = pltpu.with_memory_space_constraint(kept_targets, SMEM)
-    update, partial_x, lower = pl.pallas_call(
+    update, partial_x, lower, kept_near = pl.pallas_call(
         near_kernel,
         out_shape=(
             pltpu.VMEM((columns, size), jnp.float32),
             pltpu.VMEM((depth - 1, columns, size), jnp.float32),
             pltpu.VMEM((depth - 1, size, size), jnp.bfloat16),
+            pltpu.VMEM((size // 2, 2 * size), jnp.bfloat16),
         ),
         in_specs=[whole(SMEM)] + [whole(VMEM)] * 2,
-        out_specs=(whole(VMEM),) * 3,
+        out_specs=(whole(VMEM),) * 4,
         scratch_shapes=[pltpu.VMEM((size, 2 * size), jnp.bfloat16)],
         cost_estimate=pl.CostEstimate(flops=0, bytes_accessed=0, transcendentals=0),
     )(kept_targets, *[in_vmem(ready) for ready in (held, picks)])
@@ -576,11 +624,11 @@
         in_specs=[whole(SMEM)] + [whole(VMEM)] * 6,
         out_specs=(whole(VMEM),) * 2,
         scratch_shapes=[
-            pltpu.VMEM((size, 2 * size), jnp.bfloat16),
+            pltpu.VMEM((size, size), jnp.bfloat16),
             pltpu.VMEM((size, 2 * size), jnp.bfloat16),
         ],
         cost_estimate=pl.CostEstimate(flops=3 * 10**9, bytes_accessed=0, transcendentals=0),
-    )(kept_targets, *[in_vmem(ready) for ready in (held, far, picks, update, partial, known_leaf)])
+    )(kept_targets, *[in_vmem(ready) for ready in (kept_near, far, picks, update, partial, known_leaf)])
     pair_pieces = (xor_permute(leaf_inv, "rhs", 1), xor_permute(far_piece, "rhs", 1))
     leaf_x, sep_x = pl.pallas_call(
         functools.partial(finish_kernel, (1, 2)),

time: 15.9 us -> 16 us (level)
  waiting for transfers between devices: 1.12 us -> 0.94 us
  transfers between devices with their start and end apart: 8 -> 8, of which waited for: 4 -> 5; matrix products, arithmetic and copies ran while one was open for 0% -> 0% of each run, Pallas kernels for 16% -> 16%
where the time goes in v7:
time: 16 us; the launch traced here: 15.8 us
  starting transfers between devices  9.62 us (60%)
  Pallas kernels  3.67 us (23%)
  between operations  1.45 us (9%)
  waiting for transfers between devices  0.94 us (6%)
    ppermute x3, starting transfers between devices, exchange(): return lax.ppermute(values_in, ('leaf', 'rhs'), partners)  7.14 us
    ppermute x5, starting transfers between devices, xor_permute(): lax.ppermute(values_in, axis, [(source, source ^ offset) for source in ra...  2.48 us
    pallas_call x1, Pallas kernels, body(): pl.pallas_call(functools.partial(finish_kernel, (1, 2)), out_shape=(jax.S...  0.91 us
    pallas_call x1, Pallas kernels, body(): pl.pallas_call(functools.partial(prepare_kernel, (1 + depth) * columns),...  0.78 us
    pallas_call x1, Pallas kernels, body(): pl.pallas_call(top_kernel, out_shape=(pltpu.VMEM((columns, size), jnp.bfl...  0.61 us
    pallas_call x1, Pallas kernels, body(): pl.pallas_call(near_kernel, out_shape=(pltpu.VMEM((columns, size), jnp.fl...  0.54 us
    ppermute x3, waiting for transfers between devices, exchange(): return lax.ppermute(values_in, ('leaf', 'rhs'), partners)  0.49 us
    ppermute x5, waiting for transfers between devices, xor_permute(): lax.ppermute(values_in, axis, [(source, source ^ offset) for source in ra...  0.44 us
  transfers between devices with their start and end apart: 8, of which 5 were waited for; matrix products, arithmetic and copies ran while one was open for 0% of the time, Pallas kernels for 16%

profile of v7, /device:TPU:0, one launch (start us, length us, event | category | flops | bytes accessed | tf_op | source)
XLA Modules:
  0.0 15.8 jit_solution(12237850481491187459)
XLA Ops:
  0.6 0.0 copy-start.3
  0.6 0.0 copy-start.1
  0.7 0.0 copy-start
  0.7 0.0 copy-start.2
  0.7 0.0 copy-start.5
  0.7 0.0 copy-start.4
  1.4 0.0 copy-done.3
  1.4 0.1 copy-done.1
  1.5 0.0 copy-done.2
  1.5 0.0 copy-done.5
  1.5 0.0 copy-done.4
  1.5 0.2 %shard_map.96 = (bf16[16,256]{1,0:T(8,128)(2,1)S(1)}, bf16[16,128]{1,0:T(8,128)(2,1)S(1)}, bf16[16,256]{1,0:T(8,128)(2,1)S(1)}, bf16[32,512]{1,0:T(8,128)(2,1)S(1)}) custom-call(s32[1]{0:T(128)S(6)} %copy.10.live_ref, f32[8,128]{1,0:T(8,128)S(1)} %shard_map.95._, f32[2,16,512]{2,1,0:T(8,128)S(1)} %copy-done.1, bf16[2,8,512]{2,1,0:T(8,128)(2,1)S(1)} %bitcast.4, ...), custom_call_target="tpu_custom_call" | custom-call | tf_op jit(solution)/shard_map/pallas_call | solution.py:521
  1.7 2.5 %collective-permute-start = (bf16[16,256]{1,0:T(8,128)(2,1)S(1)}, bf16[16,256]{1,0:T(8,128)(2,1)S(1)}, u32[]{:S(2)}, u32[]{:S(2)}) collective-permute-start(bf16[16,256]{1,0:T(8,128)(2,1)S(1)} %get-tuple-element.26), channel_id=1, source_target_pairs={{0,5},{1,4},{2,7},{3,6},{4,1},{5,0},{6,3},{7,2},{8,13},{9,12},{10,... | collective-permute-start | bytes 24584 | tf_op jit(solution)/shard_map/ppermute | solution.py:539
  4.2 0.7 %collective-permute-start.1 = (bf16[16,128]{1,0:T(8,128)(2,1)S(1)}, bf16[16,128]{1,0:T(8,128)(2,1)S(1)}, u32[]{:S(2)}, u32[]{:S(2)}) collective-permute-start(bf16[16,128]{1,0:T(8,128)(2,1)S(1)} %get-tuple-element.27), channel_id=1, source_target_pairs={{0,1},{1,0},{2,3},{3,2},{4,5},{5,4},{6,7},{7,6},{8,9},{9,8},{10,11... | collective-permute-start | bytes 12296 | tf_op jit(solution)/shard_map/ppermute | solution.py:146
  4.8 0.0 copy-done
  4.8 1.1 %collective-permute-start.2 = (bf16[2,128,512]{2,1,0:T(8,128)(2,1)S(1)}, bf16[2,128,512]{2,1,0:T(8,128)(2,1)S(1)}, u32[]{:S(2)}, u32[]{:S(2)}) collective-permute-start(bf16[2,128,512]{2,1,0:T(8,128)(2,1)S(1)} %copy-done), channel_id=1, source_target_pairs={{0,3},{1,2},{2,1},{3,0},{4,7},{5,6},{6,5},{7,4},{8,11},{9,10},{10,... | collective-permute-start | bytes 786440 | tf_op jit(solution)/shard_map/ppermute | solution.py:146
  5.9 0.0 collective-permute-done.1.pair_ref
  5.9 0.0 collective-permute-done.received_ref.first_ref
  5.9 1.8 %collective-permute-start.4 = (bf16[32,384]{1,0:T(8,128)(2,1)S(1)}, bf16[32,384]{1,0:T(8,128)(2,1)S(1)}, u32[]{:S(2)}, u32[]{:S(2)}) collective-permute-start(bf16[32,384]{1,0:T(8,128)(2,1)S(1)} %get-tuple-element.31), channel_id=1, source_target_pairs={{0,9},{1,8},{2,11},{3,10},{4,13},{5,12},{6,15},{7,14},{8,1},{9,0},... | collective-permute-start | bytes 73736 | tf_op jit(solution)/shard_map/ppermute | solution.py:539
  7.7 0.3 %collective-permute-start.3 = (bf16[16,128]{1,0:T(8,128)(2,1)S(1)}, bf16[16,128]{1,0:T(8,128)(2,1)S(1)}, u32[]{:S(2)}, u32[]{:S(2)}) collective-permute-start(bf16[16,128]{1,0:T(8,128)(2,1)S(1)} %get-tuple-element.28._), channel_id=1, source_target_pairs={{0,1},{1,0},{2,3},{3,2},{4,5},{5,4},{6,7},{7,6},{8,9},{9,8},{10,11... | collective-permute-start | bytes 12296 | tf_op jit(solution)/shard_map/ppermute | solution.py:146
  8.0 0.8 %shard_map.98 = (bf16[128,1024]{1,0:T(8,128)(2,1)S(1)}, bf16[6,128,128]{2,1,0:T(8,128)(2,1)S(1)}, s32[3,8]{1,0:T(4,128)S(4)}) custom-call(s32[1]{0:T(128)S(6)} %copy.10.live_ref, s32[3,8]{1,0:T(4,128)} %targets_ref.1, bf16[2,8,512]{2,1,0:T(8,128)(2,1)} %bitcast.3, bf16[16,128]{1,0:T(8,128)(2,1)S(1)} %get-tuple-element.28._), custom_call_target="tpu_custom_call" | custom-call | tf_op jit(solution)/shard_map/pallas_call | solution.py:554
  8.8 0.1 collective-permute-done.3.pair_ref
  8.9 0.4 %collective-permute-done.4.second_ref = bf16[32,384]{1,0:T(8,128)(2,1)S(1)} collective-permute-done((bf16[32,384]{1,0:T(8,128)(2,1)S(1)}, bf16[32,384]{1,0:T(8,128)(2,1)S(1)}, u32[]{:S(2)}, u32[]{:S(2)}) %collective-permute-start.4) | collective-permute-done | bytes 24608 | tf_op jit(solution)/shard_map/ppermute | solution.py:539
  9.3 2.9 %collective-permute-start.5 = (bf16[96,128]{1,0:T(8,128)(2,1)S(1)}, bf16[96,128]{1,0:T(8,128)(2,1)S(1)}, u32[]{:S(2)}, u32[]{:S(2)}) collective-permute-start(bf16[96,128]{1,0:T(8,128)(2,1)S(1)} %get-tuple-element.36), channel_id=1, source_target_pairs={{0,16},{1,17},{2,18},{3,19},{4,20},{5,21},{6,22},{7,23},{8,24},{9,... | collective-permute-start | bytes 73736 | tf_op jit(solution)/shard_map/ppermute | solution.py:539
  12.2 0.2 %collective-permute-start.6 = (bf16[2,128,512]{2,1,0:T(8,128)(2,1)S(1)}, bf16[2,128,512]{2,1,0:T(8,128)(2,1)S(1)}, u32[]{:S(2)}, u32[]{:S(2)}) collective-permute-start(bf16[2,128,512]{2,1,0:T(8,128)(2,1)S(1)} %copy-done), channel_id=1, source_target_pairs={{0,1},{1,0},{2,3},{3,2},{4,5},{5,4},{6,7},{7,6},{8,9},{9,8},{10,11... | collective-permute-start | bytes 786440 | tf_op jit(solution)/shard_map/ppermute | solution.py:146
  12.5 0.5 %shard_map.100 = (f32[16,128]{1,0:T(8,128)S(1)}, f32[2,16,128]{2,1,0:T(8,128)S(1)}, bf16[2,128,128]{2,1,0:T(8,128)(2,1)S(1)}, bf16[64,256]{1,0:T(8,128)(2,1)S(1)}) custom-call(s32[3,8]{1,0:T(4,128)S(4)} %get-tuple-element.29.targets_ref, bf16[64,256]{1,0:T(8,128)(2,1)S(1)} %get-tuple-element.33.near_ref, bf16[6,128,128]{2,1,0:T(8,128)(2,1)S(1)} %get-tuple-element.32._.pick_ref), custom_call_target="tpu_custom_call" | custom-call | tf_op jit(solution)/shard_map/pallas_call | solution.py:580
  13.0 0.3 %collective-permute-done.2.piece_ref = bf16[2,128,512]{2,1,0:T(8,128)(2,1)S(1)} collective-permute-done((bf16[2,128,512]{2,1,0:T(8,128)(2,1)S(1)}, bf16[2,128,512]{2,1,0:T(8,128)(2,1)S(1)}, u32[]{:S(2)}, u32[]{:S(2)}) %collective-permute-start.2) | collective-permute-done | bytes 262176 | tf_op jit(solution)/shard_map/ppermute | solution.py:146
  13.3 0.2 %collective-permute-start.7 = (bf16[2,128,512]{2,1,0:T(8,128)(2,1)S(1)}, bf16[2,128,512]{2,1,0:T(8,128)(2,1)S(1)}, u32[]{:S(2)}, u32[]{:S(2)}) collective-permute-start(bf16[2,128,512]{2,1,0:T(8,128)(2,1)S(1)} %shard_map.101.refs_1_._), channel_id=1, source_target_pairs={{0,1},{1,0},{2,3},{3,2},{4,5},{5,4},{6,7},{7,6},{8,9},{9,8},{10,11... | collective-permute-start | bytes 786440 | tf_op jit(solution)/shard_map/ppermute | solution.py:146
  13.5 0.2 %shard_map.102._.partial_ref = f32[2,16,512]{2,1,0:T(8,128)S(1)} custom-call(bf16[32,512]{1,0:T(8,128)(2,1)S(1)} %get-tuple-element.30.z_ref, bf16[2,128,512]{2,1,0:T(8,128)(2,1)S(1)} %copy-done, bf16[2,128,512]{2,1,0:T(8,128)(2,1)S(1)} %shard_map.101.refs_1_._), custom_call_target="tpu_custom_call" | custom-call | tf_op jit(solution)/shard_map/pallas_call | solution.py:611
  13.6 0.4 %shard_map.103 = (f32[128,128]{1,0:T(8,128)S(1)}, bf16[2,128,128]{2,1,0:T(8,128)(2,1)S(1)}, f32[16,1024]{1,0:T(8,128)S(1)}, bf16[128,1024]{1,0:T(8,128)(2,1)S(1)}) custom-call(f32[2,16,128]{2,1,0:T(8,128)S(1)} %get-tuple-element.37.partial_ref, bf16[2,128,128]{2,1,0:T(8,128)(2,1)S(1)} %get-tuple-element.38.lower_ref, ...), custom_call_target="tpu_custom_call" | custom-call | tf_op jit(solution)/shard_map/pallas_call | solution.py:599
  14.1 0.1 collective-permute-done.5.far_ref
  14.2 0.6 %shard_map.104 = (bf16[16,128]{1,0:T(8,128)(2,1)S(1)}, f32[128,16]{1,0:T(8,128)S(1)}) custom-call(s32[3,8]{1,0:T(4,128)S(4)} %get-tuple-element.29.targets_ref, bf16[64,256]{1,0:T(8,128)(2,1)S(1)} %get-tuple-element.35.near_ref, bf16[96,128]{1,0:T(8,128)(2,1)S(1)} %collective-permute-done.5.far_ref, bf16[6,128,128]{2,1,0:T(8,128)(2,1)S(1)} %get-tuple-element.32._.pick_ref, ...), custom_call_target="tpu_custom_call" | custom-call | flops 3000000000 | tf_op jit(solution)/shard_map/pallas_call | solution.py:618
  14.8 0.0 collective-permute-done.6.refs_0_
  14.8 0.1 collective-permute-done.7.refs_1_
  14.9 0.9 %shard_map.105 = (f32[2,16,512]{2,1,0:T(8,128)}, f32[2,3,8,16]{3,2,1,0:T(8,128)}) custom-call(s32[1]{0:T(128)S(6)} %copy.10.live_ref, s32[3,8]{1,0:T(4,128)S(4)} %get-tuple-element.29.targets_ref, bf16[32,512]{1,0:T(8,128)(2,1)S(1)} %get-tuple-element.30.z_ref, f32[2,16,512]{2,1,0:T(8,128)S(1)} %shard_map.102._.partial_ref, ...), custom_call_target="tpu_custom_call" | custom-call | tf_op jit(solution)/shard_map/pallas_call | solution.py:633
  (4 shorter events, 0.0 us)
Async XLA Ops:
  0.6 0.8 %copy-start.3 = (f32[2,16,3,8]{1,3,2,0:T(8,128)S(1)}, f32[2,16,3,8]{1,3,2,0:T(8,128)}, u32[]{:S(2)}) copy-start(f32[2,16,3,8]{1,3,2,0:T(8,128)} %param.9) | copy-start | bytes 9220
  0.6 0.8 %copy-start.1 = (f32[2,16,512]{2,1,0:T(8,128)S(1)}, f32[2,16,512]{2,1,0:T(8,128)}, u32[]{:S(2)}) copy-start(f32[2,16,512]{2,1,0:T(8,128)} %leaf_rhs_ref.1) | copy-start | bytes 196612
  0.7 4.2 %copy-start = (bf16[2,128,512]{2,1,0:T(8,128)(2,1)S(1)}, bf16[2,128,512]{2,1,0:T(8,128)(2,1)}, u32[]{:S(2)}) copy-start(bf16[2,128,512]{2,1,0:T(8,128)(2,1)} %refs_0_.1) | copy-start | bytes 786436
  0.7 0.8 %copy-start.2 = (bf16[2,512,8]{1,2,0:T(8,128)(2,1)S(1)}, bf16[2,512,8]{1,2,0:T(8,128)(2,1)}, u32[]{:S(2)}) copy-start(bf16[2,512,8]{1,2,0:T(8,128)(2,1)} %param.11) | copy-start | bytes 49156
  0.7 0.8 %copy-start.5 = (bf16[2,8,48]{2,1,0:T(8,128)(2,1)S(1)}, bf16[2,8,48]{2,1,0:T(8,128)(2,1)}, u32[]{:S(2)}) copy-start(bf16[2,8,48]{2,1,0:T(8,128)(2,1)} %sep_low_ref.1) | copy-start | bytes 4612
  0.7 0.8 %copy-start.4 = (bf16[2,8,112]{2,1,0:T(8,128)(2,1)S(1)}, bf16[2,8,112]{2,1,0:T(8,128)(2,1)}, u32[]{:S(2)}) copy-start(bf16[2,8,112]{2,1,0:T(8,128)(2,1)} %inv_ref.1) | copy-start | bytes 10756
  1.7 4.2 %collective-permute-start = (bf16[16,256]{1,0:T(8,128)(2,1)S(1)}, bf16[16,256]{1,0:T(8,128)(2,1)S(1)}, u32[]{:S(2)}, u32[]{:S(2)}) collective-permute-start(bf16[16,256]{1,0:T(8,128)(2,1)S(1)} %get-tuple-element.26), channel_id=1, source_target_pairs={{0,5},{1,4},{2,7},{3,6},{4,1},{5,0},{6,3},{7,2},{8,13},{9,12},{10,... | collective-permute-start | bytes 24584 | tf_op jit(solution)/shard_map/ppermute | solution.py:539
  4.2 1.8 %collective-permute-start.1 = (bf16[16,128]{1,0:T(8,128)(2,1)S(1)}, bf16[16,128]{1,0:T(8,128)(2,1)S(1)}, u32[]{:S(2)}, u32[]{:S(2)}) collective-permute-start(bf16[16,128]{1,0:T(8,128)(2,1)S(1)} %get-tuple-element.27), channel_id=1, source_target_pairs={{0,1},{1,0},{2,3},{3,2},{4,5},{5,4},{6,7},{7,6},{8,9},{9,8},{10,11... | collective-permute-start | bytes 12296 | tf_op jit(solution)/shard_map/ppermute | solution.py:146
  4.8 8.4 %collective-permute-start.2 = (bf16[2,128,512]{2,1,0:T(8,128)(2,1)S(1)}, bf16[2,128,512]{2,1,0:T(8,128)(2,1)S(1)}, u32[]{:S(2)}, u32[]{:S(2)}) collective-permute-start(bf16[2,128,512]{2,1,0:T(8,128)(2,1)S(1)} %copy-done), channel_id=1, source_target_pairs={{0,3},{1,2},{2,1},{3,0},{4,7},{5,6},{6,5},{7,4},{8,11},{9,10},{10,... | collective-permute-start | bytes 786440 | tf_op jit(solution)/shard_map/ppermute | solution.py:146
  5.9 3.3 %collective-permute-start.4 = (bf16[32,384]{1,0:T(8,128)(2,1)S(1)}, bf16[32,384]{1,0:T(8,128)(2,1)S(1)}, u32[]{:S(2)}, u32[]{:S(2)}) collective-permute-start(bf16[32,384]{1,0:T(8,128)(2,1)S(1)} %get-tuple-element.31), channel_id=1, source_target_pairs={{0,9},{1,8},{2,11},{3,10},{4,13},{5,12},{6,15},{7,14},{8,1},{9,0},... | collective-permute-start | bytes 73736 | tf_op jit(solution)/shard_map/ppermute | solution.py:539
  7.7 1.2 %collective-permute-start.3 = (bf16[16,128]{1,0:T(8,128)(2,1)S(1)}, bf16[16,128]{1,0:T(8,128)(2,1)S(1)}, u32[]{:S(2)}, u32[]{:S(2)}) collective-permute-start(bf16[16,128]{1,0:T(8,128)(2,1)S(1)} %get-tuple-element.28._), channel_id=1, source_target_pairs={{0,1},{1,0},{2,3},{3,2},{4,5},{5,4},{6,7},{7,6},{8,9},{9,8},{10,11... | collective-permute-start | bytes 12296 | tf_op jit(solution)/shard_map/ppermute | solution.py:146
  9.3 4.9 %collective-permute-start.5 = (bf16[96,128]{1,0:T(8,128)(2,1)S(1)}, bf16[96,128]{1,0:T(8,128)(2,1)S(1)}, u32[]{:S(2)}, u32[]{:S(2)}) collective-permute-start(bf16[96,128]{1,0:T(8,128)(2,1)S(1)} %get-tuple-element.36), channel_id=1, source_target_pairs={{0,16},{1,17},{2,18},{3,19},{4,20},{5,21},{6,22},{7,23},{8,24},{9,... | collective-permute-start | bytes 73736 | tf_op jit(solution)/shard_map/ppermute | solution.py:539
  12.2 2.6 %collective-permute-start.6 = (bf16[2,128,512]{2,1,0:T(8,128)(2,1)S(1)}, bf16[2,128,512]{2,1,0:T(8,128)(2,1)S(1)}, u32[]{:S(2)}, u32[]{:S(2)}) collective-permute-start(bf16[2,128,512]{2,1,0:T(8,128)(2,1)S(1)} %copy-done), channel_id=1, source_target_pairs={{0,1},{1,0},{2,3},{3,2},{4,5},{5,4},{6,7},{7,6},{8,9},{9,8},{10,11... | collective-permute-start | bytes 786440 | tf_op jit(solution)/shard_map/ppermute | solution.py:146
  13.3 1.6 %collective-permute-start.7 = (bf16[2,128,512]{2,1,0:T(8,128)(2,1)S(1)}, bf16[2,128,512]{2,1,0:T(8,128)(2,1)S(1)}, u32[]{:S(2)}, u32[]{:S(2)}) collective-permute-start(bf16[2,128,512]{2,1,0:T(8,128)(2,1)S(1)} %shard_map.101.refs_1_._), channel_id=1, source_target_pairs={{0,1},{1,0},{2,3},{3,2},{4,5},{5,4},{6,7},{7,6},{8,9},{9,8},{10,11... | collective-permute-start | bytes 786440 | tf_op jit(solution)/shard_map/ppermute | solution.py:146

commit v8 on v7

--- a/solution.py
+++ b/solution.py
@@ -205,11 +205,10 @@
     return real_acc[:columns] - imag_acc[columns:], imag_acc[:columns] + real_acc[columns:]
 
 
-def leaf_kernel(steps, z_ref, *refs):
-    out_ref = refs[-1]
-    products = [piece_product(step, z_ref, piece_ref) for step, piece_ref in zip(steps, refs[:-1])]
+def leaf_kernel(step, z_ref, piece_ref, _, out_ref):
+    product = piece_product(step, z_ref, piece_ref)
     for part in range(2):
-        out_ref[part] = sum(product[part] for product in products)
+        out_ref[part] = product[part]
 
 
 def prepare_kernel(low_start, live_ref, targets_ref, low_ref, _, panel_ref, pick_ref, kept_ref):
@@ -290,8 +289,13 @@
     send_ref[5 * rows :, half:] = second_ref[rows:, tile + half : 2 * tile]
 
 
-def hold_kernel(piece_ref, _, out_ref):
-    out_ref[...] = piece_ref[...]
+def far_kernel(step, z_ref, pair_z_ref, piece_ref, own_ref, out_ref, pair_out_ref):
+    own_product, pair_product = [
+        piece_product(step, source_ref, piece_ref) for source_ref in (z_ref, pair_z_ref)
+    ]
+    for part in range(2):
+        out_ref[part] = own_ref[part] + own_product[part]
+        pair_out_ref[part] = pair_product[part]
 
 
 def owner(targets_ref, level, block):
@@ -447,6 +451,7 @@
     lower_ref,
     leaf_ref,
     operator_ref,
+    far_ref,
     *refs,
 ):
     piece_refs, (leaf_out_ref, sep_out_ref) = refs[: len(steps)], refs[len(steps) : len(steps) + 2]
@@ -477,7 +482,7 @@
     products = [piece_product(step, z_ref, piece_ref) for step, piece_ref in zip(steps, piece_refs)]
     copies = []
     for part in range(2):
-        leaf_w = partial_ref[part] + sum(product[part] for product in products)
+        leaf_w = partial_ref[part] + far_ref[part] + sum(product[part] for product in products)
         leaf_place[part] = (
             jnp.where(live, leaf_w, 0.0) - from_tree[:, part * leaf_rows : (part + 1) * leaf_rows]
         )
@@ -590,12 +595,25 @@
         scratch_shapes=[pltpu.VMEM((size, 2 * size), jnp.bfloat16)],
         cost_estimate=pl.CostEstimate(flops=0, bytes_accessed=0, transcendentals=0),
     )(kept_targets, *[in_vmem(ready) for ready in (held, picks)])
-    far_piece = pl.pallas_call(
-        hold_kernel,
-        out_shape=pltpu.VMEM(leaf_inv.shape, leaf_inv.dtype),
-        in_specs=[whole(VMEM)] * 2,
+    own_part = pl.pallas_call(
+        functools.partial(leaf_kernel, 0),
+        out_shape=pltpu.VMEM((2, columns, leaf_rows), jnp.float32),
+        in_specs=[whole(VMEM)] * 3,
         out_specs=whole(VMEM),
-    )(in_vmem(xor_permute(leaf_inv, "rhs", 3)), in_vmem(update))
+        cost_estimate=pl.CostEstimate(flops=0, bytes_accessed=0, transcendentals=0),
+    )(*[in_vmem(ready) for ready in (leaf_z, leaf_inv, update)])
+    partial, pair_far = pl.pallas_call(
+        functools.partial(far_kernel, 3),
+        out_shape=(pltpu.VMEM((2, columns, leaf_rows), jnp.float32),) * 2,
+        in_specs=[whole(VMEM)] * 4,
+        out_specs=(whole(VMEM),) * 2,
+        cost_estimate=pl.CostEstimate(flops=0, bytes_accessed=0, transcendentals=0),
+    )(
+        *[
+            in_vmem(ready)
+            for ready in (leaf_z, xor_permute(leaf_z, "rhs", 1), xor_permute(leaf_inv, "rhs", 3), own_part)
+        ]
+    )
     known, back, known_leaf, operator = pl.pallas_call(
         operator_kernel,
         out_shape=(
@@ -607,14 +625,7 @@
         in_specs=[whole(VMEM)] * 4,
         out_specs=(whole(VMEM),) * 4,
         cost_estimate=pl.CostEstimate(flops=0, bytes_accessed=0, transcendentals=0),
-    )(*[in_vmem(ready) for ready in (partial_x, lower, panel_rows, far_piece)])
-    partial = pl.pallas_call(
-        functools.partial(leaf_kernel, (0, 3)),
-        out_shape=pltpu.VMEM((2, columns, leaf_rows), jnp.float32),
-        in_specs=[whole(VMEM)] * 3,
-        out_specs=whole(VMEM),
-        cost_estimate=pl.CostEstimate(flops=0, bytes_accessed=0, transcendentals=0),
-    )(*[in_vmem(ready) for ready in (leaf_z, leaf_inv, far_piece)])
+    )(*[in_vmem(ready) for ready in (partial_x, lower, panel_rows, partial)])
     parent_x, top_x = pl.pallas_call(
         top_kernel,
         out_shape=(
@@ -629,9 +640,9 @@
         ],
         cost_estimate=pl.CostEstimate(flops=3 * 10**9, bytes_accessed=0, transcendentals=0),
     )(kept_targets, *[in_vmem(ready) for ready in (kept_near, far, picks, update, partial, known_leaf)])
-    pair_pieces = (xor_permute(leaf_inv, "rhs", 1), xor_permute(far_piece, "rhs", 1))
+    pair_parts = (xor_permute(pair_far, "rhs", 1), xor_permute(leaf_inv, "rhs", 1))
     leaf_x, sep_x = pl.pallas_call(
-        functools.partial(finish_kernel, (1, 2)),
+        functools.partial(finish_kernel, (1,)),
         out_shape=(
             jax.ShapeDtypeStruct((2, columns, leaf_rows), jnp.float32),
             jax.ShapeDtypeStruct((2, depth, width, columns), jnp.float32),
@@ -648,7 +659,7 @@
         kept_targets,
         *[
             in_vmem(ready)
-            for ready in (leaf_z, partial, parent_x, top_x, known, back, known_leaf, operator) + pair_pieces
+            for ready in (leaf_z, partial, parent_x, top_x, known, back, known_leaf, operator) + pair_parts
         ],
     )
     return leaf_x, sep_x.transpose(0, 3, 1, 2)

time: 16 us -> 15.9 us (level)
  waiting for transfers between devices: 0.94 us -> 0.45 us
  starting transfers between devices: 9.62 us -> 9.93 us
    ppermute x3, waiting for transfers between devices: 0.49 us -> 0.19 us  [exchange(): return lax.ppermute(values_in, ('leaf', 'rhs'), partners)]
    ppermute x5 -> x6, starting transfers between devices: 2.48 us -> 2.78 us  [xor_permute(): lax.ppermute(values_in, axis, [(source, source ^ offset) for source in ra...]
    ppermute x5 -> x6, waiting for transfers between devices: 0.44 us -> 0.26 us  [xor_permute(): lax.ppermute(values_in, axis, [(source, source ^ offset) for source in ra...]
  transfers between devices with their start and end apart: 8 -> 9, of which waited for: 5 -> 4; matrix products, arithmetic and copies ran while one was open for 0% -> 0% of each run, Pallas kernels for 16% -> 17%
where the time goes in v8:
time: 15.9 us; the launch traced here: 15.7 us
  starting transfers between devices  9.93 us (62%)
  Pallas kernels  3.77 us (24%)
  between operations  1.46 us (9%)
  waiting for transfers between devices  0.45 us (3%)
    ppermute x3, starting transfers between devices, exchange(): return lax.ppermute(values_in, ('leaf', 'rhs'), partners)  7.14 us
    ppermute x6, starting transfers between devices, xor_permute(): lax.ppermute(values_in, axis, [(source, source ^ offset) for source in ra...  2.78 us
    pallas_call x1, Pallas kernels, body(): pl.pallas_call(functools.partial(finish_kernel, (1,)), out_shape=(jax.Sha...  0.91 us
    pallas_call x1, Pallas kernels, body(): pl.pallas_call(functools.partial(prepare_kernel, (1 + depth) * columns),...  0.78 us
    pallas_call x1, Pallas kernels, body(): pl.pallas_call(top_kernel, out_shape=(pltpu.VMEM((columns, size), jnp.bfl...  0.61 us
    pallas_call x1, Pallas kernels, body(): pl.pallas_call(near_kernel, out_shape=(pltpu.VMEM((columns, size), jnp.fl...  0.54 us
    pallas_call x1, Pallas kernels, body(): pl.pallas_call(operator_kernel, out_shape=(pltpu.VMEM((size, size), jnp.f...  0.39 us
  transfers between devices with their start and end apart: 9, of which 4 were waited for; matrix products, arithmetic and copies ran while one was open for 0% of the time, Pallas kernels for 17%

profile of v8, /device:TPU:0, one launch (start us, length us, event | category | flops | bytes accessed | tf_op | source)
XLA Modules:
  0.0 15.7 jit_solution(18357837798061459155)
XLA Ops:
  0.6 0.0 copy-start.1
  0.6 0.0 copy-start.3
  0.7 0.0 copy-start
  0.7 0.0 copy-start.2
  0.7 0.0 copy-start.5
  0.7 0.0 copy-start.4
  1.4 0.1 copy-done.1
  1.5 0.0 copy-done.3
  1.5 0.0 copy-done.2
  1.5 0.0 copy-done.5
  1.5 0.0 copy-done.4
  1.5 0.2 %shard_map.96 = (bf16[16,256]{1,0:T(8,128)(2,1)S(1)}, bf16[16,128]{1,0:T(8,128)(2,1)S(1)}, bf16[16,256]{1,0:T(8,128)(2,1)S(1)}, bf16[32,512]{1,0:T(8,128)(2,1)S(1)}) custom-call(s32[1]{0:T(128)S(6)} %copy.10.live_ref, f32[8,128]{1,0:T(8,128)S(1)} %shard_map.95._, f32[2,16,512]{2,1,0:T(8,128)S(1)} %copy-done.1, bf16[2,8,512]{2,1,0:T(8,128)(2,1)S(1)} %bitcast.4, ...), custom_call_target="tpu_custom_call" | custom-call | tf_op jit(solution)/shard_map/pallas_call | solution.py:526
  1.7 2.5 %collective-permute-start = (bf16[16,256]{1,0:T(8,128)(2,1)S(1)}, bf16[16,256]{1,0:T(8,128)(2,1)S(1)}, u32[]{:S(2)}, u32[]{:S(2)}) collective-permute-start(bf16[16,256]{1,0:T(8,128)(2,1)S(1)} %get-tuple-element.28), channel_id=1, source_target_pairs={{0,5},{1,4},{2,7},{3,6},{4,1},{5,0},{6,3},{7,2},{8,13},{9,12},{10,... | collective-permute-start | bytes 24584 | tf_op jit(solution)/shard_map/ppermute | solution.py:544
  4.1 0.7 %collective-permute-start.1 = (bf16[16,128]{1,0:T(8,128)(2,1)S(1)}, bf16[16,128]{1,0:T(8,128)(2,1)S(1)}, u32[]{:S(2)}, u32[]{:S(2)}) collective-permute-start(bf16[16,128]{1,0:T(8,128)(2,1)S(1)} %get-tuple-element.29), channel_id=1, source_target_pairs={{0,1},{1,0},{2,3},{3,2},{4,5},{5,4},{6,7},{7,6},{8,9},{9,8},{10,11... | collective-permute-start | bytes 12296 | tf_op jit(solution)/shard_map/ppermute | solution.py:146
  4.8 0.0 copy-done
  4.8 1.1 %collective-permute-start.3 = (bf16[2,128,512]{2,1,0:T(8,128)(2,1)S(1)}, bf16[2,128,512]{2,1,0:T(8,128)(2,1)S(1)}, u32[]{:S(2)}, u32[]{:S(2)}) collective-permute-start(bf16[2,128,512]{2,1,0:T(8,128)(2,1)S(1)} %copy-done), channel_id=1, source_target_pairs={{0,3},{1,2},{2,1},{3,0},{4,7},{5,6},{6,5},{7,4},{8,11},{9,10},{10,... | collective-permute-start | bytes 786440 | tf_op jit(solution)/shard_map/ppermute | solution.py:146
  5.9 0.0 collective-permute-done.1.pair_ref
  5.9 0.0 collective-permute-done.received_ref.first_ref
  5.9 1.8 %collective-permute-start.5 = (bf16[32,384]{1,0:T(8,128)(2,1)S(1)}, bf16[32,384]{1,0:T(8,128)(2,1)S(1)}, u32[]{:S(2)}, u32[]{:S(2)}) collective-permute-start(bf16[32,384]{1,0:T(8,128)(2,1)S(1)} %get-tuple-element.33), channel_id=1, source_target_pairs={{0,9},{1,8},{2,11},{3,10},{4,13},{5,12},{6,15},{7,14},{8,1},{9,0},... | collective-permute-start | bytes 73736 | tf_op jit(solution)/shard_map/ppermute | solution.py:544
  7.7 0.3 %collective-permute-start.2 = (bf16[32,512]{1,0:T(8,128)(2,1)S(1)}, bf16[32,512]{1,0:T(8,128)(2,1)S(1)}, u32[]{:S(2)}, u32[]{:S(2)}) collective-permute-start(bf16[32,512]{1,0:T(8,128)(2,1)S(1)} %get-tuple-element.32.z_ref), channel_id=1, source_target_pairs={{0,1},{1,0},{2,3},{3,2},{4,5},{5,4},{6,7},{7,6},{8,9},{9,8},{10,11... | collective-permute-start | bytes 98312 | tf_op jit(solution)/shard_map/ppermute | solution.py:146
  8.0 0.2 %collective-permute-start.4 = (bf16[16,128]{1,0:T(8,128)(2,1)S(1)}, bf16[16,128]{1,0:T(8,128)(2,1)S(1)}, u32[]{:S(2)}, u32[]{:S(2)}) collective-permute-start(bf16[16,128]{1,0:T(8,128)(2,1)S(1)} %get-tuple-element.30._), channel_id=1, source_target_pairs={{0,1},{1,0},{2,3},{3,2},{4,5},{5,4},{6,7},{7,6},{8,9},{9,8},{10,11... | collective-permute-start | bytes 12296 | tf_op jit(solution)/shard_map/ppermute | solution.py:146
  8.2 0.8 %shard_map.98 = (bf16[128,1024]{1,0:T(8,128)(2,1)S(1)}, bf16[6,128,128]{2,1,0:T(8,128)(2,1)S(1)}, s32[3,8]{1,0:T(4,128)S(4)}) custom-call(s32[1]{0:T(128)S(6)} %copy.10.live_ref, s32[3,8]{1,0:T(4,128)} %targets_ref.1, bf16[2,8,512]{2,1,0:T(8,128)(2,1)} %bitcast.3, bf16[16,128]{1,0:T(8,128)(2,1)S(1)} %get-tuple-element.30._), custom_call_target="tpu_custom_call" | custom-call | tf_op jit(solution)/shard_map/pallas_call | solution.py:559
  9.0 0.1 collective-permute-done.4.pair_ref
  9.1 0.1 collective-permute-done.5.second_ref
  9.3 2.9 %collective-permute-start.6 = (bf16[96,128]{1,0:T(8,128)(2,1)S(1)}, bf16[96,128]{1,0:T(8,128)(2,1)S(1)}, u32[]{:S(2)}, u32[]{:S(2)}) collective-permute-start(bf16[96,128]{1,0:T(8,128)(2,1)S(1)} %get-tuple-element.39), channel_id=1, source_target_pairs={{0,16},{1,17},{2,18},{3,19},{4,20},{5,21},{6,22},{7,23},{8,24},{9,... | collective-permute-start | bytes 73736 | tf_op jit(solution)/shard_map/ppermute | solution.py:544
  12.2 0.2 %collective-permute-start.8 = (bf16[2,128,512]{2,1,0:T(8,128)(2,1)S(1)}, bf16[2,128,512]{2,1,0:T(8,128)(2,1)S(1)}, u32[]{:S(2)}, u32[]{:S(2)}) collective-permute-start(bf16[2,128,512]{2,1,0:T(8,128)(2,1)S(1)} %copy-done), channel_id=1, source_target_pairs={{0,1},{1,0},{2,3},{3,2},{4,5},{5,4},{6,7},{7,6},{8,9},{9,8},{10,11... | collective-permute-start | bytes 786440 | tf_op jit(solution)/shard_map/ppermute | solution.py:146
  12.4 0.5 %shard_map.100 = (f32[16,128]{1,0:T(8,128)S(1)}, f32[2,16,128]{2,1,0:T(8,128)S(1)}, bf16[2,128,128]{2,1,0:T(8,128)(2,1)S(1)}, bf16[64,256]{1,0:T(8,128)(2,1)S(1)}) custom-call(s32[3,8]{1,0:T(4,128)S(4)} %get-tuple-element.31.targets_ref, bf16[64,256]{1,0:T(8,128)(2,1)S(1)} %get-tuple-element.35.near_ref, bf16[6,128,128]{2,1,0:T(8,128)(2,1)S(1)} %get-tuple-element.34._.pick_ref), custom_call_target="tpu_custom_call" | custom-call | tf_op jit(solution)/shard_map/pallas_call | solution.py:585
  13.0 0.1 shard_map.101.own_ref
  13.1 0.0 collective-permute-done.2.pair_z_ref
  13.2 0.1 collective-permute-done.3.piece_ref
  13.2 0.2 %shard_map.102 = (f32[2,16,512]{2,1,0:T(8,128)S(1)}, f32[2,16,512]{2,1,0:T(8,128)S(1)}) custom-call(bf16[32,512]{1,0:T(8,128)(2,1)S(1)} %get-tuple-element.32.z_ref, bf16[32,512]{1,0:T(8,128)(2,1)S(1)} %collective-permute-done.2.pair_z_ref, bf16[2,128,512]{2,1,0:T(8,128)(2,1)S(1)} %collective-permute-done.3.piece_ref, f32[2,16,512]{2,1,0:T(8,128)S(1)} %shard_map.101.own_ref), custom_call_target="tpu_custom_call" | custom-call | tf_op jit(solution)/shard_map/pallas_call | solution.py:605
  13.4 0.3 %collective-permute-start.7 = (f32[2,16,512]{2,1,0:T(8,128)S(1)}, f32[2,16,512]{2,1,0:T(8,128)S(1)}, u32[]{:S(2)}, u32[]{:S(2)}) collective-permute-start(f32[2,16,512]{2,1,0:T(8,128)S(1)} %get-tuple-element.49), channel_id=1, source_target_pairs={{0,1},{1,0},{2,3},{3,2},{4,5},{5,4},{6,7},{7,6},{8,9},{9,8},{10,11... | collective-permute-start | bytes 196616 | tf_op jit(solution)/shard_map/ppermute | solution.py:146
  13.7 0.4 %shard_map.103 = (f32[128,128]{1,0:T(8,128)S(1)}, bf16[2,128,128]{2,1,0:T(8,128)(2,1)S(1)}, f32[16,1024]{1,0:T(8,128)S(1)}, bf16[128,1024]{1,0:T(8,128)(2,1)S(1)}) custom-call(f32[2,16,128]{2,1,0:T(8,128)S(1)} %get-tuple-element.40.partial_ref, bf16[2,128,128]{2,1,0:T(8,128)(2,1)S(1)} %get-tuple-element.41.lower_ref, ...), custom_call_target="tpu_custom_call" | custom-call | tf_op jit(solution)/shard_map/pallas_call | solution.py:617
  14.1 0.1 collective-permute-done.6.far_ref
  14.2 0.6 %shard_map.104 = (bf16[16,128]{1,0:T(8,128)(2,1)S(1)}, f32[128,16]{1,0:T(8,128)S(1)}) custom-call(s32[3,8]{1,0:T(4,128)S(4)} %get-tuple-element.31.targets_ref, bf16[64,256]{1,0:T(8,128)(2,1)S(1)} %get-tuple-element.38.near_ref, bf16[96,128]{1,0:T(8,128)(2,1)S(1)} %collective-permute-done.6.far_ref, bf16[6,128,128]{2,1,0:T(8,128)(2,1)S(1)} %get-tuple-element.34._.pick_ref, ...), custom_call_target="tpu_custom_call" | custom-call | flops 3000000000 | tf_op jit(solution)/shard_map/pallas_call | solution.py:629
  14.8 0.0 collective-permute-done.8.refs_0_
  14.8 0.0 collective-permute-done.7.far_ref
  14.8 0.9 %shard_map.105 = (f32[2,16,512]{2,1,0:T(8,128)}, f32[2,3,8,16]{3,2,1,0:T(8,128)}) custom-call(s32[1]{0:T(128)S(6)} %copy.10.live_ref, s32[3,8]{1,0:T(4,128)S(4)} %get-tuple-element.31.targets_ref, bf16[32,512]{1,0:T(8,128)(2,1)S(1)} %get-tuple-element.32.z_ref, f32[2,16,512]{2,1,0:T(8,128)S(1)} %get-tuple-element.37._.partial_ref, ...), custom_call_target="tpu_custom_call" | custom-call | tf_op jit(solution)/shard_map/pallas_call | solution.py:644
  (3 shorter events, 0.0 us)
Async XLA Ops:
  0.6 0.8 %copy-start.1 = (f32[2,16,512]{2,1,0:T(8,128)S(1)}, f32[2,16,512]{2,1,0:T(8,128)}, u32[]{:S(2)}) copy-start(f32[2,16,512]{2,1,0:T(8,128)} %leaf_rhs_ref.1) | copy-start | bytes 196612
  0.6 0.8 %copy-start.3 = (f32[2,16,3,8]{1,3,2,0:T(8,128)S(1)}, f32[2,16,3,8]{1,3,2,0:T(8,128)}, u32[]{:S(2)}) copy-start(f32[2,16,3,8]{1,3,2,0:T(8,128)} %param.9) | copy-start | bytes 9220
  0.7 4.2 %copy-start = (bf16[2,128,512]{2,1,0:T(8,128)(2,1)S(1)}, bf16[2,128,512]{2,1,0:T(8,128)(2,1)}, u32[]{:S(2)}) copy-start(bf16[2,128,512]{2,1,0:T(8,128)(2,1)} %piece_ref.1) | copy-start | bytes 786436
  0.7 0.8 %copy-start.2 = (bf16[2,512,8]{1,2,0:T(8,128)(2,1)S(1)}, bf16[2,512,8]{1,2,0:T(8,128)(2,1)}, u32[]{:S(2)}) copy-start(bf16[2,512,8]{1,2,0:T(8,128)(2,1)} %param.11) | copy-start | bytes 49156
  0.7 0.8 %copy-start.5 = (bf16[2,8,48]{2,1,0:T(8,128)(2,1)S(1)}, bf16[2,8,48]{2,1,0:T(8,128)(2,1)}, u32[]{:S(2)}) copy-start(bf16[2,8,48]{2,1,0:T(8,128)(2,1)} %sep_low_ref.1) | copy-start | bytes 4612
  0.7 0.8 %copy-start.4 = (bf16[2,8,112]{2,1,0:T(8,128)(2,1)S(1)}, bf16[2,8,112]{2,1,0:T(8,128)(2,1)}, u32[]{:S(2)}) copy-start(bf16[2,8,112]{2,1,0:T(8,128)(2,1)} %inv_ref.1) | copy-start | bytes 10756
  1.7 4.2 %collective-permute-start = (bf16[16,256]{1,0:T(8,128)(2,1)S(1)}, bf16[16,256]{1,0:T(8,128)(2,1)S(1)}, u32[]{:S(2)}, u32[]{:S(2)}) collective-permute-start(bf16[16,256]{1,0:T(8,128)(2,1)S(1)} %get-tuple-element.28), channel_id=1, source_target_pairs={{0,5},{1,4},{2,7},{3,6},{4,1},{5,0},{6,3},{7,2},{8,13},{9,12},{10,... | collective-permute-start | bytes 24584 | tf_op jit(solution)/shard_map/ppermute | solution.py:544
  4.1 1.8 %collective-permute-start.1 = (bf16[16,128]{1,0:T(8,128)(2,1)S(1)}, bf16[16,128]{1,0:T(8,128)(2,1)S(1)}, u32[]{:S(2)}, u32[]{:S(2)}) collective-permute-start(bf16[16,128]{1,0:T(8,128)(2,1)S(1)} %get-tuple-element.29), channel_id=1, source_target_pairs={{0,1},{1,0},{2,3},{3,2},{4,5},{5,4},{6,7},{7,6},{8,9},{9,8},{10,11... | collective-permute-start | bytes 12296 | tf_op jit(solution)/shard_map/ppermute | solution.py:146
  4.8 8.4 %collective-permute-start.3 = (bf16[2,128,512]{2,1,0:T(8,128)(2,1)S(1)}, bf16[2,128,512]{2,1,0:T(8,128)(2,1)S(1)}, u32[]{:S(2)}, u32[]{:S(2)}) collective-permute-start(bf16[2,128,512]{2,1,0:T(8,128)(2,1)S(1)} %copy-done), channel_id=1, source_target_pairs={{0,3},{1,2},{2,1},{3,0},{4,7},{5,6},{6,5},{7,4},{8,11},{9,10},{10,... | collective-permute-start | bytes 786440 | tf_op jit(solution)/shard_map/ppermute | solution.py:146
  5.9 3.3 %collective-permute-start.5 = (bf16[32,384]{1,0:T(8,128)(2,1)S(1)}, bf16[32,384]{1,0:T(8,128)(2,1)S(1)}, u32[]{:S(2)}, u32[]{:S(2)}) collective-permute-start(bf16[32,384]{1,0:T(8,128)(2,1)S(1)} %get-tuple-element.33), channel_id=1, source_target_pairs={{0,9},{1,8},{2,11},{3,10},{4,13},{5,12},{6,15},{7,14},{8,1},{9,0},... | collective-permute-start | bytes 73736 | tf_op jit(solution)/shard_map/ppermute | solution.py:544
  7.7 5.4 %collective-permute-start.2 = (bf16[32,512]{1,0:T(8,128)(2,1)S(1)}, bf16[32,512]{1,0:T(8,128)(2,1)S(1)}, u32[]{:S(2)}, u32[]{:S(2)}) collective-permute-start(bf16[32,512]{1,0:T(8,128)(2,1)S(1)} %get-tuple-element.32.z_ref), channel_id=1, source_target_pairs={{0,1},{1,0},{2,3},{3,2},{4,5},{5,4},{6,7},{7,6},{8,9},{9,8},{10,11... | collective-permute-start | bytes 98312 | tf_op jit(solution)/shard_map/ppermute | solution.py:146
  8.0 1.2 %collective-permute-start.4 = (bf16[16,128]{1,0:T(8,128)(2,1)S(1)}, bf16[16,128]{1,0:T(8,128)(2,1)S(1)}, u32[]{:S(2)}, u32[]{:S(2)}) collective-permute-start(bf16[16,128]{1,0:T(8,128)(2,1)S(1)} %get-tuple-element.30._), channel_id=1, source_target_pairs={{0,1},{1,0},{2,3},{3,2},{4,5},{5,4},{6,7},{7,6},{8,9},{9,8},{10,11... | collective-permute-start | bytes 12296 | tf_op jit(solution)/shard_map/ppermute | solution.py:146
  9.3 4.9 %collective-permute-start.6 = (bf16[96,128]{1,0:T(8,128)(2,1)S(1)}, bf16[96,128]{1,0:T(8,128)(2,1)S(1)}, u32[]{:S(2)}, u32[]{:S(2)}) collective-permute-start(bf16[96,128]{1,0:T(8,128)(2,1)S(1)} %get-tuple-element.39), channel_id=1, source_target_pairs={{0,16},{1,17},{2,18},{3,19},{4,20},{5,21},{6,22},{7,23},{8,24},{9,... | collective-permute-start | bytes 73736 | tf_op jit(solution)/shard_map/ppermute | solution.py:544
  12.2 2.6 %collective-permute-start.8 = (bf16[2,128,512]{2,1,0:T(8,128)(2,1)S(1)}, bf16[2,128,512]{2,1,0:T(8,128)(2,1)S(1)}, u32[]{:S(2)}, u32[]{:S(2)}) collective-permute-start(bf16[2,128,512]{2,1,0:T(8,128)(2,1)S(1)} %copy-done), channel_id=1, source_target_pairs={{0,1},{1,0},{2,3},{3,2},{4,5},{5,4},{6,7},{7,6},{8,9},{9,8},{10,11... | collective-permute-start | bytes 786440 | tf_op jit(solution)/shard_map/ppermute | solution.py:146
  13.4 1.4 %collective-permute-start.7 = (f32[2,16,512]{2,1,0:T(8,128)S(1)}, f32[2,16,512]{2,1,0:T(8,128)S(1)}, u32[]{:S(2)}, u32[]{:S(2)}) collective-permute-start(f32[2,16,512]{2,1,0:T(8,128)S(1)} %get-tuple-element.49), channel_id=1, source_target_pairs={{0,1},{1,0},{2,3},{3,2},{4,5},{5,4},{6,7},{7,6},{8,9},{9,8},{10,11... | collective-permute-start | bytes 196616 | tf_op jit(solution)/shard_map/ppermute | solution.py:146

commit v9 on v8

--- a/solution.py
+++ b/solution.py
@@ -218,7 +218,6 @@
     depth, devices = targets_ref.shape
     width, leaf_rows = low_ref.shape[1:]
     slab = 2 * width
-    device = lax.axis_index("leaf")
     live = lax.broadcasted_iota(jnp.int32, (1, leaf_rows), 1) < live_ref[0] * 128
     low = [jnp.where(live, low_ref[part].astype(jnp.float32), 0.0) for part in range(2)]
     rows = jnp.concatenate(
@@ -228,8 +227,7 @@
         ],
         axis=0,
     ).astype(jnp.bfloat16)
-    panel_ref[...] = jnp.zeros_like(panel_ref)
-    panel_ref[pl.ds(pl.multiple_of(device * slab, slab), slab), :] = rows
+    panel_ref[...] = rows
     size = devices * slab
     row = lax.broadcasted_iota(jnp.int32, (size, size), 0)
     lane_row = lax.broadcasted_iota(jnp.int32, (1, size), 1)
@@ -391,10 +389,14 @@
     stacked = [solved[level] for level in range(1, top + 1)]
     stacked.append(jnp.zeros((size - top * columns, size), jnp.float32))
     solved_ref[...] = jnp.concatenate(stacked, axis=0).T
-    parent = conjugate(known, width).astype(jnp.bfloat16)
-    leaf_ref[...] = jnp.dot(parent, panel_ref[...], preferred_element_type=jnp.float32)
+    slab = 2 * width
+    rows = pl.ds(pl.multiple_of(lax.axis_index("leaf") * slab, slab), slab)
+    own = solved_ref[rows, :][:, :columns]
+    own = jnp.concatenate([own[:width], -own[width:]], axis=0).astype(jnp.bfloat16)
+    first = (((0,), (0,)), ((), ()))
+    leaf_ref[...] = lax.dot_general(own, panel_ref[...], first, preferred_element_type=jnp.float32)
     operator_ref[...] = lax.dot_general(
-        operator, panel_ref[...], (((0,), (0,)), ((), ())), preferred_element_type=jnp.float32
+        back_ref[0, rows, :], panel_ref[...], first, preferred_element_type=jnp.float32
     ).astype(jnp.bfloat16)
 
 
@@ -559,7 +561,7 @@
     panel_rows, picks, kept_targets = pl.pallas_call(
         functools.partial(prepare_kernel, (1 + depth) * columns),
         out_shape=(
-            pltpu.VMEM((size, 2 * leaf_rows), jnp.bfloat16),
+            pltpu.VMEM((slab, 2 * leaf_rows), jnp.bfloat16),
             pltpu.VMEM((2 * depth, size, size), jnp.bfloat16),
             pltpu.SMEM(targets.shape, jnp.int32),
         ),

time: 15.9 us -> 16 us (level)
  transfers between devices with their start and end apart: 9 -> 9, of which waited for: 4 -> 3; matrix products, arithmetic and copies ran while one was open for 0% -> 0% of each run, Pallas kernels for 17% -> 17%
where the time goes in v9:
time: 16 us; the launch traced here: 15.8 us
  starting transfers between devices  9.92 us (62%)
  Pallas kernels  3.87 us (24%)
  between operations  1.47 us (9%)
  waiting for transfers between devices  0.39 us (2%)
    ppermute x3, starting transfers between devices, exchange(): return lax.ppermute(values_in, ('leaf', 'rhs'), partners)  7.14 us
    ppermute x6, starting transfers between devices, xor_permute(): lax.ppermute(values_in, axis, [(source, source ^ offset) for source in ra...  2.78 us
    pallas_call x1, Pallas kernels, body(): pl.pallas_call(functools.partial(finish_kernel, (1,)), out_shape=(jax.Sha...  0.91 us
    pallas_call x1, Pallas kernels, body(): pl.pallas_call(functools.partial(prepare_kernel, (1 + depth) * columns),...  0.78 us
    pallas_call x1, Pallas kernels, body(): pl.pallas_call(top_kernel, out_shape=(pltpu.VMEM((columns, size), jnp.bfl...  0.61 us
    pallas_call x1, Pallas kernels, body(): pl.pallas_call(near_kernel, out_shape=(pltpu.VMEM((columns, size), jnp.fl...  0.54 us
    pallas_call x1, Pallas kernels, body(): pl.pallas_call(operator_kernel, out_shape=(pltpu.VMEM((size, size), jnp.f...  0.5 us
  transfers between devices with their start and end apart: 9, of which 3 were waited for; matrix products, arithmetic and copies ran while one was open for 0% of the time, Pallas kernels for 17%

profile of v9, /device:TPU:0, one launch (start us, length us, event | category | flops | bytes accessed | tf_op | source)
XLA Modules:
  0.0 15.8 jit_solution(14163702058905556476)
XLA Ops:
  0.6 0.0 copy-start.3
  0.6 0.0 copy-start.1
  0.7 0.0 copy-start
  0.7 0.0 copy-start.2
  0.7 0.0 copy-start.5
  0.7 0.0 copy-start.4
  1.4 0.0 copy-done.3
  1.4 0.1 copy-done.1
  1.5 0.0 copy-done.2
  1.5 0.0 copy-done.5
  1.5 0.0 copy-done.4
  1.5 0.2 %shard_map.96 = (bf16[16,256]{1,0:T(8,128)(2,1)S(1)}, bf16[16,128]{1,0:T(8,128)(2,1)S(1)}, bf16[16,256]{1,0:T(8,128)(2,1)S(1)}, bf16[32,512]{1,0:T(8,128)(2,1)S(1)}) custom-call(s32[1]{0:T(128)S(6)} %copy.10.live_ref, f32[8,128]{1,0:T(8,128)S(1)} %shard_map.95._, f32[2,16,512]{2,1,0:T(8,128)S(1)} %copy-done.1, bf16[2,8,512]{2,1,0:T(8,128)(2,1)S(1)} %bitcast.4, ...), custom_call_target="tpu_custom_call" | custom-call | tf_op jit(solution)/shard_map/pallas_call | solution.py:528
  1.7 2.5 %collective-permute-start = (bf16[16,256]{1,0:T(8,128)(2,1)S(1)}, bf16[16,256]{1,0:T(8,128)(2,1)S(1)}, u32[]{:S(2)}, u32[]{:S(2)}) collective-permute-start(bf16[16,256]{1,0:T(8,128)(2,1)S(1)} %get-tuple-element.28), channel_id=1, source_target_pairs={{0,5},{1,4},{2,7},{3,6},{4,1},{5,0},{6,3},{7,2},{8,13},{9,12},{10,... | collective-permute-start | bytes 24584 | tf_op jit(solution)/shard_map/ppermute | solution.py:546
  4.2 0.7 %collective-permute-start.1 = (bf16[16,128]{1,0:T(8,128)(2,1)S(1)}, bf16[16,128]{1,0:T(8,128)(2,1)S(1)}, u32[]{:S(2)}, u32[]{:S(2)}) collective-permute-start(bf16[16,128]{1,0:T(8,128)(2,1)S(1)} %get-tuple-element.29), channel_id=1, source_target_pairs={{0,1},{1,0},{2,3},{3,2},{4,5},{5,4},{6,7},{7,6},{8,9},{9,8},{10,11... | collective-permute-start | bytes 12296 | tf_op jit(solution)/shard_map/ppermute | solution.py:146
  4.8 0.0 copy-done
  4.8 1.1 %collective-permute-start.3 = (bf16[2,128,512]{2,1,0:T(8,128)(2,1)S(1)}, bf16[2,128,512]{2,1,0:T(8,128)(2,1)S(1)}, u32[]{:S(2)}, u32[]{:S(2)}) collective-permute-start(bf16[2,128,512]{2,1,0:T(8,128)(2,1)S(1)} %copy-done), channel_id=1, source_target_pairs={{0,3},{1,2},{2,1},{3,0},{4,7},{5,6},{6,5},{7,4},{8,11},{9,10},{10,... | collective-permute-start | bytes 786440 | tf_op jit(solution)/shard_map/ppermute | solution.py:146
  5.9 0.0 collective-permute-done.1.pair_ref
  5.9 0.0 collective-permute-done.received_ref.first_ref
  5.9 1.8 %collective-permute-start.5 = (bf16[32,384]{1,0:T(8,128)(2,1)S(1)}, bf16[32,384]{1,0:T(8,128)(2,1)S(1)}, u32[]{:S(2)}, u32[]{:S(2)}) collective-permute-start(bf16[32,384]{1,0:T(8,128)(2,1)S(1)} %get-tuple-element.33), channel_id=1, source_target_pairs={{0,9},{1,8},{2,11},{3,10},{4,13},{5,12},{6,15},{7,14},{8,1},{9,0},... | collective-permute-start | bytes 73736 | tf_op jit(solution)/shard_map/ppermute | solution.py:546
  7.7 0.3 %collective-permute-start.2 = (bf16[32,512]{1,0:T(8,128)(2,1)S(1)}, bf16[32,512]{1,0:T(8,128)(2,1)S(1)}, u32[]{:S(2)}, u32[]{:S(2)}) collective-permute-start(bf16[32,512]{1,0:T(8,128)(2,1)S(1)} %get-tuple-element.32.z_ref), channel_id=1, source_target_pairs={{0,1},{1,0},{2,3},{3,2},{4,5},{5,4},{6,7},{7,6},{8,9},{9,8},{10,11... | collective-permute-start | bytes 98312 | tf_op jit(solution)/shard_map/ppermute | solution.py:146
  8.0 0.2 %collective-permute-start.4 = (bf16[16,128]{1,0:T(8,128)(2,1)S(1)}, bf16[16,128]{1,0:T(8,128)(2,1)S(1)}, u32[]{:S(2)}, u32[]{:S(2)}) collective-permute-start(bf16[16,128]{1,0:T(8,128)(2,1)S(1)} %get-tuple-element.30._), channel_id=1, source_target_pairs={{0,1},{1,0},{2,3},{3,2},{4,5},{5,4},{6,7},{7,6},{8,9},{9,8},{10,11... | collective-permute-start | bytes 12296 | tf_op jit(solution)/shard_map/ppermute | solution.py:146
  8.2 0.8 %shard_map.98 = (bf16[16,1024]{1,0:T(8,128)(2,1)S(1)}, bf16[6,128,128]{2,1,0:T(8,128)(2,1)S(1)}, s32[3,8]{1,0:T(4,128)S(4)}) custom-call(s32[1]{0:T(128)S(6)} %copy.10.live_ref, s32[3,8]{1,0:T(4,128)} %targets_ref.1, bf16[2,8,512]{2,1,0:T(8,128)(2,1)} %bitcast.3, bf16[16,128]{1,0:T(8,128)(2,1)S(1)} %get-tuple-element.30._), custom_call_target="tpu_custom_call" | custom-call | tf_op jit(solution)/shard_map/pallas_call | solution.py:561
  9.0 0.1 collective-permute-done.4.pair_ref
  9.1 0.1 collective-permute-done.5.second_ref
  9.3 2.9 %collective-permute-start.6 = (bf16[96,128]{1,0:T(8,128)(2,1)S(1)}, bf16[96,128]{1,0:T(8,128)(2,1)S(1)}, u32[]{:S(2)}, u32[]{:S(2)}) collective-permute-start(bf16[96,128]{1,0:T(8,128)(2,1)S(1)} %get-tuple-element.39), channel_id=1, source_target_pairs={{0,16},{1,17},{2,18},{3,19},{4,20},{5,21},{6,22},{7,23},{8,24},{9,... | collective-permute-start | bytes 73736 | tf_op jit(solution)/shard_map/ppermute | solution.py:546
  12.2 0.2 %collective-permute-start.8 = (bf16[2,128,512]{2,1,0:T(8,128)(2,1)S(1)}, bf16[2,128,512]{2,1,0:T(8,128)(2,1)S(1)}, u32[]{:S(2)}, u32[]{:S(2)}) collective-permute-start(bf16[2,128,512]{2,1,0:T(8,128)(2,1)S(1)} %copy-done), channel_id=1, source_target_pairs={{0,1},{1,0},{2,3},{3,2},{4,5},{5,4},{6,7},{7,6},{8,9},{9,8},{10,11... | collective-permute-start | bytes 786440 | tf_op jit(solution)/shard_map/ppermute | solution.py:146
  12.5 0.5 %shard_map.100 = (f32[16,128]{1,0:T(8,128)S(1)}, f32[2,16,128]{2,1,0:T(8,128)S(1)}, bf16[2,128,128]{2,1,0:T(8,128)(2,1)S(1)}, bf16[64,256]{1,0:T(8,128)(2,1)S(1)}) custom-call(s32[3,8]{1,0:T(4,128)S(4)} %get-tuple-element.31.targets_ref, bf16[64,256]{1,0:T(8,128)(2,1)S(1)} %get-tuple-element.35.near_ref, bf16[6,128,128]{2,1,0:T(8,128)(2,1)S(1)} %get-tuple-element.34._.pick_ref), custom_call_target="tpu_custom_call" | custom-call | tf_op jit(solution)/shard_map/pallas_call | solution.py:587
  13.0 0.1 shard_map.101.own_ref
  13.1 0.0 collective-permute-done.2.pair_z_ref
  13.2 0.1 collective-permute-done.3.piece_ref
  13.3 0.2 %shard_map.102 = (f32[2,16,512]{2,1,0:T(8,128)S(1)}, f32[2,16,512]{2,1,0:T(8,128)S(1)}) custom-call(bf16[32,512]{1,0:T(8,128)(2,1)S(1)} %get-tuple-element.32.z_ref, bf16[32,512]{1,0:T(8,128)(2,1)S(1)} %collective-permute-done.2.pair_z_ref, bf16[2,128,512]{2,1,0:T(8,128)(2,1)S(1)} %collective-permute-done.3.piece_ref, f32[2,16,512]{2,1,0:T(8,128)S(1)} %shard_map.101.own_ref), custom_call_target="tpu_custom_call" | custom-call | tf_op jit(solution)/shard_map/pallas_call | solution.py:607
  13.4 0.2 %collective-permute-start.7 = (f32[2,16,512]{2,1,0:T(8,128)S(1)}, f32[2,16,512]{2,1,0:T(8,128)S(1)}, u32[]{:S(2)}, u32[]{:S(2)}) collective-permute-start(f32[2,16,512]{2,1,0:T(8,128)S(1)} %get-tuple-element.49), channel_id=1, source_target_pairs={{0,1},{1,0},{2,3},{3,2},{4,5},{5,4},{6,7},{7,6},{8,9},{9,8},{10,11... | collective-permute-start | bytes 196616 | tf_op jit(solution)/shard_map/ppermute | solution.py:146
  13.7 0.5 %shard_map.103 = (f32[128,128]{1,0:T(8,128)S(1)}, bf16[2,128,128]{2,1,0:T(8,128)(2,1)S(1)}, f32[16,1024]{1,0:T(8,128)S(1)}, bf16[128,1024]{1,0:T(8,128)(2,1)S(1)}) custom-call(f32[2,16,128]{2,1,0:T(8,128)S(1)} %get-tuple-element.40.partial_ref, bf16[2,128,128]{2,1,0:T(8,128)(2,1)S(1)} %get-tuple-element.41.lower_ref, ...), custom_call_target="tpu_custom_call" | custom-call | tf_op jit(solution)/shard_map/pallas_call | solution.py:619
  14.2 0.0 collective-permute-done.6.far_ref
  14.2 0.6 %shard_map.104 = (bf16[16,128]{1,0:T(8,128)(2,1)S(1)}, f32[128,16]{1,0:T(8,128)S(1)}) custom-call(s32[3,8]{1,0:T(4,128)S(4)} %get-tuple-element.31.targets_ref, bf16[64,256]{1,0:T(8,128)(2,1)S(1)} %get-tuple-element.38.near_ref, bf16[96,128]{1,0:T(8,128)(2,1)S(1)} %collective-permute-done.6.far_ref, bf16[6,128,128]{2,1,0:T(8,128)(2,1)S(1)} %get-tuple-element.34._.pick_ref, ...), custom_call_target="tpu_custom_call" | custom-call | flops 3000000000 | tf_op jit(solution)/shard_map/pallas_call | solution.py:631
  14.8 0.0 collective-permute-done.8.refs_0_
  14.8 0.0 collective-permute-done.7.far_ref
  14.9 0.9 %shard_map.105 = (f32[2,16,512]{2,1,0:T(8,128)}, f32[2,3,8,16]{3,2,1,0:T(8,128)}) custom-call(s32[1]{0:T(128)S(6)} %copy.10.live_ref, s32[3,8]{1,0:T(4,128)S(4)} %get-tuple-element.31.targets_ref, bf16[32,512]{1,0:T(8,128)(2,1)S(1)} %get-tuple-element.32.z_ref, f32[2,16,512]{2,1,0:T(8,128)S(1)} %get-tuple-element.37._.partial_ref, ...), custom_call_target="tpu_custom_call" | custom-call | tf_op jit(solution)/shard_map/pallas_call | solution.py:646
  (3 shorter events, 0.0 us)
Async XLA Ops:
  0.6 0.8 %copy-start.3 = (f32[2,16,3,8]{1,3,2,0:T(8,128)S(1)}, f32[2,16,3,8]{1,3,2,0:T(8,128)}, u32[]{:S(2)}) copy-start(f32[2,16,3,8]{1,3,2,0:T(8,128)} %param.9) | copy-start | bytes 9220
  0.6 0.8 %copy-start.1 = (f32[2,16,512]{2,1,0:T(8,128)S(1)}, f32[2,16,512]{2,1,0:T(8,128)}, u32[]{:S(2)}) copy-start(f32[2,16,512]{2,1,0:T(8,128)} %leaf_rhs_ref.1) | copy-start | bytes 196612
  0.7 4.2 %copy-start = (bf16[2,128,512]{2,1,0:T(8,128)(2,1)S(1)}, bf16[2,128,512]{2,1,0:T(8,128)(2,1)}, u32[]{:S(2)}) copy-start(bf16[2,128,512]{2,1,0:T(8,128)(2,1)} %piece_ref.1) | copy-start | bytes 786436
  0.7 0.8 %copy-start.2 = (bf16[2,512,8]{1,2,0:T(8,128)(2,1)S(1)}, bf16[2,512,8]{1,2,0:T(8,128)(2,1)}, u32[]{:S(2)}) copy-start(bf16[2,512,8]{1,2,0:T(8,128)(2,1)} %param.11) | copy-start | bytes 49156
  0.7 0.8 %copy-start.5 = (bf16[2,8,48]{2,1,0:T(8,128)(2,1)S(1)}, bf16[2,8,48]{2,1,0:T(8,128)(2,1)}, u32[]{:S(2)}) copy-start(bf16[2,8,48]{2,1,0:T(8,128)(2,1)} %sep_low_ref.1) | copy-start | bytes 4612
  0.7 0.8 %copy-start.4 = (bf16[2,8,112]{2,1,0:T(8,128)(2,1)S(1)}, bf16[2,8,112]{2,1,0:T(8,128)(2,1)}, u32[]{:S(2)}) copy-start(bf16[2,8,112]{2,1,0:T(8,128)(2,1)} %inv_ref.1) | copy-start | bytes 10756
  1.7 4.2 %collective-permute-start = (bf16[16,256]{1,0:T(8,128)(2,1)S(1)}, bf16[16,256]{1,0:T(8,128)(2,1)S(1)}, u32[]{:S(2)}, u32[]{:S(2)}) collective-permute-start(bf16[16,256]{1,0:T(8,128)(2,1)S(1)} %get-tuple-element.28), channel_id=1, source_target_pairs={{0,5},{1,4},{2,7},{3,6},{4,1},{5,0},{6,3},{7,2},{8,13},{9,12},{10,... | collective-permute-start | bytes 24584 | tf_op jit(solution)/shard_map/ppermute | solution.py:546
  4.2 1.8 %collective-permute-start.1 = (bf16[16,128]{1,0:T(8,128)(2,1)S(1)}, bf16[16,128]{1,0:T(8,128)(2,1)S(1)}, u32[]{:S(2)}, u32[]{:S(2)}) collective-permute-start(bf16[16,128]{1,0:T(8,128)(2,1)S(1)} %get-tuple-element.29), channel_id=1, source_target_pairs={{0,1},{1,0},{2,3},{3,2},{4,5},{5,4},{6,7},{7,6},{8,9},{9,8},{10,11... | collective-permute-start | bytes 12296 | tf_op jit(solution)/shard_map/ppermute | solution.py:146
  4.8 8.4 %collective-permute-start.3 = (bf16[2,128,512]{2,1,0:T(8,128)(2,1)S(1)}, bf16[2,128,512]{2,1,0:T(8,128)(2,1)S(1)}, u32[]{:S(2)}, u32[]{:S(2)}) collective-permute-start(bf16[2,128,512]{2,1,0:T(8,128)(2,1)S(1)} %copy-done), channel_id=1, source_target_pairs={{0,3},{1,2},{2,1},{3,0},{4,7},{5,6},{6,5},{7,4},{8,11},{9,10},{10,... | collective-permute-start | bytes 786440 | tf_op jit(solution)/shard_map/ppermute | solution.py:146
  5.9 3.3 %collective-permute-start.5 = (bf16[32,384]{1,0:T(8,128)(2,1)S(1)}, bf16[32,384]{1,0:T(8,128)(2,1)S(1)}, u32[]{:S(2)}, u32[]{:S(2)}) collective-permute-start(bf16[32,384]{1,0:T(8,128)(2,1)S(1)} %get-tuple-element.33), channel_id=1, source_target_pairs={{0,9},{1,8},{2,11},{3,10},{4,13},{5,12},{6,15},{7,14},{8,1},{9,0},... | collective-permute-start | bytes 73736 | tf_op jit(solution)/shard_map/ppermute | solution.py:546
  7.7 5.4 %collective-permute-start.2 = (bf16[32,512]{1,0:T(8,128)(2,1)S(1)}, bf16[32,512]{1,0:T(8,128)(2,1)S(1)}, u32[]{:S(2)}, u32[]{:S(2)}) collective-permute-start(bf16[32,512]{1,0:T(8,128)(2,1)S(1)} %get-tuple-element.32.z_ref), channel_id=1, source_target_pairs={{0,1},{1,0},{2,3},{3,2},{4,5},{5,4},{6,7},{7,6},{8,9},{9,8},{10,11... | collective-permute-start | bytes 98312 | tf_op jit(solution)/shard_map/ppermute | solution.py:146
  8.0 1.2 %collective-permute-start.4 = (bf16[16,128]{1,0:T(8,128)(2,1)S(1)}, bf16[16,128]{1,0:T(8,128)(2,1)S(1)}, u32[]{:S(2)}, u32[]{:S(2)}) collective-permute-start(bf16[16,128]{1,0:T(8,128)(2,1)S(1)} %get-tuple-element.30._), channel_id=1, source_target_pairs={{0,1},{1,0},{2,3},{3,2},{4,5},{5,4},{6,7},{7,6},{8,9},{9,8},{10,11... | collective-permute-start | bytes 12296 | tf_op jit(solution)/shard_map/ppermute | solution.py:146
  9.3 4.9 %collective-permute-start.6 = (bf16[96,128]{1,0:T(8,128)(2,1)S(1)}, bf16[96,128]{1,0:T(8,128)(2,1)S(1)}, u32[]{:S(2)}, u32[]{:S(2)}) collective-permute-start(bf16[96,128]{1,0:T(8,128)(2,1)S(1)} %get-tuple-element.39), channel_id=1, source_target_pairs={{0,16},{1,17},{2,18},{3,19},{4,20},{5,21},{6,22},{7,23},{8,24},{9,... | collective-permute-start | bytes 73736 | tf_op jit(solution)/shard_map/ppermute | solution.py:546
  12.2 2.6 %collective-permute-start.8 = (bf16[2,128,512]{2,1,0:T(8,128)(2,1)S(1)}, bf16[2,128,512]{2,1,0:T(8,128)(2,1)S(1)}, u32[]{:S(2)}, u32[]{:S(2)}) collective-permute-start(bf16[2,128,512]{2,1,0:T(8,128)(2,1)S(1)} %copy-done), channel_id=1, source_target_pairs={{0,1},{1,0},{2,3},{3,2},{4,5},{5,4},{6,7},{7,6},{8,9},{9,8},{10,11... | collective-permute-start | bytes 786440 | tf_op jit(solution)/shard_map/ppermute | solution.py:146
  13.4 1.4 %collective-permute-start.7 = (f32[2,16,512]{2,1,0:T(8,128)S(1)}, f32[2,16,512]{2,1,0:T(8,128)S(1)}, u32[]{:S(2)}, u32[]{:S(2)}) collective-permute-start(f32[2,16,512]{2,1,0:T(8,128)S(1)} %get-tuple-element.49), channel_id=1, source_target_pairs={{0,1},{1,0},{2,3},{3,2},{4,5},{5,4},{6,7},{7,6},{8,9},{9,8},{10,11... | collective-permute-start | bytes 196616 | tf_op jit(solution)/shard_map/ppermute | solution.py:146

commit v10 on v8

--- a/solution.py
+++ b/solution.py
@@ -295,7 +295,7 @@
     ]
     for part in range(2):
         out_ref[part] = own_ref[part] + own_product[part]
-        pair_out_ref[part] = pair_product[part]
+        pair_out_ref[part] = pair_product[part].astype(jnp.bfloat16)
 
 
 def owner(targets_ref, level, block):
@@ -482,7 +482,7 @@
     products = [piece_product(step, z_ref, piece_ref) for step, piece_ref in zip(steps, piece_refs)]
     copies = []
     for part in range(2):
-        leaf_w = partial_ref[part] + far_ref[part] + sum(product[part] for product in products)
+        leaf_w = partial_ref[part] + far_ref[part].astype(jnp.float32) + sum(product[part] for product in products)
         leaf_place[part] = (
             jnp.where(live, leaf_w, 0.0) - from_tree[:, part * leaf_rows : (part + 1) * leaf_rows]
         )
@@ -604,7 +604,10 @@
     )(*[in_vmem(ready) for ready in (leaf_z, leaf_inv, update)])
     partial, pair_far = pl.pallas_call(
         functools.partial(far_kernel, 3),
-        out_shape=(pltpu.VMEM((2, columns, leaf_rows), jnp.float32),) * 2,
+        out_shape=(
+            pltpu.VMEM((2, columns, leaf_rows), jnp.float32),
+            pltpu.VMEM((2, columns, leaf_rows), jnp.bfloat16),
+        ),
         in_specs=[whole(VMEM)] * 4,
         out_specs=(whole(VMEM),) * 2,
         cost_estimate=pl.CostEstimate(flops=0, bytes_accessed=0, transcendentals=0),

time: 15.9 us -> 15.9 us (level)
  no operation moved by 1% of the time
where the time goes in v10:
time: 15.9 us; the launch traced here: 15.7 us
  starting transfers between devices  9.93 us (62%)
  Pallas kernels  3.76 us (24%)
  between operations  1.46 us (9%)
  waiting for transfers between devices  0.45 us (3%)
    ppermute x3, starting transfers between devices, exchange(): return lax.ppermute(values_in, ('leaf', 'rhs'), partners)  7.14 us
    ppermute x6, starting transfers between devices, xor_permute(): lax.ppermute(values_in, axis, [(source, source ^ offset) for source in ra...  2.78 us
    pallas_call x1, Pallas kernels, body(): pl.pallas_call(functools.partial(finish_kernel, (1,)), out_shape=(jax.Sha...  0.91 us
    pallas_call x1, Pallas kernels, body(): pl.pallas_call(functools.partial(prepare_kernel, (1 + depth) * columns),...  0.78 us
    pallas_call x1, Pallas kernels, body(): pl.pallas_call(top_kernel, out_shape=(pltpu.VMEM((columns, size), jnp.bfl...  0.61 us
    pallas_call x1, Pallas kernels, body(): pl.pallas_call(near_kernel, out_shape=(pltpu.VMEM((columns, size), jnp.fl...  0.54 us
    pallas_call x1, Pallas kernels, body(): pl.pallas_call(operator_kernel, out_shape=(pltpu.VMEM((size, size), jnp.f...  0.39 us
  transfers between devices with their start and end apart: 9, of which 4 were waited for; matrix products, arithmetic and copies ran while one was open for 0% of the time, Pallas kernels for 17%

profile of v10, /device:TPU:0, one launch (start us, length us, event | category | flops | bytes accessed | tf_op | source)
XLA Modules:
  0.0 15.7 jit_solution(13251453483882956845)
XLA Ops:
  0.6 0.0 copy-start.1
  0.6 0.0 copy-start.3
  0.7 0.0 copy-start
  0.7 0.0 copy-start.2
  0.7 0.0 copy-start.5
  0.7 0.0 copy-start.4
  1.4 0.1 copy-done.1
  1.5 0.0 copy-done.3
  1.5 0.0 copy-done.2
  1.5 0.0 copy-done.5
  1.5 0.0 copy-done.4
  1.5 0.2 %shard_map.96 = (bf16[16,256]{1,0:T(8,128)(2,1)S(1)}, bf16[16,128]{1,0:T(8,128)(2,1)S(1)}, bf16[16,256]{1,0:T(8,128)(2,1)S(1)}, bf16[32,512]{1,0:T(8,128)(2,1)S(1)}) custom-call(s32[1]{0:T(128)S(6)} %copy.10.live_ref, f32[8,128]{1,0:T(8,128)S(1)} %shard_map.95._, f32[2,16,512]{2,1,0:T(8,128)S(1)} %copy-done.1, bf16[2,8,512]{2,1,0:T(8,128)(2,1)S(1)} %bitcast.4, ...), custom_call_target="tpu_custom_call" | custom-call | tf_op jit(solution)/shard_map/pallas_call | solution.py:526
  1.7 2.5 %collective-permute-start = (bf16[16,256]{1,0:T(8,128)(2,1)S(1)}, bf16[16,256]{1,0:T(8,128)(2,1)S(1)}, u32[]{:S(2)}, u32[]{:S(2)}) collective-permute-start(bf16[16,256]{1,0:T(8,128)(2,1)S(1)} %get-tuple-element.28), channel_id=1, source_target_pairs={{0,5},{1,4},{2,7},{3,6},{4,1},{5,0},{6,3},{7,2},{8,13},{9,12},{10,... | collective-permute-start | bytes 24584 | tf_op jit(solution)/shard_map/ppermute | solution.py:544
  4.1 0.7 %collective-permute-start.1 = (bf16[16,128]{1,0:T(8,128)(2,1)S(1)}, bf16[16,128]{1,0:T(8,128)(2,1)S(1)}, u32[]{:S(2)}, u32[]{:S(2)}) collective-permute-start(bf16[16,128]{1,0:T(8,128)(2,1)S(1)} %get-tuple-element.29), channel_id=1, source_target_pairs={{0,1},{1,0},{2,3},{3,2},{4,5},{5,4},{6,7},{7,6},{8,9},{9,8},{10,11... | collective-permute-start | bytes 12296 | tf_op jit(solution)/shard_map/ppermute | solution.py:146
  4.8 0.0 copy-done
  4.8 1.1 %collective-permute-start.3 = (bf16[2,128,512]{2,1,0:T(8,128)(2,1)S(1)}, bf16[2,128,512]{2,1,0:T(8,128)(2,1)S(1)}, u32[]{:S(2)}, u32[]{:S(2)}) collective-permute-start(bf16[2,128,512]{2,1,0:T(8,128)(2,1)S(1)} %copy-done), channel_id=1, source_target_pairs={{0,3},{1,2},{2,1},{3,0},{4,7},{5,6},{6,5},{7,4},{8,11},{9,10},{10,... | collective-permute-start | bytes 786440 | tf_op jit(solution)/shard_map/ppermute | solution.py:146
  5.9 0.0 collective-permute-done.1.pair_ref
  5.9 0.0 collective-permute-done.received_ref.first_ref
  5.9 1.8 %collective-permute-start.5 = (bf16[32,384]{1,0:T(8,128)(2,1)S(1)}, bf16[32,384]{1,0:T(8,128)(2,1)S(1)}, u32[]{:S(2)}, u32[]{:S(2)}) collective-permute-start(bf16[32,384]{1,0:T(8,128)(2,1)S(1)} %get-tuple-element.33), channel_id=1, source_target_pairs={{0,9},{1,8},{2,11},{3,10},{4,13},{5,12},{6,15},{7,14},{8,1},{9,0},... | collective-permute-start | bytes 73736 | tf_op jit(solution)/shard_map/ppermute | solution.py:544
  7.7 0.3 %collective-permute-start.2 = (bf16[32,512]{1,0:T(8,128)(2,1)S(1)}, bf16[32,512]{1,0:T(8,128)(2,1)S(1)}, u32[]{:S(2)}, u32[]{:S(2)}) collective-permute-start(bf16[32,512]{1,0:T(8,128)(2,1)S(1)} %get-tuple-element.32.z_ref), channel_id=1, source_target_pairs={{0,1},{1,0},{2,3},{3,2},{4,5},{5,4},{6,7},{7,6},{8,9},{9,8},{10,11... | collective-permute-start | bytes 98312 | tf_op jit(solution)/shard_map/ppermute | solution.py:146
  8.0 0.2 %collective-permute-start.4 = (bf16[16,128]{1,0:T(8,128)(2,1)S(1)}, bf16[16,128]{1,0:T(8,128)(2,1)S(1)}, u32[]{:S(2)}, u32[]{:S(2)}) collective-permute-start(bf16[16,128]{1,0:T(8,128)(2,1)S(1)} %get-tuple-element.30._), channel_id=1, source_target_pairs={{0,1},{1,0},{2,3},{3,2},{4,5},{5,4},{6,7},{7,6},{8,9},{9,8},{10,11... | collective-permute-start | bytes 12296 | tf_op jit(solution)/shard_map/ppermute | solution.py:146
  8.2 0.8 %shard_map.98 = (bf16[128,1024]{1,0:T(8,128)(2,1)S(1)}, bf16[6,128,128]{2,1,0:T(8,128)(2,1)S(1)}, s32[3,8]{1,0:T(4,128)S(4)}) custom-call(s32[1]{0:T(128)S(6)} %copy.10.live_ref, s32[3,8]{1,0:T(4,128)} %targets_ref.1, bf16[2,8,512]{2,1,0:T(8,128)(2,1)} %bitcast.3, bf16[16,128]{1,0:T(8,128)(2,1)S(1)} %get-tuple-element.30._), custom_call_target="tpu_custom_call" | custom-call | tf_op jit(solution)/shard_map/pallas_call | solution.py:559
  9.0 0.1 collective-permute-done.4.pair_ref
  9.1 0.1 collective-permute-done.5.second_ref
  9.3 2.9 %collective-permute-start.6 = (bf16[96,128]{1,0:T(8,128)(2,1)S(1)}, bf16[96,128]{1,0:T(8,128)(2,1)S(1)}, u32[]{:S(2)}, u32[]{:S(2)}) collective-permute-start(bf16[96,128]{1,0:T(8,128)(2,1)S(1)} %get-tuple-element.39), channel_id=1, source_target_pairs={{0,16},{1,17},{2,18},{3,19},{4,20},{5,21},{6,22},{7,23},{8,24},{9,... | collective-permute-start | bytes 73736 | tf_op jit(solution)/shard_map/ppermute | solution.py:544
  12.2 0.2 %collective-permute-start.8 = (bf16[2,128,512]{2,1,0:T(8,128)(2,1)S(1)}, bf16[2,128,512]{2,1,0:T(8,128)(2,1)S(1)}, u32[]{:S(2)}, u32[]{:S(2)}) collective-permute-start(bf16[2,128,512]{2,1,0:T(8,128)(2,1)S(1)} %copy-done), channel_id=1, source_target_pairs={{0,1},{1,0},{2,3},{3,2},{4,5},{5,4},{6,7},{7,6},{8,9},{9,8},{10,11... | collective-permute-start | bytes 786440 | tf_op jit(solution)/shard_map/ppermute | solution.py:146
  12.4 0.5 %shard_map.100 = (f32[16,128]{1,0:T(8,128)S(1)}, f32[2,16,128]{2,1,0:T(8,128)S(1)}, bf16[2,128,128]{2,1,0:T(8,128)(2,1)S(1)}, bf16[64,256]{1,0:T(8,128)(2,1)S(1)}) custom-call(s32[3,8]{1,0:T(4,128)S(4)} %get-tuple-element.31.targets_ref, bf16[64,256]{1,0:T(8,128)(2,1)S(1)} %get-tuple-element.35.near_ref, bf16[6,128,128]{2,1,0:T(8,128)(2,1)S(1)} %get-tuple-element.34._.pick_ref), custom_call_target="tpu_custom_call" | custom-call | tf_op jit(solution)/shard_map/pallas_call | solution.py:585
  13.0 0.1 shard_map.101.own_ref
  13.1 0.0 collective-permute-done.2.pair_z_ref
  13.2 0.1 collective-permute-done.3.piece_ref
  13.2 0.2 %shard_map.102 = (f32[2,16,512]{2,1,0:T(8,128)S(1)}, bf16[2,16,512]{2,1,0:T(8,128)(2,1)S(1)}) custom-call(bf16[32,512]{1,0:T(8,128)(2,1)S(1)} %get-tuple-element.32.z_ref, bf16[32,512]{1,0:T(8,128)(2,1)S(1)} %collective-permute-done.2.pair_z_ref, bf16[2,128,512]{2,1,0:T(8,128)(2,1)S(1)} %collective-permute-done.3.piece_ref, f32[2,16,512]{2,1,0:T(8,128)S(1)} %shard_map.101.own_ref), custom_call_target="tpu_custom_call" | custom-call | tf_op jit(solution)/shard_map/pallas_call | solution.py:605
  13.4 0.3 %collective-permute-start.7 = (bf16[2,16,512]{2,1,0:T(8,128)(2,1)S(1)}, bf16[2,16,512]{2,1,0:T(8,128)(2,1)S(1)}, u32[]{:S(2)}, u32[]{:S(2)}) collective-permute-start(bf16[2,16,512]{2,1,0:T(8,128)(2,1)S(1)} %get-tuple-element.49), channel_id=1, source_target_pairs={{0,1},{1,0},{2,3},{3,2},{4,5},{5,4},{6,7},{7,6},{8,9},{9,8},{10,11... | collective-permute-start | bytes 98312 | tf_op jit(solution)/shard_map/ppermute | solution.py:146
  13.7 0.4 %shard_map.103 = (f32[128,128]{1,0:T(8,128)S(1)}, bf16[2,128,128]{2,1,0:T(8,128)(2,1)S(1)}, f32[16,1024]{1,0:T(8,128)S(1)}, bf16[128,1024]{1,0:T(8,128)(2,1)S(1)}) custom-call(f32[2,16,128]{2,1,0:T(8,128)S(1)} %get-tuple-element.40.partial_ref, bf16[2,128,128]{2,1,0:T(8,128)(2,1)S(1)} %get-tuple-element.41.lower_ref, ...), custom_call_target="tpu_custom_call" | custom-call | tf_op jit(solution)/shard_map/pallas_call | solution.py:620
  14.1 0.1 collective-permute-done.6.far_ref
  14.2 0.6 %shard_map.104 = (bf16[16,128]{1,0:T(8,128)(2,1)S(1)}, f32[128,16]{1,0:T(8,128)S(1)}) custom-call(s32[3,8]{1,0:T(4,128)S(4)} %get-tuple-element.31.targets_ref, bf16[64,256]{1,0:T(8,128)(2,1)S(1)} %get-tuple-element.38.near_ref, bf16[96,128]{1,0:T(8,128)(2,1)S(1)} %collective-permute-done.6.far_ref, bf16[6,128,128]{2,1,0:T(8,128)(2,1)S(1)} %get-tuple-element.34._.pick_ref, ...), custom_call_target="tpu_custom_call" | custom-call | flops 3000000000 | tf_op jit(solution)/shard_map/pallas_call | solution.py:632
  14.8 0.0 collective-permute-done.8.refs_0_
  14.8 0.0 collective-permute-done.7.far_ref
  14.8 0.9 %shard_map.105 = (f32[2,16,512]{2,1,0:T(8,128)}, f32[2,3,8,16]{3,2,1,0:T(8,128)}) custom-call(s32[1]{0:T(128)S(6)} %copy.10.live_ref, s32[3,8]{1,0:T(4,128)S(4)} %get-tuple-element.31.targets_ref, bf16[32,512]{1,0:T(8,128)(2,1)S(1)} %get-tuple-element.32.z_ref, f32[2,16,512]{2,1,0:T(8,128)S(1)} %get-tuple-element.37._.partial_ref, ...), custom_call_target="tpu_custom_call" | custom-call | tf_op jit(solution)/shard_map/pallas_call | solution.py:647
  (3 shorter events, 0.0 us)
Async XLA Ops:
  0.6 0.8 %copy-start.1 = (f32[2,16,512]{2,1,0:T(8,128)S(1)}, f32[2,16,512]{2,1,0:T(8,128)}, u32[]{:S(2)}) copy-start(f32[2,16,512]{2,1,0:T(8,128)} %leaf_rhs_ref.1) | copy-start | bytes 196612
  0.6 0.8 %copy-start.3 = (f32[2,16,3,8]{1,3,2,0:T(8,128)S(1)}, f32[2,16,3,8]{1,3,2,0:T(8,128)}, u32[]{:S(2)}) copy-start(f32[2,16,3,8]{1,3,2,0:T(8,128)} %param.9) | copy-start | bytes 9220
  0.7 4.2 %copy-start = (bf16[2,128,512]{2,1,0:T(8,128)(2,1)S(1)}, bf16[2,128,512]{2,1,0:T(8,128)(2,1)}, u32[]{:S(2)}) copy-start(bf16[2,128,512]{2,1,0:T(8,128)(2,1)} %piece_ref.1) | copy-start | bytes 786436
  0.7 0.8 %copy-start.2 = (bf16[2,512,8]{1,2,0:T(8,128)(2,1)S(1)}, bf16[2,512,8]{1,2,0:T(8,128)(2,1)}, u32[]{:S(2)}) copy-start(bf16[2,512,8]{1,2,0:T(8,128)(2,1)} %param.11) | copy-start | bytes 49156
  0.7 0.8 %copy-start.5 = (bf16[2,8,48]{2,1,0:T(8,128)(2,1)S(1)}, bf16[2,8,48]{2,1,0:T(8,128)(2,1)}, u32[]{:S(2)}) copy-start(bf16[2,8,48]{2,1,0:T(8,128)(2,1)} %sep_low_ref.1) | copy-start | bytes 4612
  0.7 0.8 %copy-start.4 = (bf16[2,8,112]{2,1,0:T(8,128)(2,1)S(1)}, bf16[2,8,112]{2,1,0:T(8,128)(2,1)}, u32[]{:S(2)}) copy-start(bf16[2,8,112]{2,1,0:T(8,128)(2,1)} %inv_ref.1) | copy-start | bytes 10756
  1.7 4.2 %collective-permute-start = (bf16[16,256]{1,0:T(8,128)(2,1)S(1)}, bf16[16,256]{1,0:T(8,128)(2,1)S(1)}, u32[]{:S(2)}, u32[]{:S(2)}) collective-permute-start(bf16[16,256]{1,0:T(8,128)(2,1)S(1)} %get-tuple-element.28), channel_id=1, source_target_pairs={{0,5},{1,4},{2,7},{3,6},{4,1},{5,0},{6,3},{7,2},{8,13},{9,12},{10,... | collective-permute-start | bytes 24584 | tf_op jit(solution)/shard_map/ppermute | solution.py:544
  4.1 1.8 %collective-permute-start.1 = (bf16[16,128]{1,0:T(8,128)(2,1)S(1)}, bf16[16,128]{1,0:T(8,128)(2,1)S(1)}, u32[]{:S(2)}, u32[]{:S(2)}) collective-permute-start(bf16[16,128]{1,0:T(8,128)(2,1)S(1)} %get-tuple-element.29), channel_id=1, source_target_pairs={{0,1},{1,0},{2,3},{3,2},{4,5},{5,4},{6,7},{7,6},{8,9},{9,8},{10,11... | collective-permute-start | bytes 12296 | tf_op jit(solution)/shard_map/ppermute | solution.py:146
  4.8 8.4 %collective-permute-start.3 = (bf16[2,128,512]{2,1,0:T(8,128)(2,1)S(1)}, bf16[2,128,512]{2,1,0:T(8,128)(2,1)S(1)}, u32[]{:S(2)}, u32[]{:S(2)}) collective-permute-start(bf16[2,128,512]{2,1,0:T(8,128)(2,1)S(1)} %copy-done), channel_id=1, source_target_pairs={{0,3},{1,2},{2,1},{3,0},{4,7},{5,6},{6,5},{7,4},{8,11},{9,10},{10,... | collective-permute-start | bytes 786440 | tf_op jit(solution)/shard_map/ppermute | solution.py:146
  5.9 3.3 %collective-permute-start.5 = (bf16[32,384]{1,0:T(8,128)(2,1)S(1)}, bf16[32,384]{1,0:T(8,128)(2,1)S(1)}, u32[]{:S(2)}, u32[]{:S(2)}) collective-permute-start(bf16[32,384]{1,0:T(8,128)(2,1)S(1)} %get-tuple-element.33), channel_id=1, source_target_pairs={{0,9},{1,8},{2,11},{3,10},{4,13},{5,12},{6,15},{7,14},{8,1},{9,0},... | collective-permute-start | bytes 73736 | tf_op jit(solution)/shard_map/ppermute | solution.py:544
  7.7 5.4 %collective-permute-start.2 = (bf16[32,512]{1,0:T(8,128)(2,1)S(1)}, bf16[32,512]{1,0:T(8,128)(2,1)S(1)}, u32[]{:S(2)}, u32[]{:S(2)}) collective-permute-start(bf16[32,512]{1,0:T(8,128)(2,1)S(1)} %get-tuple-element.32.z_ref), channel_id=1, source_target_pairs={{0,1},{1,0},{2,3},{3,2},{4,5},{5,4},{6,7},{7,6},{8,9},{9,8},{10,11... | collective-permute-start | bytes 98312 | tf_op jit(solution)/shard_map/ppermute | solution.py:146
  8.0 1.2 %collective-permute-start.4 = (bf16[16,128]{1,0:T(8,128)(2,1)S(1)}, bf16[16,128]{1,0:T(8,128)(2,1)S(1)}, u32[]{:S(2)}, u32[]{:S(2)}) collective-permute-start(bf16[16,128]{1,0:T(8,128)(2,1)S(1)} %get-tuple-element.30._), channel_id=1, source_target_pairs={{0,1},{1,0},{2,3},{3,2},{4,5},{5,4},{6,7},{7,6},{8,9},{9,8},{10,11... | collective-permute-start | bytes 12296 | tf_op jit(solution)/shard_map/ppermute | solution.py:146
  9.3 4.9 %collective-permute-start.6 = (bf16[96,128]{1,0:T(8,128)(2,1)S(1)}, bf16[96,128]{1,0:T(8,128)(2,1)S(1)}, u32[]{:S(2)}, u32[]{:S(2)}) collective-permute-start(bf16[96,128]{1,0:T(8,128)(2,1)S(1)} %get-tuple-element.39), channel_id=1, source_target_pairs={{0,16},{1,17},{2,18},{3,19},{4,20},{5,21},{6,22},{7,23},{8,24},{9,... | collective-permute-start | bytes 73736 | tf_op jit(solution)/shard_map/ppermute | solution.py:544
  12.2 2.6 %collective-permute-start.8 = (bf16[2,128,512]{2,1,0:T(8,128)(2,1)S(1)}, bf16[2,128,512]{2,1,0:T(8,128)(2,1)S(1)}, u32[]{:S(2)}, u32[]{:S(2)}) collective-permute-start(bf16[2,128,512]{2,1,0:T(8,128)(2,1)S(1)} %copy-done), channel_id=1, source_target_pairs={{0,1},{1,0},{2,3},{3,2},{4,5},{5,4},{6,7},{7,6},{8,9},{9,8},{10,11... | collective-permute-start | bytes 786440 | tf_op jit(solution)/shard_map/ppermute | solution.py:146
  13.4 1.4 %collective-permute-start.7 = (bf16[2,16,512]{2,1,0:T(8,128)(2,1)S(1)}, bf16[2,16,512]{2,1,0:T(8,128)(2,1)S(1)}, u32[]{:S(2)}, u32[]{:S(2)}) collective-permute-start(bf16[2,16,512]{2,1,0:T(8,128)(2,1)S(1)} %get-tuple-element.49), channel_id=1, source_target_pairs={{0,1},{1,0},{2,3},{3,2},{4,5},{5,4},{6,7},{7,6},{8,9},{9,8},{10,11... | collective-permute-start | bytes 98312 | tf_op jit(solution)/shard_map/ppermute | solution.py:146
